TPU v7x, 256 devices: a whole 4x4x8 slice. The times are simulated.
256 devices in a mesh: ep: 32 (over z, y), dp: 8 (over x, core).
Axes of the slice: x: 4, y: 4, z: 8, core: 2. Of those that a mesh axis runs over, the one named last changes fastest.
Arguments:
- hidden_rows: bfloat16 [64, 1792, 1024], P('ep', None, 'dp'), may hold values from -6 to 6
- out_grad: bfloat16 [64, 1792, 3584], P('ep', None, 'dp'), may hold values from -0.75 to 0.75
- row_counts: int32 [64], P('ep'), may hold values from 1 to 1792, as said below
- replicas: int32 [32, 8], replicated, may hold values from -1 to 63, as said below
- next_replicas: int32 [32, 8], replicated, may hold values from -1 to 63, as said below
- owner_map: int32 [32], replicated, may hold values from 0 to 31, each once
- master: float32 [32, 3584, 1024], P('ep', 'dp'), may hold values from -0.1875 to 0.1875
- first_moment: bfloat16 [32, 3584, 1024], P('ep', 'dp'), may hold values from -3 to 3
- second_moment: bfloat16 [32, 3584, 1024], P('ep', 'dp'), may hold values from 0.0099487305 to 1
Outputs:
- new_master: float32 [32, 3584, 1024], P('ep', 'dp')
- new_first_moment: bfloat16 [32, 3584, 1024], P('ep', 'dp')
- new_second_moment: bfloat16 [32, 3584, 1024], P('ep', 'dp')
- next_copies: bfloat16 [64, 3584, 1024], P('ep', 'dp')
Inputs may be any that keep to these rules, and one draw needn't show every extreme that they name: Rows of slot g past row_counts[g] are unused; some slot is full in every draw. `replicas`: each of the 64 slots appears in exactly one list; a list holds its slots first and -1 after them; every expert has 1 to 8 copies and some expert has exactly 8. `next_replicas`: same form as replicas. `owner_map`: each ep index owns exactly one expert.
All inputs are finite; a program needn't handle non-finite values.
Results may differ from a plain program's by a relative error of at most 0.017.
Values may be sent and summed in bfloat16 or wider, within the bound.
No kernel may reach another device: no remote copies, remote signals or barrier semaphores. Data moves between devices by JAX's collectives and lax.ppermute only.
A program may use at most 64 MiB of HBM per device.

v0:
```python
import jax
import jax.numpy as jnp
from jax import lax
from jax.sharding import PartitionSpec as P

beta_first = 0.9
beta_second = 0.95
learn_rate = 0.001
adam_epsilon = 1e-08


def holder_experts(replicas, total_slots):
    slot_ids = jnp.arange(total_slots, dtype=jnp.int32)
    hold_table = jnp.any(replicas[:, :, None] == slot_ids[None, None, :], axis=1).astype(jnp.int32)
    expert_ids = jnp.arange(replicas.shape[0], dtype=jnp.int32)
    return jnp.sum(hold_table * expert_ids[:, None], axis=0)


def slot_owners(replicas, owner_map, total_slots):
    experts = holder_experts(replicas, total_slots)
    picked = experts[:, None] == jnp.arange(owner_map.shape[0], dtype=jnp.int32)[None, :]
    return jnp.sum(jnp.where(picked, owner_map[None, :], 0), axis=1)


def adam_update(master, first_moment, second_moment, gradient):
    first_new = beta_first * first_moment.astype(jnp.float32) + (1.0 - beta_first) * gradient
    second_new = (
        beta_second * second_moment.astype(jnp.float32) + (1.0 - beta_second) * gradient * gradient
    )
    updated = master - learn_rate * first_new / (jnp.sqrt(second_new) + adam_epsilon)
    return (first_new, second_new, updated)


def shards(
    hidden_rows,
    out_grad,
    row_counts,
    replicas,
    next_replicas,
    owner_map,
    master,
    first_moment,
    second_moment,
):
    ep_count = lax.axis_size("ep")
    slot_count = hidden_rows.shape[0]
    row_total = hidden_rows.shape[1]
    local_width = out_grad.shape[2]
    hidden_width = master.shape[2]
    piece_rows = local_width // ep_count
    total_slots = slot_count * ep_count
    live_rows = jnp.arange(row_total, dtype=jnp.int32)[None, :] < row_counts[:, None]
    masked = jnp.where(live_rows[:, :, None], out_grad, jnp.zeros_like(out_grad))
    slot_grads = jnp.einsum(
        "srd,srk->sdk",
        masked,
        lax.all_gather(hidden_rows, "dp", axis=2, tiled=True),
        preferred_element_type=jnp.float32,
    )
    blocks = slot_grads.reshape(slot_count, ep_count, piece_rows, hidden_width)
    received = lax.all_to_all(
        blocks.astype(jnp.bfloat16), "ep", split_axis=1, concat_axis=1, tiled=True
    ).astype(blocks.dtype)
    owner_ids = jnp.arange(ep_count, dtype=jnp.int32)
    owners_now = slot_owners(replicas, owner_map, total_slots).reshape(ep_count, slot_count)
    select_now = (owners_now[None, :, :] == owner_ids[:, None, None]).astype(jnp.float32)
    owner_pieces = jnp.einsum(
        "kqs,sqrf->krf", select_now, received, precision=lax.Precision.HIGHEST
    )
    owners_next = slot_owners(next_replicas, owner_map, total_slots).reshape(ep_count, slot_count)
    select_next = (jnp.transpose(owners_next)[:, :, None] == owner_ids[None, None, :]).astype(
        jnp.bfloat16
    )
    arrived = lax.all_to_all(
        owner_pieces.astype(jnp.bfloat16), "ep", split_axis=0, concat_axis=0, tiled=True
    ).astype(owner_pieces.dtype)
    gradient = arrived.reshape(1, local_width, hidden_width)
    first_new, second_new, updated = adam_update(master, first_moment, second_moment, gradient)
    new_first = first_new.astype(jnp.bfloat16)
    new_second = second_new.astype(jnp.bfloat16)
    weight_blocks = updated.astype(jnp.bfloat16).reshape(ep_count, piece_rows, hidden_width)
    weight_pieces = lax.all_to_all(weight_blocks, "ep", split_axis=0, concat_axis=0, tiled=True)
    gathered_copies = jnp.einsum(
        "sqk,krf->sqrf", select_next, weight_pieces, preferred_element_type=jnp.float32
    ).astype(jnp.bfloat16)
    arrived_copies = lax.all_to_all(gathered_copies, "ep", split_axis=1, concat_axis=1, tiled=True)
    next_copies = arrived_copies.reshape(slot_count, local_width, hidden_width)
    return (updated, new_first, new_second, next_copies)


def solution(mesh):
    placed = (
        P("ep", None, "dp"),
        P("ep", None, "dp"),
        P("ep"),
        P(),
        P(),
        P(),
        P("ep", "dp", None),
        P("ep", "dp", None),
        P("ep", "dp", None),
    )
    return jax.shard_map(
        shards,
        mesh=mesh,
        in_specs=placed,
        out_specs=(
            P("ep", "dp", None),
            P("ep", "dp", None),
            P("ep", "dp", None),
            P("ep", "dp", None),
        ),
        check_vma=False,
    )
```

profile of v0, /device:TPU:6, one launch (start us, length us, event | category | flops | bytes accessed | tf_op | source)
XLA Modules:
  0.0 264.1 jit_solution(10217868261258518174)
XLA Ops:
  7.2 0.0 all-gather.2.cloned.1.call-start
  7.2 0.7 all-gather.2.cloned.1.call-update
  7.9 0.7 iota_compare_fusion.6
  8.6 55.4 %all-gather.2.cloned.1.call-done = bf16[2,1792,1024]{2,1,0:T(8,128)(2,1)} async-done(((bf16[2,1792,128]{2,1,0:T(8,128)(2,1)}), bf16[2,1792,1024]{2,1,0:T(8,128)(2,1)}) %all-gather.2.cloned.1.call-update) | async-done | bytes 7340048 | tf_op jit(solution)/shard_map/all_gather | solution.py:57
  64.1 7.5 %fusion.6 = bf16[2,448,1024]{2,1,0:T(8,128)(2,1)S(1)} fusion(bf16[2,1792,1024]{2,1,0:T(8,128)(2,1)} %all-gather.2.cloned.1.call-done, bf16[2,1792,448]{1,2,0:T(8,128)(2,1)} %param.10, pred[2,1792]{1,0:T(4,128)(4,1)S(1)} %iota_compare_fusion.6), kind=kOutput, calls=%fused_computation.10 | convolution fusion | flops 3290857472 | bytes 12389888 | tf_op jit(solution)/shard_map/srd,srk->sdk/dot_general | solution.py:54
  71.6 3.1 %copy.51 = bf16[2,448,1024]{2,0,1:T(2,128)(2,1)} copy(bf16[2,448,1024]{2,1,0:T(8,128)(2,1)S(1)} %fusion.6) | data formatting | bytes 3670016 | tf_op jit(solution)/shard_map/convert_element_type | solution.py:62
  74.7 10.0 %all-to-all-start = ((bf16[2,32,14,1024]{3,0,2,1:T(2,128)(2,1)}), bf16[2,32,14,1024]{3,0,2,1:T(2,128)(2,1)S(1)}, u32[]{:S(2)}, u32[]{:S(2)}) async-start(bf16[2,32,14,1024]{3,0,2,1:T(2,128)(2,1)} %bitcast.18), calls=%async_computation | async-start | bytes 3670016 | tf_op jit(solution)/shard_map/all_to_all | solution.py:61
  84.7 0.0 copy-done
  84.7 0.1 copy.49
  84.8 0.0 copy-done.1
  84.8 0.1 copy.54
  84.9 0.1 fusion.16
  85.0 0.1 fusion.17
  85.2 0.0 copy-done.2
  85.2 0.1 select_reduce_fusion
  85.3 0.1 eq.86
  85.4 0.1 copy.50
  85.5 44.3 %all-to-all-done = bf16[2,32,14,1024]{3,0,2,1:T(2,128)(2,1)S(1)} async-done(((bf16[2,32,14,1024]{3,0,2,1:T(2,128)(2,1)}), bf16[2,32,14,1024]{3,0,2,1:T(2,128)(2,1)S(1)}, u32[]{:S(2)}, u32[]{:S(2)}) %all-to-all-start) | async-done | bytes 1835040 | tf_op jit(solution)/shard_map/all_to_all | solution.py:61
  129.8 0.7 bitcast_convert_fusion
  130.4 0.5 copy.53
  131.0 33.1 %all_to_all.20 = bf16[32,14,1024]{2,1,0:T(8,128)(2,1)S(1)} all-to-all(bf16[32,14,1024]{2,1,0:T(8,128)(2,1)S(1)} %copy.53), channel_id=1, replica_groups=mesh['ep'=32,'dp'=8] {'ep'}, dimensions={0} | all-to-all | bytes 1835008 | tf_op jit(solution)/shard_map/all_to_all | solution.py:74
  164.0 0.2 reshape.95
  164.3 5.0 %fusion.25 = (bf16[1,448,1024]{2,1,0:T(8,128)(2,1)S(1)}, f32[1,448,1024]{2,1,0:T(8,128)}, bf16[1,448,1024]{2,1,0:T(8,128)(2,1)}, bf16[1,448,1024]{2,1,0:T(8,128)(2,1)}) fusion(f32[1,448,1024]{2,1,0:T(8,128)} %param.15, f32[1,448,1024]{2,1,0:T(8,128)S(1)} %reshape.95, bf16[1,448,1024]{2,1,0:T(8,128)(2,1)} %param.17, bf16[1,448,1024]{2,1,0:T(8,128)(2,1)} %param.16), kind=kLoop, calls=%fused_computation.35 | loop fusion | flops 7340032 | bytes 10092544 | tf_op jit(solution)/shard_map/convert_element_type | solution.py:81
  169.3 1.2 reshape.92
  170.5 5.8 %all-to-all-start.2 = ((bf16[32,14,1024]{2,1,0:T(8,128)(2,1)}), bf16[32,14,1024]{2,1,0:T(8,128)(2,1)S(1)}, u32[]{:S(2)}, u32[]{:S(2)}) async-start(bf16[32,14,1024]{2,1,0:T(8,128)(2,1)} %reshape.92), calls=%async_computation.2 | async-start | bytes 2097152 | tf_op jit(solution)/shard_map/all_to_all | solution.py:82
  176.3 0.1 reshape.91
  176.4 0.1 copy.55
  176.5 26.3 %all-to-all-done.2 = bf16[32,14,1024]{2,1,0:T(8,128)(2,1)S(1)} async-done(((bf16[32,14,1024]{2,1,0:T(8,128)(2,1)}), bf16[32,14,1024]{2,1,0:T(8,128)(2,1)S(1)}, u32[]{:S(2)}, u32[]{:S(2)}) %all-to-all-start.2) | async-done | bytes 917536 | tf_op jit(solution)/shard_map/all_to_all | solution.py:82
  202.8 1.5 convolution_convert_fusion
  204.3 1.9 copy.57
  206.2 49.3 %all_to_all.21 = bf16[2,32,14,1024]{3,0,2,1:T(2,128)(2,1)S(1)} all-to-all(bf16[2,32,14,1024]{3,0,2,1:T(2,128)(2,1)S(1)} %copy.57), channel_id=1, replica_groups=mesh['ep'=32,'dp'=8] {'ep'}, dimensions={1} | all-to-all | bytes 3670016 | tf_op jit(solution)/shard_map/all_to_all | solution.py:86
  255.5 1.8 copy.58
  (4 shorter events, 0.0 us)
Async XLA Ops:
  7.2 56.9 %all-gather.2.cloned.1.call-start = ((), (), s32[]{:S(2)}) async-start(), calls=%async_computation.4 | async-start | bytes 8257536 | tf_op jit(solution)/shard_map/all_gather | solution.py:57
  74.7 10.0 %copy-start = (s32[32,8]{0,1:T(8,128)S(1)}, s32[32,8]{0,1:T(8,128)}, u32[]{:S(2)}) copy-start(s32[32,8]{0,1:T(8,128)} %param.12) | copy-start | bytes 3076
  74.7 10.1 %copy-start.1 = (s32[32,8]{0,1:T(8,128)S(1)}, s32[32,8]{0,1:T(8,128)}, u32[]{:S(2)}) copy-start(s32[32,8]{0,1:T(8,128)} %param.13) | copy-start | bytes 3076
  74.7 10.4 %copy-start.2 = (s32[32]{0:T(128)S(1)}, s32[32]{0:T(128)}, u32[]{:S(2)}) copy-start(s32[32]{0:T(128)} %param.14) | copy-start | bytes 388
  74.7 55.0 %all-to-all-start = ((bf16[2,32,14,1024]{3,0,2,1:T(2,128)(2,1)}), bf16[2,32,14,1024]{3,0,2,1:T(2,128)(2,1)S(1)}, u32[]{:S(2)}, u32[]{:S(2)}) async-start(bf16[2,32,14,1024]{3,0,2,1:T(2,128)(2,1)} %bitcast.18), calls=%async_computation | async-start | bytes 3670016 | tf_op jit(solution)/shard_map/all_to_all | solution.py:61
  170.5 32.3 %all-to-all-start.2 = ((bf16[32,14,1024]{2,1,0:T(8,128)(2,1)}), bf16[32,14,1024]{2,1,0:T(8,128)(2,1)S(1)}, u32[]{:S(2)}, u32[]{:S(2)}) async-start(bf16[32,14,1024]{2,1,0:T(8,128)(2,1)} %reshape.92), calls=%async_computation.2 | async-start | bytes 2097152 | tf_op jit(solution)/shard_map/all_to_all | solution.py:82
Sparse Core Ops, SparseCore 0:
  9.8 54.1 all-gather.1
where the time goes:
time: 265 us; the launch traced here: 264 us
  waiting for transfers between devices  127 us (48%)
  blocking collectives  82.4 us (31%)
  starting transfers between devices  15.8 us (6%)
  between operations  14.1 us (5%)
  matrix products  9.67 us (4%)
  local copies, waits for them, and re-layouts  9.23 us (3%)
  other arithmetic  6.13 us (2%)
    all_gather x1, waiting for transfers between devices, shards(): lax.all_gather(hidden_rows, 'dp', axis=2, tiled=True)  55.4 us
    all_to_all x1, blocking collectives, shards(): lax.all_to_all(gathered_copies, 'ep', split_axis=1, concat_axis=1, tiled=...  49.3 us
    all_to_all x1, waiting for transfers between devices, shards(): lax.all_to_all(blocks.astype(jnp.bfloat16), 'ep', split_axis=1, concat_ax...  44.3 us
    all_to_all x1, blocking collectives, shards(): lax.all_to_all(owner_pieces.astype(jnp.bfloat16), 'ep', split_axis=0, con...  33.1 us
    all_to_all x1, waiting for transfers between devices, shards(): lax.all_to_all(weight_blocks, 'ep', split_axis=0, concat_axis=0, tiled=True)  26.3 us
    all_to_all x1, starting transfers between devices, shards(): lax.all_to_all(blocks.astype(jnp.bfloat16), 'ep', split_axis=1, concat_ax...  9.98 us
    dot_general x1, matrix products, shards(): jnp.einsum('srd,srk->sdk', masked, lax.all_gather(hidden_rows, 'dp', axis...  7.54 us
    all_to_all x1, starting transfers between devices, shards(): lax.all_to_all(weight_blocks, 'ep', split_axis=0, concat_axis=0, tiled=True)  5.77 us
  transfers between devices with their start and end apart: 3, of which 3 were waited for; matrix products, arithmetic and copies ran while one was open for 1% of the time, Pallas kernels for 0%

commit v1 on v0

v1 whole, which is shorter than its diff:
```python
import functools

import jax
import jax.numpy as jnp
from jax import lax
from jax.experimental import pallas as pl
from jax.experimental.pallas import tpu as pltpu
from jax.sharding import PartitionSpec as P

beta_first = 0.9
beta_second = 0.95
learn_rate = 0.001
adam_epsilon = 1e-08

ROW_CUTS = 4
COL_CUTS = 8
PIECE = 112
LANES = 128
VMEM = 48 * 1024 * 1024


def any_spec():
    return pl.BlockSpec(memory_space=pl.ANY)


def smem_spec():
    return pl.BlockSpec(memory_space=pltpu.SMEM)


def grad_kernel(slot, place_ref, counts_ref, grad_ref, *refs):
    shard_refs = refs[:8]
    out_ref, grad_v, hidden_v, grad_sem, hidden_sems = refs[8:]
    shards_x = COL_CUTS // 2
    load_grad = pltpu.make_async_copy(grad_ref.at[slot], grad_v, grad_sem)
    load_grad.start()
    loads = []
    for j in range(shards_x):
        for c in range(2):
            src = shard_refs[2 * j + c]
            if len(src.shape) == 3:
                src = src.at[slot]
            load = pltpu.make_async_copy(
                src, hidden_v.at[j, :, pl.ds(c * LANES, LANES)], hidden_sems.at[j, c]
            )
            load.start()
            loads.append(load)
    load_grad.wait()
    count = counts_ref[slot]
    rows = grad_v.shape[1]
    live = lax.broadcasted_iota(jnp.int32, (PIECE, rows), 1) < count
    for r in range(ROW_CUTS):
        cut = grad_v[pl.ds(r * PIECE, PIECE), :]
        grad_v[pl.ds(r * PIECE, PIECE), :] = jnp.where(live, cut, jnp.zeros_like(cut))
    for load in loads:
        load.wait()
    x_here = place_ref[0] // 2
    core_here = lax.rem(place_ref[0], 2)

    @pl.loop(0, shards_x)
    def _(j):
        product = jnp.dot(grad_v[...], hidden_v[j], preferred_element_type=jnp.float32)
        product = product.astype(out_ref.dtype)
        x_there = lax.rem(x_here + j, shards_x)
        for c in range(2):
            column = 2 * x_there + (core_here if c == 0 else 1 - core_here)
            for r in range(ROW_CUTS):
                out_ref[r * COL_CUTS + column] = product[
                    r * PIECE : (r + 1) * PIECE, c * LANES : (c + 1) * LANES
                ]


def slot_gradient(slot, place, counts, grad_t, shards):
    rows = grad_t.shape[2]
    width = grad_t.shape[1]
    return pl.pallas_call(
        functools.partial(grad_kernel, slot),
        out_shape=jax.ShapeDtypeStruct((ROW_CUTS * COL_CUTS, PIECE, LANES), jnp.bfloat16),
        in_specs=[smem_spec(), smem_spec()] + [any_spec()] * 9,
        out_specs=pl.BlockSpec(memory_space=pltpu.VMEM),
        scratch_shapes=[
            pltpu.VMEM((width, rows), jnp.bfloat16),
            pltpu.VMEM((COL_CUTS // 2, rows, 2 * LANES), jnp.bfloat16),
            pltpu.SemaphoreType.DMA,
            pltpu.SemaphoreType.DMA((COL_CUTS // 2, 2)),
        ],
        compiler_params=pltpu.CompilerParams(vmem_limit_bytes=VMEM),
        cost_estimate=pl.CostEstimate(
            flops=2 * width * rows * 1024, bytes_accessed=8_000_000, transcendentals=0
        ),
        name="slot_gradient",
    )(place, counts, grad_t, *shards)


def list_length(lists_ref, e):
    length = jnp.int32(0)
    for j in range(lists_ref.shape[1]):
        length = length + (lists_ref[e, j] >= 0).astype(jnp.int32)
    return length


def sum_kernel(replicas_ref, owners_ref, first_ref, second_ref, out_ref, held, sems):
    loads = [
        pltpu.make_async_copy(src, held.at[s], sems.at[s])
        for s, src in enumerate((first_ref, second_ref))
    ]
    for load in loads:
        load.start()
    for load in loads:
        load.wait()

    @pl.loop(0, replicas_ref.shape[0])
    def _(e):
        def add(j, total):
            g = replicas_ref[e, j]
            return total + held[lax.rem(g, 2), g // 2].astype(jnp.float32)

        total = lax.fori_loop(
            0, list_length(replicas_ref, e), add, jnp.zeros((PIECE, LANES), jnp.float32)
        )
        out_ref[owners_ref[e]] = total.astype(out_ref.dtype)


def sum_copies(replicas, owner_map, first, second):
    pieces = first.shape[0]
    return pl.pallas_call(
        sum_kernel,
        out_shape=jax.ShapeDtypeStruct((pieces, PIECE, LANES), jnp.bfloat16),
        in_specs=[smem_spec(), smem_spec(), any_spec(), any_spec()],
        out_specs=pl.BlockSpec(memory_space=pltpu.VMEM),
        scratch_shapes=[
            pltpu.VMEM((2, pieces, PIECE, LANES), jnp.bfloat16),
            pltpu.SemaphoreType.DMA((2,)),
        ],
        compiler_params=pltpu.CompilerParams(vmem_limit_bytes=VMEM),
        name="sum_copies",
    )(replicas, owner_map, first, second)


def adam_kernel(grad_ref, master_ref, first_ref, second_ref, master_out, first_out, second_out, sent_ref):
    for c in range(COL_CUTS):
        cut = pl.ds(c * LANES, LANES)
        gradient = grad_ref[c].astype(jnp.float32)
        first_new = beta_first * first_ref[0, :, cut].astype(jnp.float32) + (1.0 - beta_first) * gradient
        second_new = (
            beta_second * second_ref[0, :, cut].astype(jnp.float32)
            + (1.0 - beta_second) * gradient * gradient
        )
        updated = master_ref[0, :, cut] - learn_rate * first_new / (jnp.sqrt(second_new) + adam_epsilon)
        master_out[0, :, cut] = updated
        first_out[0, :, cut] = first_new.astype(first_out.dtype)
        second_out[0, :, cut] = second_new.astype(second_out.dtype)
        sent_ref[c] = updated.astype(sent_ref.dtype)


def adam_update(gradient, master, first_moment, second_moment):
    rows = pl.BlockSpec((1, PIECE, COL_CUTS * LANES), lambda r: (0, r, 0))
    pieces = pl.BlockSpec((COL_CUTS, PIECE, LANES), lambda r: (r, 0, 0))
    return pl.pallas_call(
        adam_kernel,
        grid=(ROW_CUTS,),
        out_shape=(
            jax.ShapeDtypeStruct(master.shape, jnp.float32),
            jax.ShapeDtypeStruct(master.shape, jnp.bfloat16),
            jax.ShapeDtypeStruct(master.shape, jnp.bfloat16),
            jax.ShapeDtypeStruct(gradient.shape, jnp.bfloat16),
        ),
        in_specs=[pieces, rows, rows, rows],
        out_specs=(rows, rows, rows, pieces),
        compiler_params=pltpu.CompilerParams(vmem_limit_bytes=VMEM),
        name="adam_update",
    )(gradient, master, first_moment, second_moment)


def spread_kernel(lists_ref, owners_ref, weights_ref, out_ref):
    @pl.loop(0, lists_ref.shape[0])
    def _(e):
        weights = weights_ref[owners_ref[e]]

        def put(j, carry):
            g = lists_ref[e, j]
            out_ref[g // 2, lax.rem(g, 2)] = weights
            return carry

        lax.fori_loop(0, list_length(lists_ref, e), put, 0)


def spread_copies(next_replicas, owner_map, weights):
    pieces = weights.shape[0]
    return pl.pallas_call(
        spread_kernel,
        out_shape=jax.ShapeDtypeStruct((pieces, 2, PIECE, LANES), jnp.bfloat16),
        in_specs=[smem_spec(), smem_spec(), pl.BlockSpec(memory_space=pltpu.VMEM)],
        out_specs=pl.BlockSpec(memory_space=pltpu.VMEM),
        compiler_params=pltpu.CompilerParams(vmem_limit_bytes=VMEM),
        name="spread_copies",
    )(next_replicas, owner_map, weights)


def order_kernel(pieces_ref, out_ref):
    for c in range(COL_CUTS):
        out_ref[0, :, pl.ds(c * LANES, LANES)] = pieces_ref[c, 0]


def order_pieces(pieces):
    width = ROW_CUTS * PIECE
    return pl.pallas_call(
        order_kernel,
        grid=(2, ROW_CUTS),
        out_shape=jax.ShapeDtypeStruct((2, width, COL_CUTS * LANES), jnp.bfloat16),
        in_specs=[pl.BlockSpec((COL_CUTS, 1, PIECE, LANES), lambda s, r: (r, s, 0, 0))],
        out_specs=pl.BlockSpec((1, PIECE, COL_CUTS * LANES), lambda s, r: (s, r, 0)),
        compiler_params=pltpu.CompilerParams(vmem_limit_bytes=VMEM),
        name="order_pieces",
    )(pieces)


def x_shift(array, step):
    pairs = [(2 * x + c, 2 * ((x + step) % 4) + c) for x in range(4) for c in range(2)]
    return lax.ppermute(array, "dp", pairs)


def core_swap(array):
    pairs = [(2 * x + c, 2 * x + 1 - c) for x in range(4) for c in range(2)]
    return lax.ppermute(array, "dp", pairs)


def gather_hidden(own):
    ahead = x_shift(own, -1)
    behind = x_shift(own, 1)
    across = x_shift(own, 2)
    mine = [own, ahead, across, behind]
    return [shard for pair in zip(mine, [core_swap(shard) for shard in mine]) for shard in pair]


def exchange(pieces):
    return lax.all_to_all(pieces, "ep", split_axis=0, concat_axis=0, tiled=True)


def shards(
    hidden_rows,
    out_grad,
    row_counts,
    replicas,
    next_replicas,
    owner_map,
    master,
    first_moment,
    second_moment,
):
    place = lax.axis_index("dp").reshape(1).astype(jnp.int32)
    grad_t = jnp.swapaxes(out_grad, 1, 2)
    hidden_first = gather_hidden(hidden_rows[0])
    later, *hidden_first = lax.optimization_barrier((hidden_rows[1], *hidden_first))
    hidden_second = gather_hidden(later)
    received_first = exchange(slot_gradient(0, place, row_counts, grad_t, hidden_first))
    received_second = exchange(slot_gradient(1, place, row_counts, grad_t, hidden_second))
    owner_pieces = sum_copies(replicas, owner_map, received_first, received_second)
    gradient = exchange(owner_pieces)
    updated, new_first, new_second, weight_pieces = adam_update(
        gradient, master, first_moment, second_moment
    )
    copies = spread_copies(next_replicas, owner_map, exchange(weight_pieces))
    next_copies = order_pieces(exchange(copies))
    return (updated, new_first, new_second, next_copies)


def solution(mesh):
    placed = (
        P("ep", None, "dp"),
        P("ep", None, "dp"),
        P("ep"),
        P(),
        P(),
        P(),
        P("ep", "dp", None),
        P("ep", "dp", None),
        P("ep", "dp", None),
    )
    return jax.shard_map(
        shards,
        mesh=mesh,
        in_specs=placed,
        out_specs=(
            P("ep", "dp", None),
            P("ep", "dp", None),
            P("ep", "dp", None),
            P("ep", "dp", None),
        ),
        check_vma=False,
    )
```

time: 265 us -> 235 us (0.89)
  waiting for transfers between devices: 127 us -> 95.6 us
  Pallas kernels: 0 us -> 23.5 us
  starting transfers between devices: 15.8 us -> 33.2 us
  between operations: 14.1 us -> 0.77 us
  matrix products: 9.67 us -> 0 us
  local copies, waits for them, and re-layouts: 9.23 us -> 1.41 us
  other arithmetic: 6.13 us -> 0 us
  blocking collectives: 82.4 us -> 79.3 us
    all_gather x1 -> x0, waiting for transfers between devices: 55.4 us -> none  [shards(): lax.all_gather(hidden_rows, 'dp', axis=2, tiled=True)]
    ppermute x0 -> x14, waiting for transfers between devices: none -> 46 us  [the longest x6 42.3 us: x_shift(): return lax.ppermute(array, 'dp', pairs)]
    pallas_call x0 -> x6, Pallas kernels: none -> 23.5 us  [the longest x2 11.1 us: slot_gradient(): pl.pallas_call(functools.partial(grad_kernel, slot), out_shape=jax.ShapeD...]
    all_to_all x2 -> x3, waiting for transfers between devices: 70.7 us -> 49.5 us  [exchange(): return lax.all_to_all(pieces, 'ep', split_axis=0, concat_axis=0, tiled=True)]
    all_to_all x2 -> x3, starting transfers between devices: 15.7 us -> 26.7 us  [exchange(): return lax.all_to_all(pieces, 'ep', split_axis=0, concat_axis=0, tiled=True)]
    dot_general x3 -> x0, matrix products: 9.67 us -> none  [the longest x1 7.54 us: shards(): jnp.einsum('srd,srk->sdk', masked, lax.all_gather(hidden_rows, 'dp', axis...]
    ppermute x0 -> x14, starting transfers between devices: none -> 6.54 us  [the longest x6 6.49 us: x_shift(): return lax.ppermute(array, 'dp', pairs)]
    convert_element_type x3 -> x0, local copies, waits for them, and re-layouts: 5.52 us -> none  [the longest x1 3.12 us: shards(): blocks.astype(jnp.bfloat16)]
  transfers between devices with their start and end apart: 3 -> 17, of which waited for: 3 -> 10; matrix products, arithmetic and copies ran while one was open for 1% -> 0% of each run, Pallas kernels for 0% -> 2%
where the time goes in v1:
time: 235 us; the launch traced here: 234 us
  waiting for transfers between devices  95.6 us (41%)
  blocking collectives  79.3 us (34%)
  starting transfers between devices  33.2 us (14%)
  Pallas kernels  23.5 us (10%)
    all_to_all x2, blocking collectives, exchange(): return lax.all_to_all(pieces, 'ep', split_axis=0, concat_axis=0, tiled=True)  79.3 us
    all_to_all x3, waiting for transfers between devices, exchange(): return lax.all_to_all(pieces, 'ep', split_axis=0, concat_axis=0, tiled=True)  49.5 us
    ppermute x6, waiting for transfers between devices, x_shift(): return lax.ppermute(array, 'dp', pairs)  42.3 us
    all_to_all x3, starting transfers between devices, exchange(): return lax.all_to_all(pieces, 'ep', split_axis=0, concat_axis=0, tiled=True)  26.7 us
    pallas_call x2, Pallas kernels, slot_gradient(): pl.pallas_call(functools.partial(grad_kernel, slot), out_shape=jax.ShapeD...  11.1 us
    ppermute x6, starting transfers between devices, x_shift(): return lax.ppermute(array, 'dp', pairs)  6.49 us
  transfers between devices with their start and end apart: 17, of which 10 were waited for; matrix products, arithmetic and copies ran while one was open for 0% of the time, Pallas kernels for 2%

profile of v1, /device:TPU:6, one launch (start us, length us, event | category | flops | bytes accessed | tf_op | source)
XLA Modules:
  0.0 233.7 jit_solution(14692990807820397952)
XLA Ops:
  0.6 1.2 slice_bitcast_fusion
  1.9 2.3 collective-permute-start.5
  4.2 0.7 collective-permute-start.3
  4.8 0.3 collective-permute-start.1
  5.1 10.2 %collective-permute-done.5.refs_6_ = bf16[1792,128]{1,0:T(8,128)(2,1)S(1)} collective-permute-done((bf16[1792,128]{1,0:T(8,128)(2,1)S(1)}, bf16[1792,128]{1,0:T(8,128)(2,1)S(1)}, u32[]{:S(2)}, u32[]{:S(2)}) %collective-permute-start.5) | collective-permute-done | bytes 458784 | tf_op jit(solution)/shard_map/ppermute | solution.py:219
  15.4 3.8 %collective-permute-done.3.refs_4_ = bf16[1792,128]{1,0:T(8,128)(2,1)S(1)} collective-permute-done((bf16[1792,128]{1,0:T(8,128)(2,1)S(1)}, bf16[1792,128]{1,0:T(8,128)(2,1)S(1)}, u32[]{:S(2)}, u32[]{:S(2)}) %collective-permute-start.3) | collective-permute-done | bytes 458784 | tf_op jit(solution)/shard_map/ppermute | solution.py:219
  19.2 6.5 %collective-permute-done.1.refs_2_ = bf16[1792,128]{1,0:T(8,128)(2,1)S(1)} collective-permute-done((bf16[1792,128]{1,0:T(8,128)(2,1)S(1)}, bf16[1792,128]{1,0:T(8,128)(2,1)S(1)}, u32[]{:S(2)}, u32[]{:S(2)}) %collective-permute-start.1) | collective-permute-done | bytes 458784 | tf_op jit(solution)/shard_map/ppermute | solution.py:219
  25.6 0.0 collective-permute-start.2
  25.7 1.9 collective-permute-done.2.refs_3_
  27.6 5.6 %slot_gradient.2 = bf16[32,112,128]{2,1,0:T(8,128)(2,1)} custom-call(s32[1]{0:T(128)} %bitcast.place_ref, s32[2]{0:T(128)S(1)} %copy-done.3, bf16[2,448,1792]{2,1,0:T(8,128)(2,1)} %bitcast.6, bf16[1792,128]{1,0:T(8,128)(2,1)S(1)} %get-tuple-element.17.refs_0_, bf16[1792,128]{1,0:T(8,128)(2,1)S(1)} %collective-permute-done.refs_1_, ...), custom_call_target="tpu_custom_call" | custom-call | flops 1644167168 | bytes 8000000 | tf_op jit(solution)/shard_map/slot_gradient/pallas_call | solution.py:75
  33.2 11.6 %all-to-all-start = ((bf16[32,112,128]{2,1,0:T(8,128)(2,1)}), bf16[32,112,128]{2,1,0:T(8,128)(2,1)S(1)}, u32[]{:S(2)}, u32[]{:S(2)}) async-start(bf16[32,112,128]{2,1,0:T(8,128)(2,1)} %slot_gradient.2), calls=%async_computation | async-start | bytes 1835008 | tf_op jit(solution)/shard_map/all_to_all | solution.py:236
  44.8 1.7 collective-permute-start.12
  46.5 1.4 collective-permute-start.10
  47.9 0.1 collective-permute-start.8
  48.1 10.2 %collective-permute-done.12.refs_6_ = bf16[1792,128]{1,0:T(8,128)(2,1)S(1)} collective-permute-done((bf16[1792,128]{1,0:T(8,128)(2,1)S(1)}, bf16[1792,128]{1,0:T(8,128)(2,1)S(1)}, u32[]{:S(2)}, u32[]{:S(2)}) %collective-permute-start.12) | collective-permute-done | bytes 458784 | tf_op jit(solution)/shard_map/ppermute | solution.py:219
  58.3 3.2 %collective-permute-done.10.refs_4_ = bf16[1792,128]{1,0:T(8,128)(2,1)S(1)} collective-permute-done((bf16[1792,128]{1,0:T(8,128)(2,1)S(1)}, bf16[1792,128]{1,0:T(8,128)(2,1)S(1)}, u32[]{:S(2)}, u32[]{:S(2)}) %collective-permute-start.10) | collective-permute-done | bytes 458784 | tf_op jit(solution)/shard_map/ppermute | solution.py:219
  61.5 8.3 %collective-permute-done.8.refs_2_ = bf16[1792,128]{1,0:T(8,128)(2,1)S(1)} collective-permute-done((bf16[1792,128]{1,0:T(8,128)(2,1)S(1)}, bf16[1792,128]{1,0:T(8,128)(2,1)S(1)}, u32[]{:S(2)}, u32[]{:S(2)}) %collective-permute-start.8) | collective-permute-done | bytes 458784 | tf_op jit(solution)/shard_map/ppermute | solution.py:219
  69.9 0.0 collective-permute-start.9
  69.9 1.8 collective-permute-done.9.refs_3_
  71.7 5.5 %slot_gradient.3 = bf16[32,112,128]{2,1,0:T(8,128)(2,1)} custom-call(s32[1]{0:T(128)} %bitcast.place_ref, s32[2]{0:T(128)S(1)} %copy-done.3, bf16[2,448,1792]{2,1,0:T(8,128)(2,1)} %bitcast.7, bf16[1792,128]{1,0:T(8,128)(2,1)S(1)} %get-tuple-element.25.refs_0_, bf16[1792,128]{1,0:T(8,128)(2,1)S(1)} %collective-permute-done.7.refs_1_, ...), custom_call_target="tpu_custom_call" | custom-call | flops 1644167168 | bytes 8000000 | tf_op jit(solution)/shard_map/slot_gradient/pallas_call | solution.py:75
  77.2 9.5 %all-to-all-start.1 = ((bf16[32,112,128]{2,1,0:T(8,128)(2,1)}), bf16[32,112,128]{2,1,0:T(8,128)(2,1)S(1)}, u32[]{:S(2)}, u32[]{:S(2)}) async-start(bf16[32,112,128]{2,1,0:T(8,128)(2,1)} %slot_gradient.3), calls=%async_computation.1 | async-start | bytes 1835008 | tf_op jit(solution)/shard_map/all_to_all | solution.py:236
  86.7 0.1 copy.13.replicas_ref
  86.8 25.5 %all-to-all-done.1.second_ref = bf16[32,112,128]{2,1,0:T(8,128)(2,1)S(1)} async-done(((bf16[32,112,128]{2,1,0:T(8,128)(2,1)}), bf16[32,112,128]{2,1,0:T(8,128)(2,1)S(1)}, u32[]{:S(2)}, u32[]{:S(2)}) %all-to-all-start.1) | async-done | bytes 917536 | tf_op jit(solution)/shard_map/all_to_all | solution.py:236
  112.3 3.4 %sum_copies.1 = bf16[32,112,128]{2,1,0:T(8,128)(2,1)S(1)} custom-call(s32[32,8]{1,0:T(8,128)S(1)} %copy.13.replicas_ref, s32[32]{0:T(128)S(1)} %copy-done.4, bf16[32,112,128]{2,1,0:T(8,128)(2,1)S(1)} %all-to-all-done.first_ref, bf16[32,112,128]{2,1,0:T(8,128)(2,1)S(1)} %all-to-all-done.1.second_ref), custom_call_target="tpu_custom_call" | custom-call | tf_op jit(solution)/shard_map/sum_copies/pallas_call | solution.py:125
  115.8 30.1 %all_to_all.25.grad_ref = bf16[32,112,128]{2,1,0:T(8,128)(2,1)S(1)} all-to-all(bf16[32,112,128]{2,1,0:T(8,128)(2,1)S(1)} %sum_copies.1), channel_id=1, replica_groups=mesh['ep'=32,'dp'=8] {'ep'}, dimensions={0} | all-to-all | bytes 1835008 | tf_op jit(solution)/shard_map/all_to_all | solution.py:236
  145.8 3.1 %adam_update.1 = (f32[1,448,1024]{2,1,0:T(8,128)}, bf16[1,448,1024]{2,1,0:T(8,128)(2,1)}, bf16[1,448,1024]{2,1,0:T(8,128)(2,1)}, bf16[32,112,128]{2,1,0:T(8,128)(2,1)}) custom-call(bf16[32,112,128]{2,1,0:T(8,128)(2,1)S(1)} %all_to_all.25.grad_ref, f32[1,448,1024]{2,1,0:T(8,128)S(1)} %copy-done, bf16[1,448,1024]{2,1,0:T(8,128)(2,1)S(1)} %copy-done.1, ...), custom_call_target="tpu_custom_call" | custom-call | tf_op jit(solution)/shard_map/adam_update/pallas_call | solution.py:158
  148.9 5.6 %all-to-all-start.3 = ((bf16[32,112,128]{2,1,0:T(8,128)(2,1)}), bf16[32,112,128]{2,1,0:T(8,128)(2,1)S(1)}, u32[]{:S(2)}, u32[]{:S(2)}) async-start(bf16[32,112,128]{2,1,0:T(8,128)(2,1)} %get-tuple-element.29), calls=%async_computation.3 | async-start | bytes 1835008 | tf_op jit(solution)/shard_map/all_to_all | solution.py:236
  154.5 0.1 copy.14.lists_ref
  154.6 24.0 %all-to-all-done.3.weights_ref = bf16[32,112,128]{2,1,0:T(8,128)(2,1)S(1)} async-done(((bf16[32,112,128]{2,1,0:T(8,128)(2,1)}), bf16[32,112,128]{2,1,0:T(8,128)(2,1)S(1)}, u32[]{:S(2)}, u32[]{:S(2)}) %all-to-all-start.3) | async-done | bytes 917536 | tf_op jit(solution)/shard_map/all_to_all | solution.py:236
  178.6 2.7 %spread_copies.1 = bf16[32,2,112,128]{3,2,1,0:T(8,128)(2,1)S(1)} custom-call(s32[32,8]{1,0:T(8,128)S(1)} %copy.14.lists_ref, s32[32]{0:T(128)S(1)} %copy-done.4, bf16[32,112,128]{2,1,0:T(8,128)(2,1)S(1)} %all-to-all-done.3.weights_ref), custom_call_target="tpu_custom_call" | custom-call | tf_op jit(solution)/shard_map/spread_copies/pallas_call | solution.py:189
  181.3 49.2 %all_to_all.26.pieces_ref = bf16[32,2,112,128]{3,2,1,0:T(8,128)(2,1)S(1)} all-to-all(bf16[32,2,112,128]{3,2,1,0:T(8,128)(2,1)S(1)} %spread_copies.1), channel_id=1, replica_groups=mesh['ep'=32,'dp'=8] {'ep'}, dimensions={0} | all-to-all | bytes 3670016 | tf_op jit(solution)/shard_map/all_to_all | solution.py:236
  230.6 3.2 %order_pieces.1 = bf16[2,448,1024]{2,1,0:T(8,128)(2,1)} custom-call(bf16[32,2,112,128]{3,2,1,0:T(8,128)(2,1)S(1)} %all_to_all.26.pieces_ref), custom_call_target="tpu_custom_call" | custom-call | tf_op jit(solution)/shard_map/order_pieces/pallas_call | solution.py:206
  (27 shorter events, 0.1 us)
Async XLA Ops:
  0.6 27.0 %copy-start.3 = (s32[2]{0:T(128)S(1)}, s32[2]{0:T(128)}, u32[]{:S(2)}) copy-start(s32[2]{0:T(128)} %counts_ref.3) | copy-start | bytes 28
  1.9 13.5 %collective-permute-start.5 = (bf16[1792,128]{1,0:T(8,128)(2,1)S(1)}, bf16[1792,128]{1,0:T(8,128)(2,1)S(1)}, u32[]{:S(2)}, u32[]{:S(2)}) collective-permute-start(bf16[1792,128]{1,0:T(8,128)(2,1)S(1)} %get-tuple-element.17.refs_0_), channel_id=1, source_target_pairs={{0,2},{1,3},{2,4},{3,5},{4,6},{5,7},{6,0},{7,1},{8,10},{9,11},{10,... | collective-permute-start | bytes 1376264 | tf_op jit(solution)/shard_map/ppermute | solution.py:219
  4.2 15.0 %collective-permute-start.3 = (bf16[1792,128]{1,0:T(8,128)(2,1)S(1)}, bf16[1792,128]{1,0:T(8,128)(2,1)S(1)}, u32[]{:S(2)}, u32[]{:S(2)}) collective-permute-start(bf16[1792,128]{1,0:T(8,128)(2,1)S(1)} %get-tuple-element.17.refs_0_), channel_id=1, source_target_pairs={{0,4},{1,5},{2,6},{3,7},{4,0},{5,1},{6,2},{7,3},{8,12},{9,13},{10,... | collective-permute-start | bytes 1376264 | tf_op jit(solution)/shard_map/ppermute | solution.py:219
  4.8 20.8 %collective-permute-start.1 = (bf16[1792,128]{1,0:T(8,128)(2,1)S(1)}, bf16[1792,128]{1,0:T(8,128)(2,1)S(1)}, u32[]{:S(2)}, u32[]{:S(2)}) collective-permute-start(bf16[1792,128]{1,0:T(8,128)(2,1)S(1)} %get-tuple-element.17.refs_0_), channel_id=1, source_target_pairs={{0,6},{1,7},{2,0},{3,1},{4,2},{5,3},{6,4},{7,5},{8,14},{9,15},{10,... | collective-permute-start | bytes 1376264 | tf_op jit(solution)/shard_map/ppermute | solution.py:219
  5.1 20.5 %collective-permute-start = (bf16[1792,128]{1,0:T(8,128)(2,1)S(1)}, bf16[1792,128]{1,0:T(8,128)(2,1)S(1)}, u32[]{:S(2)}, u32[]{:S(2)}) collective-permute-start(bf16[1792,128]{1,0:T(8,128)(2,1)S(1)} %get-tuple-element.17.refs_0_), channel_id=1, source_target_pairs={{0,1},{1,0},{2,3},{3,2},{4,5},{5,4},{6,7},{7,6},{8,9},{9,8},{10,11... | collective-permute-start | bytes 1376264 | tf_op jit(solution)/shard_map/ppermute | solution.py:224
  15.3 10.3 %collective-permute-start.6 = (bf16[1792,128]{1,0:T(8,128)(2,1)S(1)}, bf16[1792,128]{1,0:T(8,128)(2,1)S(1)}, u32[]{:S(2)}, u32[]{:S(2)}) collective-permute-start(bf16[1792,128]{1,0:T(8,128)(2,1)S(1)} %collective-permute-done.5.refs_6_), channel_id=1, source_target_pairs={{0,1},{1,0},{2,3},{3,2},{4,5},{5,4},{6,7},{7,6},{8,9},{9,8},{10,11... | collective-permute-start | bytes 1376264 | tf_op jit(solution)/shard_map/ppermute | solution.py:224
  19.2 6.5 %collective-permute-start.4 = (bf16[1792,128]{1,0:T(8,128)(2,1)S(1)}, bf16[1792,128]{1,0:T(8,128)(2,1)}, u32[]{:S(2)}, u32[]{:S(2)}) collective-permute-start(bf16[1792,128]{1,0:T(8,128)(2,1)S(1)} %collective-permute-done.3.refs_4_), channel_id=1, source_target_pairs={{0,1},{1,0},{2,3},{3,2},{4,5},{5,4},{6,7},{7,6},{8,9},{9,8},{10,11... | collective-permute-start | bytes 1376264 | tf_op jit(solution)/shard_map/ppermute | solution.py:224
  25.6 1.9 collective-permute-start.2
  33.2 44.0 %all-to-all-start = ((bf16[32,112,128]{2,1,0:T(8,128)(2,1)}), bf16[32,112,128]{2,1,0:T(8,128)(2,1)S(1)}, u32[]{:S(2)}, u32[]{:S(2)}) async-start(bf16[32,112,128]{2,1,0:T(8,128)(2,1)} %slot_gradient.2), calls=%async_computation | async-start | bytes 1835008 | tf_op jit(solution)/shard_map/all_to_all | solution.py:236
  44.8 13.5 %collective-permute-start.12 = (bf16[1792,128]{1,0:T(8,128)(2,1)S(1)}, bf16[1792,128]{1,0:T(8,128)(2,1)S(1)}, u32[]{:S(2)}, u32[]{:S(2)}) collective-permute-start(bf16[1792,128]{1,0:T(8,128)(2,1)S(1)} %get-tuple-element.25.refs_0_), channel_id=1, source_target_pairs={{0,2},{1,3},{2,4},{3,5},{4,6},{5,7},{6,0},{7,1},{8,10},{9,11},{10,... | collective-permute-start | bytes 1376264 | tf_op jit(solution)/shard_map/ppermute | solution.py:219
  46.5 15.0 %collective-permute-start.10 = (bf16[1792,128]{1,0:T(8,128)(2,1)S(1)}, bf16[1792,128]{1,0:T(8,128)(2,1)S(1)}, u32[]{:S(2)}, u32[]{:S(2)}) collective-permute-start(bf16[1792,128]{1,0:T(8,128)(2,1)S(1)} %get-tuple-element.25.refs_0_), channel_id=1, source_target_pairs={{0,4},{1,5},{2,6},{3,7},{4,0},{5,1},{6,2},{7,3},{8,12},{9,13},{10,... | collective-permute-start | bytes 1376264 | tf_op jit(solution)/shard_map/ppermute | solution.py:219
  47.9 21.9 %collective-permute-start.8 = (bf16[1792,128]{1,0:T(8,128)(2,1)S(1)}, bf16[1792,128]{1,0:T(8,128)(2,1)S(1)}, u32[]{:S(2)}, u32[]{:S(2)}) collective-permute-start(bf16[1792,128]{1,0:T(8,128)(2,1)S(1)} %get-tuple-element.25.refs_0_), channel_id=1, source_target_pairs={{0,6},{1,7},{2,0},{3,1},{4,2},{5,3},{6,4},{7,5},{8,14},{9,15},{10,... | collective-permute-start | bytes 1376264 | tf_op jit(solution)/shard_map/ppermute | solution.py:219
  48.1 21.8 %collective-permute-start.7 = (bf16[1792,128]{1,0:T(8,128)(2,1)S(1)}, bf16[1792,128]{1,0:T(8,128)(2,1)S(1)}, u32[]{:S(2)}, u32[]{:S(2)}) collective-permute-start(bf16[1792,128]{1,0:T(8,128)(2,1)S(1)} %get-tuple-element.25.refs_0_), channel_id=1, source_target_pairs={{0,1},{1,0},{2,3},{3,2},{4,5},{5,4},{6,7},{7,6},{8,9},{9,8},{10,11... | collective-permute-start | bytes 1376264 | tf_op jit(solution)/shard_map/ppermute | solution.py:224
  58.3 11.6 %collective-permute-start.13 = (bf16[1792,128]{1,0:T(8,128)(2,1)S(1)}, bf16[1792,128]{1,0:T(8,128)(2,1)S(1)}, u32[]{:S(2)}, u32[]{:S(2)}) collective-permute-start(bf16[1792,128]{1,0:T(8,128)(2,1)S(1)} %collective-permute-done.12.refs_6_), channel_id=1, source_target_pairs={{0,1},{1,0},{2,3},{3,2},{4,5},{5,4},{6,7},{7,6},{8,9},{9,8},{10,11... | collective-permute-start | bytes 1376264 | tf_op jit(solution)/shard_map/ppermute | solution.py:224
  61.5 8.4 %collective-permute-start.11 = (bf16[1792,128]{1,0:T(8,128)(2,1)S(1)}, bf16[1792,128]{1,0:T(8,128)(2,1)S(1)}, u32[]{:S(2)}, u32[]{:S(2)}) collective-permute-start(bf16[1792,128]{1,0:T(8,128)(2,1)S(1)} %collective-permute-done.10.refs_4_), channel_id=1, source_target_pairs={{0,1},{1,0},{2,3},{3,2},{4,5},{5,4},{6,7},{7,6},{8,9},{9,8},{10,11... | collective-permute-start | bytes 1376264 | tf_op jit(solution)/shard_map/ppermute | solution.py:224
  69.9 1.8 collective-permute-start.9
  77.2 9.6 %copy-start.5 = (s32[32,8]{0,1:T(8,128)S(1)}, s32[32,8]{0,1:T(8,128)}, u32[]{:S(2)}) copy-start(s32[32,8]{0,1:T(8,128)} %param.12) | copy-start | bytes 3076
  77.2 35.1 %copy-start.4 = (s32[32]{0:T(128)S(1)}, s32[32]{0:T(128)}, u32[]{:S(2)}) copy-start(s32[32]{0:T(128)} %owners_ref.3) | copy-start | bytes 388
  77.2 35.1 %all-to-all-start.1 = ((bf16[32,112,128]{2,1,0:T(8,128)(2,1)}), bf16[32,112,128]{2,1,0:T(8,128)(2,1)S(1)}, u32[]{:S(2)}, u32[]{:S(2)}) async-start(bf16[32,112,128]{2,1,0:T(8,128)(2,1)} %slot_gradient.3), calls=%async_computation.1 | async-start | bytes 1835008 | tf_op jit(solution)/shard_map/all_to_all | solution.py:236
  86.8 59.0 %copy-start.1 = (bf16[1,448,1024]{2,1,0:T(8,128)(2,1)S(1)}, bf16[1,448,1024]{2,1,0:T(8,128)(2,1)}, u32[]{:S(2)}) copy-start(bf16[1,448,1024]{2,1,0:T(8,128)(2,1)} %first_ref.1) | copy-start | bytes 2752516
  112.3 33.5 %copy-start = (f32[1,448,1024]{2,1,0:T(8,128)S(1)}, f32[1,448,1024]{2,1,0:T(8,128)}, u32[]{:S(2)}) copy-start(f32[1,448,1024]{2,1,0:T(8,128)} %master_ref.1) | copy-start | bytes 5505028
  112.3 33.5 %copy-start.2 = (bf16[1,448,1024]{2,1,0:T(8,128)(2,1)S(1)}, bf16[1,448,1024]{2,1,0:T(8,128)(2,1)}, u32[]{:S(2)}) copy-start(bf16[1,448,1024]{2,1,0:T(8,128)(2,1)} %second_ref.1) | copy-start | bytes 2752516
  148.9 5.6 %copy-start.6 = (s32[32,8]{0,1:T(8,128)S(1)}, s32[32,8]{0,1:T(8,128)}, u32[]{:S(2)}) copy-start(s32[32,8]{0,1:T(8,128)} %param.13) | copy-start | bytes 3076
  148.9 29.7 %all-to-all-start.3 = ((bf16[32,112,128]{2,1,0:T(8,128)(2,1)}), bf16[32,112,128]{2,1,0:T(8,128)(2,1)S(1)}, u32[]{:S(2)}, u32[]{:S(2)}) async-start(bf16[32,112,128]{2,1,0:T(8,128)(2,1)} %get-tuple-element.29), calls=%async_computation.3 | async-start | bytes 1835008 | tf_op jit(solution)/shard_map/all_to_all | solution.py:236

commit v2 on v1

v2 whole, which is shorter than its diff:
```python
import functools

import jax
import jax.numpy as jnp
from jax import lax
from jax.experimental import pallas as pl
from jax.experimental.pallas import tpu as pltpu
from jax.sharding import PartitionSpec as P

beta_first = 0.9
beta_second = 0.95
learn_rate = 0.001
adam_epsilon = 1e-08

ROW_CUTS = 4
COL_CUTS = 8
PIECE = 112
LANES = 128
VMEM = 48 * 1024 * 1024
VMEM_FAR = 48 * 1024 * 1024
VMEM_ALL = 62 * 1024 * 1024


def any_spec():
    return pl.BlockSpec(memory_space=pl.ANY)


def smem_spec():
    return pl.BlockSpec(memory_space=pltpu.SMEM)


def grad_kernel(slot, columns, place_ref, counts_ref, grad_ref, *refs):
    taken = sum(len(parts) for _, parts in columns)
    part_refs = refs[:taken]
    out_ref, grad_v, hidden_v, grad_sem, hidden_sems = refs[-5:]
    rows = grad_v.shape[1]
    load_grad = pltpu.make_async_copy(grad_ref.at[slot], grad_v, grad_sem)
    load_grad.start()
    loads = []
    at = 0
    for i, (_, parts) in enumerate(columns):
        for core, start, size in parts:
            load = pltpu.make_async_copy(
                part_refs[at],
                hidden_v.at[i, pl.ds(start, size), pl.ds(core * LANES, LANES)],
                hidden_sems.at[at],
            )
            load.start()
            loads.append((i, load))
            at += 1
    load_grad.wait()
    live = lax.broadcasted_iota(jnp.int32, (PIECE, rows), 1) < counts_ref[slot]
    for r in range(ROW_CUTS):
        cut = grad_v[pl.ds(r * PIECE, PIECE), :]
        grad_v[pl.ds(r * PIECE, PIECE), :] = jnp.where(live, cut, jnp.zeros_like(cut))
    x_here = place_ref[0] // 2
    core_here = lax.rem(place_ref[0], 2)
    for i, (step, _) in enumerate(columns):
        for j, load in loads:
            if i == j:
                load.wait()
        product = jnp.dot(grad_v[...], hidden_v[i], preferred_element_type=jnp.float32)
        product = product.astype(out_ref.dtype)
        x_there = lax.rem(x_here + step, COL_CUTS // 2)
        for c in range(2):
            column = 2 * x_there + (core_here if c == 0 else 1 - core_here)
            for r in range(ROW_CUTS):
                out_ref[r * COL_CUTS + column] = product[
                    r * PIECE : (r + 1) * PIECE, c * LANES : (c + 1) * LANES
                ]


def grad_far_kernel(slot, columns, place_ref, counts_ref, grad_ref, *refs):
    *inner, near_ref, out_ref, stage, grad_v, hidden_v, grad_sem, hidden_sems, out_sems = refs
    del near_ref
    grad_kernel(
        slot, columns, place_ref, counts_ref, grad_ref, *inner, stage, grad_v, hidden_v, grad_sem, hidden_sems
    )
    x_there = lax.rem(place_ref[0] // 2 + columns[0][0], COL_CUTS // 2)
    stores = []
    for r in range(ROW_CUTS):
        pair = pl.ds(r * COL_CUTS + 2 * x_there, 2)
        stores.append(pltpu.make_async_copy(stage.at[pair], out_ref.at[pair], out_sems.at[r]))
    for store in stores:
        store.start()
    for store in stores:
        store.wait()


def slot_gradient(slot, place, counts, grad_t, columns, near=None):
    rows = grad_t.shape[2]
    width = grad_t.shape[1]
    parts = [part for _, shard in columns for _, _, part in shard]
    plan = tuple(
        (step, tuple((core, start, part.shape[0]) for core, start, part in shard)) for step, shard in columns
    )
    piece_shape = (ROW_CUTS * COL_CUTS, PIECE, LANES)
    scratch = [
        pltpu.VMEM((width, rows), jnp.bfloat16),
        pltpu.VMEM((len(plan), rows, 2 * LANES), jnp.bfloat16),
        pltpu.SemaphoreType.DMA,
        pltpu.SemaphoreType.DMA((len(parts),)),
    ]
    specs = [smem_spec(), smem_spec()] + [any_spec()] * (1 + len(parts))
    cost = pl.CostEstimate(
        flops=2 * width * rows * 256 * len(plan), bytes_accessed=(2_000_000 + 38_000_000 * slot) * len(plan), transcendentals=0
    )
    if near is None:
        return pl.pallas_call(
            functools.partial(grad_kernel, slot, plan),
            out_shape=jax.ShapeDtypeStruct(piece_shape, jnp.bfloat16),
            in_specs=specs,
            out_specs=pl.BlockSpec(memory_space=pltpu.VMEM),
            scratch_shapes=scratch,
            compiler_params=pltpu.CompilerParams(vmem_limit_bytes=VMEM),
            cost_estimate=cost,
            name="gradient_near",
        )(place, counts, grad_t, *parts)
    return pl.pallas_call(
        functools.partial(grad_far_kernel, slot, plan),
        out_shape=jax.ShapeDtypeStruct(piece_shape, jnp.bfloat16),
        in_specs=specs + [any_spec()],
        out_specs=any_spec(),
        scratch_shapes=[pltpu.VMEM(piece_shape, jnp.bfloat16)]
        + scratch
        + [pltpu.SemaphoreType.DMA((ROW_CUTS,))],
        input_output_aliases={3 + len(parts): 0},
        compiler_params=pltpu.CompilerParams(vmem_limit_bytes=VMEM_FAR),
        cost_estimate=cost,
        name="gradient_far",
    )(place, counts, grad_t, *parts, near)


def list_length(lists_ref, e):
    length = jnp.int32(0)
    for j in range(lists_ref.shape[1]):
        length = length + (lists_ref[e, j] >= 0).astype(jnp.int32)
    return length


def sum_kernel(replicas_ref, owners_ref, first_ref, second_ref, out_ref, held, sems):
    loads = [
        pltpu.make_async_copy(src, held.at[s], sems.at[s])
        for s, src in enumerate((first_ref, second_ref))
    ]
    for load in loads:
        load.start()
    for load in loads:
        load.wait()

    @pl.loop(0, replicas_ref.shape[0])
    def _(e):
        def add(j, total):
            g = replicas_ref[e, j]
            return total + held[lax.rem(g, 2), g // 2].astype(jnp.float32)

        total = lax.fori_loop(
            0, list_length(replicas_ref, e), add, jnp.zeros((PIECE, LANES), jnp.float32)
        )
        out_ref[owners_ref[e]] = total.astype(out_ref.dtype)


def sum_copies(replicas, owner_map, first, second):
    pieces = first.shape[0]
    return pl.pallas_call(
        sum_kernel,
        out_shape=jax.ShapeDtypeStruct((pieces, PIECE, LANES), jnp.bfloat16),
        in_specs=[smem_spec(), smem_spec(), any_spec(), any_spec()],
        out_specs=pl.BlockSpec(memory_space=pltpu.VMEM),
        scratch_shapes=[
            pltpu.VMEM((2, pieces, PIECE, LANES), jnp.bfloat16),
            pltpu.SemaphoreType.DMA((2,)),
        ],
        compiler_params=pltpu.CompilerParams(vmem_limit_bytes=VMEM),
        name="sum_copies",
    )(replicas, owner_map, first, second)


def adam_cut(c, grad_ref, master_ref, first_ref, second_ref):
    cut = pl.ds(c * LANES, LANES)
    gradient = grad_ref[c].astype(jnp.float32)
    first_new = beta_first * first_ref[0, :, cut].astype(jnp.float32) + (1.0 - beta_first) * gradient
    second_new = (
        beta_second * second_ref[0, :, cut].astype(jnp.float32) + (1.0 - beta_second) * gradient * gradient
    )
    updated = master_ref[0, :, cut] - learn_rate * first_new / (jnp.sqrt(second_new) + adam_epsilon)
    return cut, first_new, second_new, updated


def weights_kernel(grad_ref, master_ref, first_ref, second_ref, sent_ref):
    for c in range(COL_CUTS):
        _, _, _, updated = adam_cut(c, grad_ref, master_ref, first_ref, second_ref)
        sent_ref[c] = updated.astype(sent_ref.dtype)


def state_kernel(grad_ref, master_ref, first_ref, second_ref, master_out, first_out, second_out):
    for c in range(COL_CUTS):
        cut, first_new, second_new, updated = adam_cut(c, grad_ref, master_ref, first_ref, second_ref)
        master_out[0, :, cut] = updated
        first_out[0, :, cut] = first_new.astype(first_out.dtype)
        second_out[0, :, cut] = second_new.astype(second_out.dtype)


def adam_update(kernel, name, kinds, gradient, master, first_moment, second_moment):
    rows = pl.BlockSpec((1, PIECE, COL_CUTS * LANES), lambda r: (0, r, 0))
    pieces = pl.BlockSpec((COL_CUTS, PIECE, LANES), lambda r: (r, 0, 0))
    if kinds is None:
        shapes = jax.ShapeDtypeStruct(gradient.shape, jnp.bfloat16)
        out_specs = pieces
    else:
        shapes = tuple(jax.ShapeDtypeStruct(master.shape, kind) for kind in kinds)
        out_specs = (rows,) * len(kinds)
    return pl.pallas_call(
        kernel,
        grid=(ROW_CUTS,),
        out_shape=shapes,
        in_specs=[pieces, rows, rows, rows],
        out_specs=out_specs,
        compiler_params=pltpu.CompilerParams(vmem_limit_bytes=VMEM),
        cost_estimate=pl.CostEstimate(flops=8_000_000, bytes_accessed=9_000_000, transcendentals=0),
        name=name,
    )(gradient, master, first_moment, second_moment)


def spread_kernel(lists_ref, owners_ref, weights_ref, out_ref, sem):
    @pl.loop(0, lists_ref.shape[0])
    def _(e):
        weights = weights_ref.at[owners_ref[e]]

        def put(j, carry):
            g = lists_ref[e, j]
            pltpu.make_async_copy(weights, out_ref.at[g // 2, lax.rem(g, 2)], sem).start()
            return carry

        lax.fori_loop(0, list_length(lists_ref, e), put, 0)

    pltpu.make_async_copy(out_ref, out_ref, sem).wait()


def spread_copies(next_replicas, owner_map, weights):
    pieces = weights.shape[0]
    return pl.pallas_call(
        spread_kernel,
        out_shape=jax.ShapeDtypeStruct((pieces, 2, PIECE, LANES), jnp.bfloat16),
        in_specs=[smem_spec(), smem_spec(), any_spec()],
        out_specs=any_spec(),
        scratch_shapes=[pltpu.SemaphoreType.DMA],
        compiler_params=pltpu.CompilerParams(vmem_limit_bytes=VMEM_ALL),
        name="spread_copies",
    )(next_replicas, owner_map, weights)


def order_kernel(pieces_ref, out_ref, sems):
    moves = []
    for s in range(2):
        for c in range(COL_CUTS):
            moves.append(
                pltpu.make_async_copy(
                    pieces_ref.at[:, c, s],
                    out_ref.at[s, :, :, pl.ds(c * LANES, LANES)],
                    sems.at[s, c],
                )
            )
    for move in moves:
        move.start()
    for move in moves:
        move.wait()


def order_pieces(pieces):
    width = ROW_CUTS * PIECE
    ordered = pl.pallas_call(
        order_kernel,
        out_shape=jax.ShapeDtypeStruct((2, ROW_CUTS, PIECE, COL_CUTS * LANES), jnp.bfloat16),
        in_specs=[any_spec()],
        out_specs=any_spec(),
        scratch_shapes=[pltpu.SemaphoreType.DMA((2, COL_CUTS))],
        compiler_params=pltpu.CompilerParams(vmem_limit_bytes=VMEM),
        name="order_pieces",
    )(pieces.reshape(ROW_CUTS, COL_CUTS, 2, PIECE, LANES))
    return ordered.reshape(2, width, COL_CUTS * LANES)


def x_shift(array, step):
    pairs = [(2 * x + c, 2 * ((x + step) % 4) + c) for x in range(4) for c in range(2)]
    return lax.ppermute(array, "dp", pairs)


def core_swap(array):
    pairs = [(2 * x + c, 2 * x + 1 - c) for x in range(4) for c in range(2)]
    return lax.ppermute(array, "dp", pairs)


def gather_near(own):
    half = own.shape[0] // 2
    ahead = x_shift(own, -1)
    behind = x_shift(own, 1)
    far = (x_shift(behind[:half], 1), x_shift(ahead[half:], -1))
    near = [
        (step, [(0, 0, shard), (1, 0, core_swap(shard))])
        for step, shard in ((0, own), (1, ahead), (3, behind))
    ]
    return near, far, (ahead, behind)


def gather_far(far):
    top, end = far
    half = top.shape[0]
    return [(2, [(0, 0, top), (1, 0, core_swap(top)), (0, half, end), (1, half, core_swap(end))])]


def exchange(pieces):
    return lax.all_to_all(pieces, "ep", split_axis=0, concat_axis=0, tiled=True)


def shards(
    hidden_rows,
    out_grad,
    row_counts,
    replicas,
    next_replicas,
    owner_map,
    master,
    first_moment,
    second_moment,
):
    place = lax.axis_index("dp").reshape(1).astype(jnp.int32)
    grad_t = jnp.swapaxes(out_grad, 1, 2)
    near, far, arrived = gather_near(hidden_rows[0])
    own_later, *_ = lax.optimization_barrier((hidden_rows[1], *arrived))
    near_later, far_later, hop_later = gather_near(own_later)
    pieces = slot_gradient(0, place, row_counts, grad_t, near)
    pieces, *far = lax.optimization_barrier((pieces, *far))
    pieces = slot_gradient(0, place, row_counts, grad_t, gather_far(far), pieces)
    pieces, *_ = lax.optimization_barrier((pieces, *hop_later))
    received_first = exchange(pieces)
    pieces = slot_gradient(1, place, row_counts, grad_t, near_later)
    pieces, *far = lax.optimization_barrier((pieces, *far_later))
    received_second = exchange(slot_gradient(1, place, row_counts, grad_t, gather_far(far), pieces))
    owner_pieces = sum_copies(replicas, owner_map, received_first, received_second)
    gradient = exchange(owner_pieces)
    state = (gradient, master, first_moment, second_moment)
    weight_pieces = adam_update(weights_kernel, "new_weights", None, *state)
    updated, new_first, new_second = adam_update(
        state_kernel, "new_state", (jnp.float32, jnp.bfloat16, jnp.bfloat16), *state
    )
    copies = spread_copies(next_replicas, owner_map, exchange(weight_pieces))
    next_copies = order_pieces(exchange(copies))
    return (updated, new_first, new_second, next_copies)


def solution(mesh):
    placed = (
        P("ep", None, "dp"),
        P("ep", None, "dp"),
        P("ep"),
        P(),
        P(),
        P(),
        P("ep", "dp", None),
        P("ep", "dp", None),
        P("ep", "dp", None),
    )
    return jax.shard_map(
        shards,
        mesh=mesh,
        in_specs=placed,
        out_specs=(
            P("ep", "dp", None),
            P("ep", "dp", None),
            P("ep", "dp", None),
            P("ep", "dp", None),
        ),
        check_vma=False,
    )
```

time: 235 us -> 332 us (1.41)
  Pallas kernels: 23.5 us -> 140 us
  blocking collectives: 79.3 us -> 29.7 us
  waiting for transfers between devices: 95.6 us -> 113 us
  starting transfers between devices: 33.2 us -> 40.5 us
  local copies, waits for them, and re-layouts: 1.41 us -> 6.74 us
    pallas_call x4 -> x7, Pallas kernels: 17.3 us -> 79 us  [the longest x1 56.8 us: order_pieces(): pl.pallas_call(order_kernel, out_shape=jax.ShapeDtypeStruct((2, ROW_CUTS,...]
    pallas_call x1, Pallas kernels: 2.74 us -> 57.7 us  [spread_copies(): pl.pallas_call(spread_kernel, out_shape=jax.ShapeDtypeStruct((pieces, 2,...]
    all_to_all x2 -> x1, blocking collectives: 79.3 us -> 29.7 us  [exchange(): return lax.all_to_all(pieces, 'ep', split_axis=0, concat_axis=0, tiled=True)]
    all_to_all x3 -> x4, waiting for transfers between devices: 49.5 us -> 96.1 us  [exchange(): return lax.all_to_all(pieces, 'ep', split_axis=0, concat_axis=0, tiled=True)]
    ppermute x6 -> x8, waiting for transfers between devices: 42.3 us -> 14.3 us  [x_shift(): return lax.ppermute(array, 'dp', pairs)]
    ppermute x6 -> x8, starting transfers between devices: 6.49 us -> 11.2 us  [x_shift(): return lax.ppermute(array, 'dp', pairs)]
    unnamed x16 -> x28, local copies, waits for them, and re-layouts: 0.18 us -> 4.08 us
    all_to_all x3 -> x4, starting transfers between devices: 26.7 us -> 27 us  [exchange(): return lax.all_to_all(pieces, 'ep', split_axis=0, concat_axis=0, tiled=True)]
  transfers between devices with their start and end apart: 17 -> 22, of which waited for: 10 -> 12; matrix products, arithmetic and copies ran while one was open for 0% -> 1% of each run, Pallas kernels for 2% -> 6%
where the time goes in v2:
time: 332 us
  Pallas kernels  140 us (42%)
  waiting for transfers between devices  113 us (34%)
  starting transfers between devices  40.5 us (12%)
  blocking collectives  29.7 us (9%)
  local copies, waits for them, and re-layouts  6.74 us (2%)
    all_to_all x4, waiting for transfers between devices, exchange(): return lax.all_to_all(pieces, 'ep', split_axis=0, concat_axis=0, tiled=True)  96.1 us
    pallas_call x1, Pallas kernels, spread_copies(): pl.pallas_call(spread_kernel, out_shape=jax.ShapeDtypeStruct((pieces, 2,...  57.7 us
    pallas_call x1, Pallas kernels, order_pieces(): pl.pallas_call(order_kernel, out_shape=jax.ShapeDtypeStruct((2, ROW_CUTS,...  56.8 us
    all_to_all x1, blocking collectives, exchange(): return lax.all_to_all(pieces, 'ep', split_axis=0, concat_axis=0, tiled=True)  29.7 us
    all_to_all x4, starting transfers between devices, exchange(): return lax.all_to_all(pieces, 'ep', split_axis=0, concat_axis=0, tiled=True)  27 us
    ppermute x8, waiting for transfers between devices, x_shift(): return lax.ppermute(array, 'dp', pairs)  14.3 us
    pallas_call x2, Pallas kernels, slot_gradient(): pl.pallas_call(functools.partial(grad_kernel, slot, plan), out_shape=jax....  11.5 us
    ppermute x8, starting transfers between devices, x_shift(): return lax.ppermute(array, 'dp', pairs)  11.2 us
  transfers between devices with their start and end apart: 22, of which 12 were waited for; matrix products, arithmetic and copies ran while one was open for 1% of the time, Pallas kernels for 6%

profile of v2, /device:TPU:6, one launch (start us, length us, event | category | flops | bytes accessed | tf_op | source)
XLA Modules:
  0.0 331.7 jit_solution(6901839279405199822)
XLA Ops:
  0.6 1.2 slice_bitcast_fusion
  1.9 0.9 collective-permute-start.1
  2.8 2.4 collective-permute-start.3
  5.2 10.2 %collective-permute-done.1.refs_2_ = bf16[1792,128]{1,0:T(8,128)(2,1)S(1)} collective-permute-done((bf16[1792,128]{1,0:T(8,128)(2,1)S(1)}, bf16[1792,128]{1,0:T(8,128)(2,1)S(1)}, u32[]{:S(2)}, u32[]{:S(2)}) %collective-permute-start.1) | collective-permute-done | bytes 458784 | tf_op jit(solution)/shard_map/ppermute | solution.py:286
  16.6 2.4 collective-permute-start.5
  19.8 0.8 copy-done.7
  20.6 3.2 collective-permute-start.10
  23.8 1.0 copy-done.8
  24.9 5.9 %gradient_near.2.refs_4_ = bf16[32,112,128]{2,1,0:T(8,128)(2,1)} custom-call(s32[1]{0:T(128)} %bitcast.place_ref, s32[2]{0:T(128)S(1)} %copy-done.9, bf16[2,448,1792]{2,1,0:T(8,128)(2,1)} %bitcast.8, bf16[1792,128]{1,0:T(8,128)(2,1)S(1)} %get-tuple-element.27.refs_0_, bf16[1792,128]{1,0:T(8,128)(2,1)S(1)} %collective-permute-done.refs_1_, ...), custom_call_target="tpu_custom_call" | custom-call | flops 1233125376 | bytes 6000000 | tf_op jit(solution)/shard_map/gradient_near/pallas_call | solution.py:109
  31.4 1.0 collective-permute-done.7.refs_1_
  32.9 3.1 gradient_far.2
  36.0 2.8 collective-permute-done.9.refs_2_
  38.8 11.5 %all-to-all-start = ((bf16[32,112,128]{2,1,0:T(8,128)(2,1)}), bf16[32,112,128]{2,1,0:T(8,128)(2,1)S(1)}, u32[]{:S(2)}, u32[]{:S(2)}) async-start(bf16[32,112,128]{2,1,0:T(8,128)(2,1)} %gradient_far.2), calls=%async_computation | async-start | bytes 1835008 | tf_op jit(solution)/shard_map/all_to_all | solution.py:313
  51.1 2.1 collective-permute-start.15
  53.5 5.6 %gradient_near.3.refs_4_ = bf16[32,112,128]{2,1,0:T(8,128)(2,1)} custom-call(s32[1]{0:T(128)} %bitcast.place_ref, s32[2]{0:T(128)S(1)} %copy-done.9, bf16[2,448,1792]{2,1,0:T(8,128)(2,1)} %bitcast.9, bf16[1792,128]{1,0:T(8,128)(2,1)S(1)} %get-tuple-element.18.refs_0_, bf16[1792,128]{1,0:T(8,128)(2,1)S(1)} %collective-permute-done.11.refs_1_, ...), custom_call_target="tpu_custom_call" | custom-call | flops 1233125376 | bytes 120000000 | tf_op jit(solution)/shard_map/gradient_near/pallas_call | solution.py:109
  59.1 1.2 collective-permute-done.15.refs_2_
  60.9 1.0 collective-permute-done.16.refs_1_
  62.2 2.3 gradient_far.3
  64.5 10.8 %all-to-all-done.first_ref = bf16[32,112,128]{2,1,0:T(8,128)(2,1)S(1)} async-done(((bf16[32,112,128]{2,1,0:T(8,128)(2,1)}), bf16[32,112,128]{2,1,0:T(8,128)(2,1)S(1)}, u32[]{:S(2)}, u32[]{:S(2)}) %all-to-all-start) | async-done | bytes 917536 | tf_op jit(solution)/shard_map/all_to_all | solution.py:313
  75.3 5.4 %all-to-all-start.1 = ((bf16[32,112,128]{2,1,0:T(8,128)(2,1)}), bf16[32,112,128]{2,1,0:T(8,128)(2,1)S(1)}, u32[]{:S(2)}, u32[]{:S(2)}) async-start(bf16[32,112,128]{2,1,0:T(8,128)(2,1)} %gradient_far.3), calls=%async_computation.1 | async-start | bytes 1835008 | tf_op jit(solution)/shard_map/all_to_all | solution.py:313
  80.8 24.0 %all-to-all-done.1.second_ref = bf16[32,112,128]{2,1,0:T(8,128)(2,1)S(1)} async-done(((bf16[32,112,128]{2,1,0:T(8,128)(2,1)}), bf16[32,112,128]{2,1,0:T(8,128)(2,1)S(1)}, u32[]{:S(2)}, u32[]{:S(2)}) %all-to-all-start.1) | async-done | bytes 917536 | tf_op jit(solution)/shard_map/all_to_all | solution.py:313
  104.8 3.4 %sum_copies.1 = bf16[32,112,128]{2,1,0:T(8,128)(2,1)S(1)} custom-call(s32[32,8]{1,0:T(8,128)S(1)} %copy.15.replicas_ref, s32[32]{0:T(128)S(1)} %copy-done.10, bf16[32,112,128]{2,1,0:T(8,128)(2,1)S(1)} %all-to-all-done.first_ref, bf16[32,112,128]{2,1,0:T(8,128)(2,1)S(1)} %all-to-all-done.1.second_ref), custom_call_target="tpu_custom_call" | custom-call | tf_op jit(solution)/shard_map/sum_copies/pallas_call | solution.py:165
  108.2 29.7 %all_to_all.25.grad_ref = bf16[32,112,128]{2,1,0:T(8,128)(2,1)S(1)} all-to-all(bf16[32,112,128]{2,1,0:T(8,128)(2,1)S(1)} %sum_copies.1), channel_id=1, replica_groups=mesh['ep'=32,'dp'=8] {'ep'}, dimensions={0} | all-to-all | bytes 1835008 | tf_op jit(solution)/shard_map/all_to_all | solution.py:313
  138.0 2.4 new_weights.1
  140.4 5.1 %all-to-all-start.3 = ((bf16[32,112,128]{2,1,0:T(8,128)(2,1)}), bf16[32,112,128]{2,1,0:T(8,128)(2,1)}, u32[]{:S(2)}, u32[]{:S(2)}) async-start(bf16[32,112,128]{2,1,0:T(8,128)(2,1)} %new_weights.1), calls=%async_computation.3 | async-start | bytes 1835008 | tf_op jit(solution)/shard_map/all_to_all | solution.py:313
  146.3 23.3 %all-to-all-done.3.weights_ref = bf16[32,112,128]{2,1,0:T(8,128)(2,1)} async-done(((bf16[32,112,128]{2,1,0:T(8,128)(2,1)}), bf16[32,112,128]{2,1,0:T(8,128)(2,1)}, u32[]{:S(2)}, u32[]{:S(2)}) %all-to-all-start.3) | async-done | bytes 917536 | tf_op jit(solution)/shard_map/all_to_all | solution.py:313
  169.6 57.7 %spread_copies.1 = bf16[32,2,112,128]{3,2,1,0:T(8,128)(2,1)} custom-call(s32[32,8]{1,0:T(8,128)} %copy.16.lists_ref, s32[32]{0:T(128)} %owners_ref.3, bf16[32,112,128]{2,1,0:T(8,128)(2,1)} %all-to-all-done.3.weights_ref), custom_call_target="tpu_custom_call" | custom-call | tf_op jit(solution)/shard_map/spread_copies/pallas_call | solution.py:242
  227.3 5.0 %all-to-all-start.4 = ((bf16[32,2,112,128]{3,2,1,0:T(8,128)(2,1)}), bf16[32,2,112,128]{3,2,1,0:T(8,128)(2,1)}, u32[]{:S(2)}, u32[]{:S(2)}) async-start(bf16[32,2,112,128]{3,2,1,0:T(8,128)(2,1)} %spread_copies.1), calls=%async_computation.4 | async-start | bytes 3670016 | tf_op jit(solution)/shard_map/all_to_all | solution.py:313
  232.3 1.5 copy-done.3
  233.8 2.8 new_state.1
  236.7 38.0 %all-to-all-done.4 = bf16[32,2,112,128]{3,2,1,0:T(8,128)(2,1)} async-done(((bf16[32,2,112,128]{3,2,1,0:T(8,128)(2,1)}), bf16[32,2,112,128]{3,2,1,0:T(8,128)(2,1)}, u32[]{:S(2)}, u32[]{:S(2)}) %all-to-all-start.4) | async-done | bytes 1835040 | tf_op jit(solution)/shard_map/all_to_all | solution.py:313
  274.7 56.8 %order_pieces.1 = bf16[2,4,112,1024]{3,2,1,0:T(8,128)(2,1)} custom-call(bf16[4,8,2,112,128]{4,3,2,1,0:T(8,128)(2,1)} %bitcast.4.pieces_ref), custom_call_target="tpu_custom_call" | custom-call | tf_op jit(solution)/shard_map/order_pieces/pallas_call | solution.py:272
  (55 shorter events, 5.8 us)
Async XLA Ops:
  0.6 23.2 %copy-start.9 = (s32[2]{0:T(128)S(1)}, s32[2]{0:T(128)}, u32[]{:S(2)}) copy-start(s32[2]{0:T(128)} %counts_ref.7) | copy-start | bytes 28
  1.9 13.5 %collective-permute-start.1 = (bf16[1792,128]{1,0:T(8,128)(2,1)S(1)}, bf16[1792,128]{1,0:T(8,128)(2,1)S(1)}, u32[]{:S(2)}, u32[]{:S(2)}) collective-permute-start(bf16[1792,128]{1,0:T(8,128)(2,1)S(1)} %get-tuple-element.27.refs_0_), channel_id=1, source_target_pairs={{0,6},{1,7},{2,0},{3,1},{4,2},{5,3},{6,4},{7,5},{8,14},{9,15},{10,... | collective-permute-start | bytes 1376264 | tf_op jit(solution)/shard_map/ppermute | solution.py:286
  2.8 12.6 %collective-permute-start.3 = (bf16[1792,128]{1,0:T(8,128)(2,1)S(1)}, bf16[1792,128]{1,0:T(8,128)(2,1)S(1)}, u32[]{:S(2)}, u32[]{:S(2)}) collective-permute-start(bf16[1792,128]{1,0:T(8,128)(2,1)S(1)} %get-tuple-element.27.refs_0_), channel_id=1, source_target_pairs={{0,2},{1,3},{2,4},{3,5},{4,6},{5,7},{6,0},{7,1},{8,10},{9,11},{10,... | collective-permute-start | bytes 1376264 | tf_op jit(solution)/shard_map/ppermute | solution.py:286
  5.2 14.6 %collective-permute-start = (bf16[1792,128]{1,0:T(8,128)(2,1)S(1)}, bf16[1792,128]{1,0:T(8,128)(2,1)S(1)}, u32[]{:S(2)}, u32[]{:S(2)}) collective-permute-start(bf16[1792,128]{1,0:T(8,128)(2,1)S(1)} %get-tuple-element.27.refs_0_), channel_id=1, source_target_pairs={{0,1},{1,0},{2,3},{3,2},{4,5},{5,4},{6,7},{7,6},{8,9},{9,8},{10,11... | collective-permute-start | bytes 1376264 | tf_op jit(solution)/shard_map/ppermute | solution.py:291
  15.4 4.4 %collective-permute-start.2 = (bf16[1792,128]{1,0:T(8,128)(2,1)S(1)}, bf16[1792,128]{1,0:T(8,128)(2,1)S(1)}, u32[]{:S(2)}, u32[]{:S(2)}) collective-permute-start(bf16[1792,128]{1,0:T(8,128)(2,1)S(1)} %collective-permute-done.1.refs_2_), channel_id=1, source_target_pairs={{0,1},{1,0},{2,3},{3,2},{4,5},{5,4},{6,7},{7,6},{8,9},{9,8},{10,11... | collective-permute-start | bytes 1376264 | tf_op jit(solution)/shard_map/ppermute | solution.py:291
  15.4 8.4 %collective-permute-start.4 = (bf16[1792,128]{1,0:T(8,128)(2,1)S(1)}, bf16[1792,128]{1,0:T(8,128)(2,1)}, u32[]{:S(2)}, u32[]{:S(2)}) collective-permute-start(bf16[1792,128]{1,0:T(8,128)(2,1)S(1)} %collective-permute-done.3.refs_4_), channel_id=1, source_target_pairs={{0,1},{1,0},{2,3},{3,2},{4,5},{5,4},{6,7},{7,6},{8,9},{9,8},{10,11... | collective-permute-start | bytes 1376264 | tf_op jit(solution)/shard_map/ppermute | solution.py:291
  16.6 14.1 %collective-permute-start.5 = (bf16[896,128]{1,0:T(8,128)(2,1)}, bf16[896,128]{1,0:T(8,128)(2,1)S(1)}, u32[]{:S(2)}, u32[]{:S(2)}) collective-permute-start(bf16[896,128]{1,0:T(8,128)(2,1)} %slice.24), channel_id=1, source_target_pairs={{0,2},{1,3},{2,4},{3,5},{4,6},{5,7},{6,0},{7,1},{8,10},{9,11},{10,... | collective-permute-start | bytes 688136 | tf_op jit(solution)/shard_map/ppermute | solution.py:286
  19.8 11.0 %collective-permute-start.6 = (bf16[896,128]{1,0:T(8,128)(2,1)}, bf16[896,128]{1,0:T(8,128)(2,1)}, u32[]{:S(2)}, u32[]{:S(2)}) collective-permute-start(bf16[896,128]{1,0:T(8,128)(2,1)} %slice.25), channel_id=1, source_target_pairs={{0,6},{1,7},{2,0},{3,1},{4,2},{5,3},{6,4},{7,5},{8,14},{9,15},{10,... | collective-permute-start | bytes 688136 | tf_op jit(solution)/shard_map/ppermute | solution.py:286
  19.8 19.0 %collective-permute-start.9 = (bf16[1792,128]{1,0:T(8,128)(2,1)S(1)}, bf16[1792,128]{1,0:T(8,128)(2,1)S(1)}, u32[]{:S(2)}, u32[]{:S(2)}) collective-permute-start(bf16[1792,128]{1,0:T(8,128)(2,1)S(1)} %get-tuple-element.18.refs_0_), channel_id=1, source_target_pairs={{0,6},{1,7},{2,0},{3,1},{4,2},{5,3},{6,4},{7,5},{8,14},{9,15},{10,... | collective-permute-start | bytes 1376264 | tf_op jit(solution)/shard_map/ppermute | solution.py:286
  20.6 18.2 %collective-permute-start.10 = (bf16[1792,128]{1,0:T(8,128)(2,1)S(1)}, bf16[1792,128]{1,0:T(8,128)(2,1)S(1)}, u32[]{:S(2)}, u32[]{:S(2)}) collective-permute-start(bf16[1792,128]{1,0:T(8,128)(2,1)S(1)} %get-tuple-element.18.refs_0_), channel_id=1, source_target_pairs={{0,2},{1,3},{2,4},{3,5},{4,6},{5,7},{6,0},{7,1},{8,10},{9,11},{10,... | collective-permute-start | bytes 1376264 | tf_op jit(solution)/shard_map/ppermute | solution.py:286
  24.9 8.0 %copy-start = (bf16[2,1792,448]{1,2,0:T(8,128)(2,1)S(1)}, bf16[2,1792,448]{1,2,0:T(8,128)(2,1)}, u32[]{:S(2)}) copy-start(bf16[2,1792,448]{1,2,0:T(8,128)(2,1)} %param.10) | copy-start | bytes 9633796
  30.8 1.6 collective-permute-start.7
  30.9 2.0 collective-permute-start.8
  38.8 36.5 %all-to-all-start = ((bf16[32,112,128]{2,1,0:T(8,128)(2,1)}), bf16[32,112,128]{2,1,0:T(8,128)(2,1)S(1)}, u32[]{:S(2)}, u32[]{:S(2)}) async-start(bf16[32,112,128]{2,1,0:T(8,128)(2,1)} %gradient_far.2), calls=%async_computation | async-start | bytes 1835008 | tf_op jit(solution)/shard_map/all_to_all | solution.py:313
  50.3 2.9 collective-permute-start.11
  50.4 2.8 collective-permute-start.12
  50.9 2.6 collective-permute-start.13
  51.0 8.1 %collective-permute-start.14 = (bf16[896,128]{1,0:T(8,128)(2,1)S(1)}, bf16[896,128]{1,0:T(8,128)(2,1)S(1)}, u32[]{:S(2)}, u32[]{:S(2)}) collective-permute-start(bf16[896,128]{1,0:T(8,128)(2,1)S(1)} %slice.26), channel_id=1, source_target_pairs={{0,2},{1,3},{2,4},{3,5},{4,6},{5,7},{6,0},{7,1},{8,10},{9,11},{10,... | collective-permute-start | bytes 688136 | tf_op jit(solution)/shard_map/ppermute | solution.py:286
  51.1 11.1 %copy-start.1 = (bf16[2,1792,448]{1,2,0:T(8,128)(2,1)S(1)}, bf16[2,1792,448]{1,2,0:T(8,128)(2,1)}, u32[]{:S(2)}) copy-start(bf16[2,1792,448]{1,2,0:T(8,128)(2,1)} %param.10) | copy-start | bytes 9633796
  51.1 9.2 %collective-permute-start.15 = (bf16[896,128]{1,0:T(8,128)(2,1)S(1)}, bf16[896,128]{1,0:T(8,128)(2,1)S(1)}, u32[]{:S(2)}, u32[]{:S(2)}) collective-permute-start(bf16[896,128]{1,0:T(8,128)(2,1)S(1)} %slice.27), channel_id=1, source_target_pairs={{0,6},{1,7},{2,0},{3,1},{4,2},{5,3},{6,4},{7,5},{8,14},{9,15},{10,... | collective-permute-start | bytes 688136 | tf_op jit(solution)/shard_map/ppermute | solution.py:286
  60.3 1.5 collective-permute-start.16
  60.3 1.8 collective-permute-start.17
  64.5 16.2 %copy-start.11 = (s32[32,8]{0,1:T(8,128)S(1)}, s32[32,8]{0,1:T(8,128)}, u32[]{:S(2)}) copy-start(s32[32,8]{0,1:T(8,128)} %param.12) | copy-start | bytes 3076
  64.5 40.3 %copy-start.10 = (s32[32]{0:T(128)S(1)}, s32[32]{0:T(128)}, u32[]{:S(2)}) copy-start(s32[32]{0:T(128)} %owners_ref.3) | copy-start | bytes 388
  75.3 29.5 %all-to-all-start.1 = ((bf16[32,112,128]{2,1,0:T(8,128)(2,1)}), bf16[32,112,128]{2,1,0:T(8,128)(2,1)S(1)}, u32[]{:S(2)}, u32[]{:S(2)}) async-start(bf16[32,112,128]{2,1,0:T(8,128)(2,1)} %gradient_far.3), calls=%async_computation.1 | async-start | bytes 1835008 | tf_op jit(solution)/shard_map/all_to_all | solution.py:313
  80.8 57.2 %copy-start.4 = (bf16[1,448,1024]{2,1,0:T(8,128)(2,1)S(1)}, bf16[1,448,1024]{2,1,0:T(8,128)(2,1)}, u32[]{:S(2)}) copy-start(bf16[1,448,1024]{2,1,0:T(8,128)(2,1)} %first_ref.3) | copy-start | bytes 2752516
  104.8 33.2 %copy-start.2 = (f32[1,448,1024]{2,1,0:T(8,128)S(1)}, f32[1,448,1024]{2,1,0:T(8,128)}, u32[]{:S(2)}) copy-start(f32[1,448,1024]{2,1,0:T(8,128)} %master_ref.3) | copy-start | bytes 5505028
  104.8 33.2 %copy-start.5 = (bf16[1,448,1024]{2,1,0:T(8,128)(2,1)S(1)}, bf16[1,448,1024]{2,1,0:T(8,128)(2,1)}, u32[]{:S(2)}) copy-start(bf16[1,448,1024]{2,1,0:T(8,128)(2,1)} %second_ref.3) | copy-start | bytes 2752516
  140.4 5.1 %copy-start.12 = (s32[32,8]{0,1:T(8,128)S(1)}, s32[32,8]{0,1:T(8,128)}, u32[]{:S(2)}) copy-start(s32[32,8]{0,1:T(8,128)} %param.13) | copy-start | bytes 3076
  140.4 29.1 %all-to-all-start.3 = ((bf16[32,112,128]{2,1,0:T(8,128)(2,1)}), bf16[32,112,128]{2,1,0:T(8,128)(2,1)}, u32[]{:S(2)}, u32[]{:S(2)}) async-start(bf16[32,112,128]{2,1,0:T(8,128)(2,1)} %new_weights.1), calls=%async_computation.3 | async-start | bytes 1835008 | tf_op jit(solution)/shard_map/all_to_all | solution.py:313
  227.2 5.1 %copy-start.6 = (bf16[1,448,1024]{2,1,0:T(8,128)(2,1)S(1)}, bf16[1,448,1024]{2,1,0:T(8,128)(2,1)}, u32[]{:S(2)}) copy-start(bf16[1,448,1024]{2,1,0:T(8,128)(2,1)} %second_ref.3) | copy-start | bytes 2752516
  227.3 47.4 %all-to-all-start.4 = ((bf16[32,2,112,128]{3,2,1,0:T(8,128)(2,1)}), bf16[32,2,112,128]{3,2,1,0:T(8,128)(2,1)}, u32[]{:S(2)}, u32[]{:S(2)}) async-start(bf16[32,2,112,128]{3,2,1,0:T(8,128)(2,1)} %spread_copies.1), calls=%async_computation.4 | async-start | bytes 3670016 | tf_op jit(solution)/shard_map/all_to_all | solution.py:313
  (3 other events, 3.3 us)

commit v3 on v2

--- a/solution.py
+++ b/solution.py
@@ -222,19 +222,17 @@
     )(gradient, master, first_moment, second_moment)
 
 
-def spread_kernel(lists_ref, owners_ref, weights_ref, out_ref, sem):
+def spread_kernel(lists_ref, owners_ref, weights_ref, out_ref):
     @pl.loop(0, lists_ref.shape[0])
     def _(e):
-        weights = weights_ref.at[owners_ref[e]]
+        weights = weights_ref[owners_ref[e]]
 
         def put(j, carry):
             g = lists_ref[e, j]
-            pltpu.make_async_copy(weights, out_ref.at[g // 2, lax.rem(g, 2)], sem).start()
+            out_ref[g // 2, lax.rem(g, 2)] = weights
             return carry
 
         lax.fori_loop(0, list_length(lists_ref, e), put, 0)
-
-    pltpu.make_async_copy(out_ref, out_ref, sem).wait()
 
 
 def spread_copies(next_replicas, owner_map, weights):
@@ -242,43 +240,30 @@
     return pl.pallas_call(
         spread_kernel,
         out_shape=jax.ShapeDtypeStruct((pieces, 2, PIECE, LANES), jnp.bfloat16),
-        in_specs=[smem_spec(), smem_spec(), any_spec()],
-        out_specs=any_spec(),
-        scratch_shapes=[pltpu.SemaphoreType.DMA],
+        in_specs=[smem_spec(), smem_spec(), pl.BlockSpec(memory_space=pltpu.VMEM)],
+        out_specs=pl.BlockSpec(memory_space=pltpu.VMEM),
         compiler_params=pltpu.CompilerParams(vmem_limit_bytes=VMEM_ALL),
         name="spread_copies",
     )(next_replicas, owner_map, weights)
 
 
-def order_kernel(pieces_ref, out_ref, sems):
-    moves = []
+def order_kernel(pieces_ref, out_ref):
     for s in range(2):
         for c in range(COL_CUTS):
-            moves.append(
-                pltpu.make_async_copy(
-                    pieces_ref.at[:, c, s],
-                    out_ref.at[s, :, :, pl.ds(c * LANES, LANES)],
-                    sems.at[s, c],
-                )
-            )
-    for move in moves:
-        move.start()
-    for move in moves:
-        move.wait()
+            out_ref[s, :, pl.ds(c * LANES, LANES)] = pieces_ref[c, s]
 
 
 def order_pieces(pieces):
     width = ROW_CUTS * PIECE
-    ordered = pl.pallas_call(
+    return pl.pallas_call(
         order_kernel,
-        out_shape=jax.ShapeDtypeStruct((2, ROW_CUTS, PIECE, COL_CUTS * LANES), jnp.bfloat16),
-        in_specs=[any_spec()],
-        out_specs=any_spec(),
-        scratch_shapes=[pltpu.SemaphoreType.DMA((2, COL_CUTS))],
+        grid=(ROW_CUTS,),
+        out_shape=jax.ShapeDtypeStruct((2, width, COL_CUTS * LANES), jnp.bfloat16),
+        in_specs=[pl.BlockSpec((COL_CUTS, 2, PIECE, LANES), lambda r: (r, 0, 0, 0))],
+        out_specs=pl.BlockSpec((2, PIECE, COL_CUTS * LANES), lambda r: (0, r, 0)),
         compiler_params=pltpu.CompilerParams(vmem_limit_bytes=VMEM),
         name="order_pieces",
-    )(pieces.reshape(ROW_CUTS, COL_CUTS, 2, PIECE, LANES))
-    return ordered.reshape(2, width, COL_CUTS * LANES)
+    )(pieces)
 
 
 def x_shift(array, step):

time: 332 us -> 226 us (0.68)
  Pallas kernels: 140 us -> 33.8 us
    pallas_call x1, Pallas kernels: 57.7 us -> 4.37 us  [spread_copies(): pl.pallas_call(spread_kernel, out_shape=jax.ShapeDtypeStruct((pieces, 2,...]
    pallas_call x1, Pallas kernels: 56.8 us -> 3.83 us  [order_pieces(): pl.pallas_call(order_kernel, grid=(ROW_CUTS,), out_shape=jax.ShapeDtypeSt...]
  transfers between devices with their start and end apart: 22 -> 22, of which waited for: 12 -> 12; matrix products, arithmetic and copies ran while one was open for 1% -> 1% of each run, Pallas kernels for 6% -> 9%
where the time goes in v3:
time: 226 us; the launch traced here: 225 us
  waiting for transfers between devices  113 us (50%)
  starting transfers between devices  40.5 us (18%)
  Pallas kernels  33.8 us (15%)
  blocking collectives  29.7 us (13%)
  local copies, waits for them, and re-layouts  6.74 us (3%)
    all_to_all x4, waiting for transfers between devices, exchange(): return lax.all_to_all(pieces, 'ep', split_axis=0, concat_axis=0, tiled=True)  96.1 us
    all_to_all x1, blocking collectives, exchange(): return lax.all_to_all(pieces, 'ep', split_axis=0, concat_axis=0, tiled=True)  29.7 us
    all_to_all x4, starting transfers between devices, exchange(): return lax.all_to_all(pieces, 'ep', split_axis=0, concat_axis=0, tiled=True)  27 us
    ppermute x8, waiting for transfers between devices, x_shift(): return lax.ppermute(array, 'dp', pairs)  14.3 us
    pallas_call x2, Pallas kernels, slot_gradient(): pl.pallas_call(functools.partial(grad_kernel, slot, plan), out_shape=jax....  11.5 us
    ppermute x8, starting transfers between devices, x_shift(): return lax.ppermute(array, 'dp', pairs)  11.2 us
    pallas_call x2, Pallas kernels, slot_gradient(): pl.pallas_call(functools.partial(grad_far_kernel, slot, plan), out_shape=...  5.37 us
    pallas_call x2, Pallas kernels, adam_update(): pl.pallas_call(kernel, grid=(ROW_CUTS,), out_shape=shapes, in_specs=[piec...  5.28 us
  transfers between devices with their start and end apart: 22, of which 12 were waited for; matrix products, arithmetic and copies ran while one was open for 1% of the time, Pallas kernels for 9%

profile of v3, /device:TPU:6, one launch (start us, length us, event | category | flops | bytes accessed | tf_op | source)
XLA Modules:
  0.0 225.2 jit_solution(17000762434874716510)
XLA Ops:
  0.6 1.2 slice_bitcast_fusion
  1.9 0.9 collective-permute-start.1
  2.8 2.4 %collective-permute-start.3 = (bf16[1792,128]{1,0:T(8,128)(2,1)S(1)}, bf16[1792,128]{1,0:T(8,128)(2,1)S(1)}, u32[]{:S(2)}, u32[]{:S(2)}) collective-permute-start(bf16[1792,128]{1,0:T(8,128)(2,1)S(1)} %get-tuple-element.27.refs_0_), channel_id=1, source_target_pairs={{0,2},{1,3},{2,4},{3,5},{4,6},{5,7},{6,0},{7,1},{8,10},{9,11},{10,... | collective-permute-start | bytes 1376264 | tf_op jit(solution)/shard_map/ppermute | solution.py:271
  5.2 10.2 %collective-permute-done.1.refs_2_ = bf16[1792,128]{1,0:T(8,128)(2,1)S(1)} collective-permute-done((bf16[1792,128]{1,0:T(8,128)(2,1)S(1)}, bf16[1792,128]{1,0:T(8,128)(2,1)S(1)}, u32[]{:S(2)}, u32[]{:S(2)}) %collective-permute-start.1) | collective-permute-done | bytes 458784 | tf_op jit(solution)/shard_map/ppermute | solution.py:271
  16.6 2.4 %collective-permute-start.5 = (bf16[896,128]{1,0:T(8,128)(2,1)}, bf16[896,128]{1,0:T(8,128)(2,1)S(1)}, u32[]{:S(2)}, u32[]{:S(2)}) collective-permute-start(bf16[896,128]{1,0:T(8,128)(2,1)} %slice.24), channel_id=1, source_target_pairs={{0,2},{1,3},{2,4},{3,5},{4,6},{5,7},{6,0},{7,1},{8,10},{9,11},{10,... | collective-permute-start | bytes 688136 | tf_op jit(solution)/shard_map/ppermute | solution.py:271
  19.8 0.8 copy-done.7
  20.6 3.2 %collective-permute-start.10 = (bf16[1792,128]{1,0:T(8,128)(2,1)S(1)}, bf16[1792,128]{1,0:T(8,128)(2,1)S(1)}, u32[]{:S(2)}, u32[]{:S(2)}) collective-permute-start(bf16[1792,128]{1,0:T(8,128)(2,1)S(1)} %get-tuple-element.18.refs_0_), channel_id=1, source_target_pairs={{0,2},{1,3},{2,4},{3,5},{4,6},{5,7},{6,0},{7,1},{8,10},{9,11},{10,... | collective-permute-start | bytes 1376264 | tf_op jit(solution)/shard_map/ppermute | solution.py:271
  23.8 1.0 copy-done.8
  24.9 5.9 %gradient_near.2.refs_4_ = bf16[32,112,128]{2,1,0:T(8,128)(2,1)} custom-call(s32[1]{0:T(128)} %bitcast.place_ref, s32[2]{0:T(128)S(1)} %copy-done.9, bf16[2,448,1792]{2,1,0:T(8,128)(2,1)} %bitcast.6, bf16[1792,128]{1,0:T(8,128)(2,1)S(1)} %get-tuple-element.27.refs_0_, bf16[1792,128]{1,0:T(8,128)(2,1)S(1)} %collective-permute-done.refs_1_, ...), custom_call_target="tpu_custom_call" | custom-call | flops 1233125376 | bytes 6000000 | tf_op jit(solution)/shard_map/gradient_near/pallas_call | solution.py:109
  31.4 1.0 collective-permute-done.7.refs_1_
  32.9 3.1 %gradient_far.2 = bf16[32,112,128]{2,1,0:T(8,128)(2,1)} custom-call(s32[1]{0:T(128)} %bitcast.place_ref, s32[2]{0:T(128)S(1)} %copy-done.9, bf16[2,448,1792]{2,1,0:T(8,128)(2,1)S(1)} %bitcast.8, bf16[896,128]{1,0:T(8,128)(2,1)S(1)} %collective-permute-done.5.refs_0_, ...), custom_call_target="tpu_custom_call", output_to_operand_aliasing={{}: (7, {})} | custom-call | flops 411041792 | bytes 2000000 | tf_op jit(solution)/shard_map/gradient_far/pallas_call | solution.py:119
  36.0 2.8 %collective-permute-done.9.refs_2_ = bf16[1792,128]{1,0:T(8,128)(2,1)S(1)} collective-permute-done((bf16[1792,128]{1,0:T(8,128)(2,1)S(1)}, bf16[1792,128]{1,0:T(8,128)(2,1)S(1)}, u32[]{:S(2)}, u32[]{:S(2)}) %collective-permute-start.9) | collective-permute-done | bytes 458784 | tf_op jit(solution)/shard_map/ppermute | solution.py:271
  38.8 11.5 %all-to-all-start = ((bf16[32,112,128]{2,1,0:T(8,128)(2,1)}), bf16[32,112,128]{2,1,0:T(8,128)(2,1)S(1)}, u32[]{:S(2)}, u32[]{:S(2)}) async-start(bf16[32,112,128]{2,1,0:T(8,128)(2,1)} %gradient_far.2), calls=%async_computation | async-start | bytes 1835008 | tf_op jit(solution)/shard_map/all_to_all | solution.py:298
  51.1 2.1 collective-permute-start.15
  53.5 5.6 %gradient_near.3.refs_4_ = bf16[32,112,128]{2,1,0:T(8,128)(2,1)} custom-call(s32[1]{0:T(128)} %bitcast.place_ref, s32[2]{0:T(128)S(1)} %copy-done.9, bf16[2,448,1792]{2,1,0:T(8,128)(2,1)} %bitcast.7, bf16[1792,128]{1,0:T(8,128)(2,1)S(1)} %get-tuple-element.18.refs_0_, bf16[1792,128]{1,0:T(8,128)(2,1)S(1)} %collective-permute-done.11.refs_1_, ...), custom_call_target="tpu_custom_call" | custom-call | flops 1233125376 | bytes 120000000 | tf_op jit(solution)/shard_map/gradient_near/pallas_call | solution.py:109
  59.1 1.2 collective-permute-done.15.refs_2_
  60.9 1.0 collective-permute-done.16.refs_1_
  62.2 2.3 %gradient_far.3 = bf16[32,112,128]{2,1,0:T(8,128)(2,1)} custom-call(s32[1]{0:T(128)} %bitcast.place_ref, s32[2]{0:T(128)S(1)} %copy-done.9, bf16[2,448,1792]{2,1,0:T(8,128)(2,1)S(1)} %bitcast.9, bf16[896,128]{1,0:T(8,128)(2,1)S(1)} %collective-permute-done.14.refs_0_, ...), custom_call_target="tpu_custom_call", output_to_operand_aliasing={{}: (7, {})} | custom-call | flops 411041792 | bytes 40000000 | tf_op jit(solution)/shard_map/gradient_far/pallas_call | solution.py:119
  64.5 10.8 %all-to-all-done.first_ref = bf16[32,112,128]{2,1,0:T(8,128)(2,1)S(1)} async-done(((bf16[32,112,128]{2,1,0:T(8,128)(2,1)}), bf16[32,112,128]{2,1,0:T(8,128)(2,1)S(1)}, u32[]{:S(2)}, u32[]{:S(2)}) %all-to-all-start) | async-done | bytes 917536 | tf_op jit(solution)/shard_map/all_to_all | solution.py:298
  75.3 5.4 %all-to-all-start.1 = ((bf16[32,112,128]{2,1,0:T(8,128)(2,1)}), bf16[32,112,128]{2,1,0:T(8,128)(2,1)S(1)}, u32[]{:S(2)}, u32[]{:S(2)}) async-start(bf16[32,112,128]{2,1,0:T(8,128)(2,1)} %gradient_far.3), calls=%async_computation.1 | async-start | bytes 1835008 | tf_op jit(solution)/shard_map/all_to_all | solution.py:298
  80.8 24.0 %all-to-all-done.1.second_ref = bf16[32,112,128]{2,1,0:T(8,128)(2,1)S(1)} async-done(((bf16[32,112,128]{2,1,0:T(8,128)(2,1)}), bf16[32,112,128]{2,1,0:T(8,128)(2,1)S(1)}, u32[]{:S(2)}, u32[]{:S(2)}) %all-to-all-start.1) | async-done | bytes 917536 | tf_op jit(solution)/shard_map/all_to_all | solution.py:298
  104.8 3.4 %sum_copies.1 = bf16[32,112,128]{2,1,0:T(8,128)(2,1)S(1)} custom-call(s32[32,8]{1,0:T(8,128)S(1)} %copy.15.replicas_ref, s32[32]{0:T(128)S(1)} %copy-done.10, bf16[32,112,128]{2,1,0:T(8,128)(2,1)S(1)} %all-to-all-done.first_ref, bf16[32,112,128]{2,1,0:T(8,128)(2,1)S(1)} %all-to-all-done.1.second_ref), custom_call_target="tpu_custom_call" | custom-call | tf_op jit(solution)/shard_map/sum_copies/pallas_call | solution.py:165
  108.2 29.7 %all_to_all.25.grad_ref = bf16[32,112,128]{2,1,0:T(8,128)(2,1)S(1)} all-to-all(bf16[32,112,128]{2,1,0:T(8,128)(2,1)S(1)} %sum_copies.1), channel_id=1, replica_groups=mesh['ep'=32,'dp'=8] {'ep'}, dimensions={0} | all-to-all | bytes 1835008 | tf_op jit(solution)/shard_map/all_to_all | solution.py:298
  138.0 2.4 %new_weights.1 = bf16[32,112,128]{2,1,0:T(8,128)(2,1)} custom-call(bf16[32,112,128]{2,1,0:T(8,128)(2,1)S(1)} %all_to_all.25.grad_ref, f32[1,448,1024]{2,1,0:T(8,128)S(1)} %copy-done.2, bf16[1,448,1024]{2,1,0:T(8,128)(2,1)S(1)} %copy-done.4, bf16[1,448,1024]{2,1,0:T(8,128)(2,1)S(1)} %copy-done.5), custom_call_target="tpu_custom_call" | custom-call | flops 8000000 | bytes 9000000 | tf_op jit(solution)/shard_map/new_weights/pallas_call | solution.py:213
  140.4 5.1 %all-to-all-start.3 = ((bf16[32,112,128]{2,1,0:T(8,128)(2,1)}), bf16[32,112,128]{2,1,0:T(8,128)(2,1)}, u32[]{:S(2)}, u32[]{:S(2)}) async-start(bf16[32,112,128]{2,1,0:T(8,128)(2,1)} %new_weights.1), calls=%async_computation.3 | async-start | bytes 1835008 | tf_op jit(solution)/shard_map/all_to_all | solution.py:298
  146.3 23.3 %all-to-all-done.3.weights_ref = bf16[32,112,128]{2,1,0:T(8,128)(2,1)} async-done(((bf16[32,112,128]{2,1,0:T(8,128)(2,1)}), bf16[32,112,128]{2,1,0:T(8,128)(2,1)}, u32[]{:S(2)}, u32[]{:S(2)}) %all-to-all-start.3) | async-done | bytes 917536 | tf_op jit(solution)/shard_map/all_to_all | solution.py:298
  169.6 4.4 %spread_copies.1 = bf16[32,2,112,128]{3,2,1,0:T(8,128)(2,1)} custom-call(s32[32,8]{1,0:T(8,128)} %copy.16.lists_ref, s32[32]{0:T(128)} %owners_ref.3, bf16[32,112,128]{2,1,0:T(8,128)(2,1)} %all-to-all-done.3.weights_ref), custom_call_target="tpu_custom_call" | custom-call | tf_op jit(solution)/shard_map/spread_copies/pallas_call | solution.py:240
  173.9 5.0 %all-to-all-start.4 = ((bf16[32,2,112,128]{3,2,1,0:T(8,128)(2,1)}), bf16[32,2,112,128]{3,2,1,0:T(8,128)(2,1)}, u32[]{:S(2)}, u32[]{:S(2)}) async-start(bf16[32,2,112,128]{3,2,1,0:T(8,128)(2,1)} %spread_copies.1), calls=%async_computation.4 | async-start | bytes 3670016 | tf_op jit(solution)/shard_map/all_to_all | solution.py:298
  179.0 1.5 copy-done.3
  180.5 2.8 %new_state.1 = (f32[1,448,1024]{2,1,0:T(8,128)}, bf16[1,448,1024]{2,1,0:T(8,128)(2,1)}, bf16[1,448,1024]{2,1,0:T(8,128)(2,1)}) custom-call(bf16[32,112,128]{2,1,0:T(8,128)(2,1)S(1)} %all_to_all.25.grad_ref, f32[1,448,1024]{2,1,0:T(8,128)S(1)} %copy-done.3, bf16[1,448,1024]{2,1,0:T(8,128)(2,1)S(1)} %copy-done.4, bf16[1,448,1024]{2,1,0:T(8,128)(2,1)S(1)} %copy-done.6), custom_call_target="tpu_custom_call" | custom-call | flops 8000000 | bytes 9000000 | tf_op jit(solution)/shard_map/new_state/pallas_call | solution.py:213
  183.3 38.0 %all-to-all-done.4.pieces_ref = bf16[32,2,112,128]{3,2,1,0:T(8,128)(2,1)} async-done(((bf16[32,2,112,128]{3,2,1,0:T(8,128)(2,1)}), bf16[32,2,112,128]{3,2,1,0:T(8,128)(2,1)}, u32[]{:S(2)}, u32[]{:S(2)}) %all-to-all-start.4) | async-done | bytes 1835040 | tf_op jit(solution)/shard_map/all_to_all | solution.py:298
  221.3 3.8 %order_pieces.1 = bf16[2,448,1024]{2,1,0:T(8,128)(2,1)} custom-call(bf16[32,2,112,128]{3,2,1,0:T(8,128)(2,1)} %all-to-all-done.4.pieces_ref), custom_call_target="tpu_custom_call" | custom-call | tf_op jit(solution)/shard_map/order_pieces/pallas_call | solution.py:258
  (55 shorter events, 5.8 us)
Async XLA Ops:
  0.6 23.2 %copy-start.9 = (s32[2]{0:T(128)S(1)}, s32[2]{0:T(128)}, u32[]{:S(2)}) copy-start(s32[2]{0:T(128)} %counts_ref.7) | copy-start | bytes 28
  1.9 13.5 %collective-permute-start.1 = (bf16[1792,128]{1,0:T(8,128)(2,1)S(1)}, bf16[1792,128]{1,0:T(8,128)(2,1)S(1)}, u32[]{:S(2)}, u32[]{:S(2)}) collective-permute-start(bf16[1792,128]{1,0:T(8,128)(2,1)S(1)} %get-tuple-element.27.refs_0_), channel_id=1, source_target_pairs={{0,6},{1,7},{2,0},{3,1},{4,2},{5,3},{6,4},{7,5},{8,14},{9,15},{10,... | collective-permute-start | bytes 1376264 | tf_op jit(solution)/shard_map/ppermute | solution.py:271
  2.8 12.6 %collective-permute-start.3 = (bf16[1792,128]{1,0:T(8,128)(2,1)S(1)}, bf16[1792,128]{1,0:T(8,128)(2,1)S(1)}, u32[]{:S(2)}, u32[]{:S(2)}) collective-permute-start(bf16[1792,128]{1,0:T(8,128)(2,1)S(1)} %get-tuple-element.27.refs_0_), channel_id=1, source_target_pairs={{0,2},{1,3},{2,4},{3,5},{4,6},{5,7},{6,0},{7,1},{8,10},{9,11},{10,... | collective-permute-start | bytes 1376264 | tf_op jit(solution)/shard_map/ppermute | solution.py:271
  5.2 14.6 %collective-permute-start = (bf16[1792,128]{1,0:T(8,128)(2,1)S(1)}, bf16[1792,128]{1,0:T(8,128)(2,1)S(1)}, u32[]{:S(2)}, u32[]{:S(2)}) collective-permute-start(bf16[1792,128]{1,0:T(8,128)(2,1)S(1)} %get-tuple-element.27.refs_0_), channel_id=1, source_target_pairs={{0,1},{1,0},{2,3},{3,2},{4,5},{5,4},{6,7},{7,6},{8,9},{9,8},{10,11... | collective-permute-start | bytes 1376264 | tf_op jit(solution)/shard_map/ppermute | solution.py:276
  15.4 4.4 %collective-permute-start.2 = (bf16[1792,128]{1,0:T(8,128)(2,1)S(1)}, bf16[1792,128]{1,0:T(8,128)(2,1)S(1)}, u32[]{:S(2)}, u32[]{:S(2)}) collective-permute-start(bf16[1792,128]{1,0:T(8,128)(2,1)S(1)} %collective-permute-done.1.refs_2_), channel_id=1, source_target_pairs={{0,1},{1,0},{2,3},{3,2},{4,5},{5,4},{6,7},{7,6},{8,9},{9,8},{10,11... | collective-permute-start | bytes 1376264 | tf_op jit(solution)/shard_map/ppermute | solution.py:276
  15.4 8.4 %collective-permute-start.4 = (bf16[1792,128]{1,0:T(8,128)(2,1)S(1)}, bf16[1792,128]{1,0:T(8,128)(2,1)}, u32[]{:S(2)}, u32[]{:S(2)}) collective-permute-start(bf16[1792,128]{1,0:T(8,128)(2,1)S(1)} %collective-permute-done.3.refs_4_), channel_id=1, source_target_pairs={{0,1},{1,0},{2,3},{3,2},{4,5},{5,4},{6,7},{7,6},{8,9},{9,8},{10,11... | collective-permute-start | bytes 1376264 | tf_op jit(solution)/shard_map/ppermute | solution.py:276
  16.6 14.1 %collective-permute-start.5 = (bf16[896,128]{1,0:T(8,128)(2,1)}, bf16[896,128]{1,0:T(8,128)(2,1)S(1)}, u32[]{:S(2)}, u32[]{:S(2)}) collective-permute-start(bf16[896,128]{1,0:T(8,128)(2,1)} %slice.24), channel_id=1, source_target_pairs={{0,2},{1,3},{2,4},{3,5},{4,6},{5,7},{6,0},{7,1},{8,10},{9,11},{10,... | collective-permute-start | bytes 688136 | tf_op jit(solution)/shard_map/ppermute | solution.py:271
  19.8 11.0 %collective-permute-start.6 = (bf16[896,128]{1,0:T(8,128)(2,1)}, bf16[896,128]{1,0:T(8,128)(2,1)}, u32[]{:S(2)}, u32[]{:S(2)}) collective-permute-start(bf16[896,128]{1,0:T(8,128)(2,1)} %slice.25), channel_id=1, source_target_pairs={{0,6},{1,7},{2,0},{3,1},{4,2},{5,3},{6,4},{7,5},{8,14},{9,15},{10,... | collective-permute-start | bytes 688136 | tf_op jit(solution)/shard_map/ppermute | solution.py:271
  19.8 19.0 %collective-permute-start.9 = (bf16[1792,128]{1,0:T(8,128)(2,1)S(1)}, bf16[1792,128]{1,0:T(8,128)(2,1)S(1)}, u32[]{:S(2)}, u32[]{:S(2)}) collective-permute-start(bf16[1792,128]{1,0:T(8,128)(2,1)S(1)} %get-tuple-element.18.refs_0_), channel_id=1, source_target_pairs={{0,6},{1,7},{2,0},{3,1},{4,2},{5,3},{6,4},{7,5},{8,14},{9,15},{10,... | collective-permute-start | bytes 1376264 | tf_op jit(solution)/shard_map/ppermute | solution.py:271
  20.6 18.2 %collective-permute-start.10 = (bf16[1792,128]{1,0:T(8,128)(2,1)S(1)}, bf16[1792,128]{1,0:T(8,128)(2,1)S(1)}, u32[]{:S(2)}, u32[]{:S(2)}) collective-permute-start(bf16[1792,128]{1,0:T(8,128)(2,1)S(1)} %get-tuple-element.18.refs_0_), channel_id=1, source_target_pairs={{0,2},{1,3},{2,4},{3,5},{4,6},{5,7},{6,0},{7,1},{8,10},{9,11},{10,... | collective-permute-start | bytes 1376264 | tf_op jit(solution)/shard_map/ppermute | solution.py:271
  24.9 8.0 %copy-start = (bf16[2,1792,448]{1,2,0:T(8,128)(2,1)S(1)}, bf16[2,1792,448]{1,2,0:T(8,128)(2,1)}, u32[]{:S(2)}) copy-start(bf16[2,1792,448]{1,2,0:T(8,128)(2,1)} %param.10) | copy-start | bytes 9633796
  30.8 1.6 collective-permute-start.7
  30.9 2.0 collective-permute-start.8
  38.8 36.5 %all-to-all-start = ((bf16[32,112,128]{2,1,0:T(8,128)(2,1)}), bf16[32,112,128]{2,1,0:T(8,128)(2,1)S(1)}, u32[]{:S(2)}, u32[]{:S(2)}) async-start(bf16[32,112,128]{2,1,0:T(8,128)(2,1)} %gradient_far.2), calls=%async_computation | async-start | bytes 1835008 | tf_op jit(solution)/shard_map/all_to_all | solution.py:298
  50.3 2.9 %collective-permute-start.11 = (bf16[1792,128]{1,0:T(8,128)(2,1)S(1)}, bf16[1792,128]{1,0:T(8,128)(2,1)S(1)}, u32[]{:S(2)}, u32[]{:S(2)}) collective-permute-start(bf16[1792,128]{1,0:T(8,128)(2,1)S(1)} %get-tuple-element.18.refs_0_), channel_id=1, source_target_pairs={{0,1},{1,0},{2,3},{3,2},{4,5},{5,4},{6,7},{7,6},{8,9},{9,8},{10,11... | collective-permute-start | bytes 1376264 | tf_op jit(solution)/shard_map/ppermute | solution.py:276
  50.4 2.8 %collective-permute-start.12 = (bf16[1792,128]{1,0:T(8,128)(2,1)S(1)}, bf16[1792,128]{1,0:T(8,128)(2,1)S(1)}, u32[]{:S(2)}, u32[]{:S(2)}) collective-permute-start(bf16[1792,128]{1,0:T(8,128)(2,1)S(1)} %collective-permute-done.9.refs_2_), channel_id=1, source_target_pairs={{0,1},{1,0},{2,3},{3,2},{4,5},{5,4},{6,7},{7,6},{8,9},{9,8},{10,11... | collective-permute-start | bytes 1376264 | tf_op jit(solution)/shard_map/ppermute | solution.py:276
  50.9 2.6 %collective-permute-start.13 = (bf16[1792,128]{1,0:T(8,128)(2,1)S(1)}, bf16[1792,128]{1,0:T(8,128)(2,1)S(1)}, u32[]{:S(2)}, u32[]{:S(2)}) collective-permute-start(bf16[1792,128]{1,0:T(8,128)(2,1)S(1)} %collective-permute-done.10.refs_4_), channel_id=1, source_target_pairs={{0,1},{1,0},{2,3},{3,2},{4,5},{5,4},{6,7},{7,6},{8,9},{9,8},{10,11... | collective-permute-start | bytes 1376264 | tf_op jit(solution)/shard_map/ppermute | solution.py:276
  51.0 8.1 %collective-permute-start.14 = (bf16[896,128]{1,0:T(8,128)(2,1)S(1)}, bf16[896,128]{1,0:T(8,128)(2,1)S(1)}, u32[]{:S(2)}, u32[]{:S(2)}) collective-permute-start(bf16[896,128]{1,0:T(8,128)(2,1)S(1)} %slice.26), channel_id=1, source_target_pairs={{0,2},{1,3},{2,4},{3,5},{4,6},{5,7},{6,0},{7,1},{8,10},{9,11},{10,... | collective-permute-start | bytes 688136 | tf_op jit(solution)/shard_map/ppermute | solution.py:271
  51.1 11.1 %copy-start.1 = (bf16[2,1792,448]{1,2,0:T(8,128)(2,1)S(1)}, bf16[2,1792,448]{1,2,0:T(8,128)(2,1)}, u32[]{:S(2)}) copy-start(bf16[2,1792,448]{1,2,0:T(8,128)(2,1)} %param.10) | copy-start | bytes 9633796
  51.1 9.2 %collective-permute-start.15 = (bf16[896,128]{1,0:T(8,128)(2,1)S(1)}, bf16[896,128]{1,0:T(8,128)(2,1)S(1)}, u32[]{:S(2)}, u32[]{:S(2)}) collective-permute-start(bf16[896,128]{1,0:T(8,128)(2,1)S(1)} %slice.27), channel_id=1, source_target_pairs={{0,6},{1,7},{2,0},{3,1},{4,2},{5,3},{6,4},{7,5},{8,14},{9,15},{10,... | collective-permute-start | bytes 688136 | tf_op jit(solution)/shard_map/ppermute | solution.py:271
  60.3 1.5 collective-permute-start.16
  60.3 1.8 collective-permute-start.17
  64.5 16.2 %copy-start.11 = (s32[32,8]{0,1:T(8,128)S(1)}, s32[32,8]{0,1:T(8,128)}, u32[]{:S(2)}) copy-start(s32[32,8]{0,1:T(8,128)} %param.12) | copy-start | bytes 3076
  64.5 40.3 %copy-start.10 = (s32[32]{0:T(128)S(1)}, s32[32]{0:T(128)}, u32[]{:S(2)}) copy-start(s32[32]{0:T(128)} %owners_ref.3) | copy-start | bytes 388
  75.3 29.5 %all-to-all-start.1 = ((bf16[32,112,128]{2,1,0:T(8,128)(2,1)}), bf16[32,112,128]{2,1,0:T(8,128)(2,1)S(1)}, u32[]{:S(2)}, u32[]{:S(2)}) async-start(bf16[32,112,128]{2,1,0:T(8,128)(2,1)} %gradient_far.3), calls=%async_computation.1 | async-start | bytes 1835008 | tf_op jit(solution)/shard_map/all_to_all | solution.py:298
  80.8 57.2 %copy-start.4 = (bf16[1,448,1024]{2,1,0:T(8,128)(2,1)S(1)}, bf16[1,448,1024]{2,1,0:T(8,128)(2,1)}, u32[]{:S(2)}) copy-start(bf16[1,448,1024]{2,1,0:T(8,128)(2,1)} %first_ref.3) | copy-start | bytes 2752516
  104.8 33.2 %copy-start.2 = (f32[1,448,1024]{2,1,0:T(8,128)S(1)}, f32[1,448,1024]{2,1,0:T(8,128)}, u32[]{:S(2)}) copy-start(f32[1,448,1024]{2,1,0:T(8,128)} %master_ref.3) | copy-start | bytes 5505028
  104.8 33.2 %copy-start.5 = (bf16[1,448,1024]{2,1,0:T(8,128)(2,1)S(1)}, bf16[1,448,1024]{2,1,0:T(8,128)(2,1)}, u32[]{:S(2)}) copy-start(bf16[1,448,1024]{2,1,0:T(8,128)(2,1)} %second_ref.3) | copy-start | bytes 2752516
  140.4 5.1 %copy-start.12 = (s32[32,8]{0,1:T(8,128)S(1)}, s32[32,8]{0,1:T(8,128)}, u32[]{:S(2)}) copy-start(s32[32,8]{0,1:T(8,128)} %param.13) | copy-start | bytes 3076
  140.4 29.1 %all-to-all-start.3 = ((bf16[32,112,128]{2,1,0:T(8,128)(2,1)}), bf16[32,112,128]{2,1,0:T(8,128)(2,1)}, u32[]{:S(2)}, u32[]{:S(2)}) async-start(bf16[32,112,128]{2,1,0:T(8,128)(2,1)} %new_weights.1), calls=%async_computation.3 | async-start | bytes 1835008 | tf_op jit(solution)/shard_map/all_to_all | solution.py:298
  173.9 5.0 %copy-start.6 = (bf16[1,448,1024]{2,1,0:T(8,128)(2,1)S(1)}, bf16[1,448,1024]{2,1,0:T(8,128)(2,1)}, u32[]{:S(2)}) copy-start(bf16[1,448,1024]{2,1,0:T(8,128)(2,1)} %second_ref.3) | copy-start | bytes 2752516
  173.9 47.4 %all-to-all-start.4 = ((bf16[32,2,112,128]{3,2,1,0:T(8,128)(2,1)}), bf16[32,2,112,128]{3,2,1,0:T(8,128)(2,1)}, u32[]{:S(2)}, u32[]{:S(2)}) async-start(bf16[32,2,112,128]{3,2,1,0:T(8,128)(2,1)} %spread_copies.1), calls=%async_computation.4 | async-start | bytes 3670016 | tf_op jit(solution)/shard_map/all_to_all | solution.py:298
  (3 other events, 3.3 us)

commit v4 on v3

--- a/solution.py
+++ b/solution.py
@@ -14,10 +14,12 @@
 
 ROW_CUTS = 4
 COL_CUTS = 8
+LEAD = 1
 PIECE = 112
 LANES = 128
 VMEM = 48 * 1024 * 1024
 VMEM_FAR = 48 * 1024 * 1024
+VMEM_LOW = 16 * 1024 * 1024
 VMEM_ALL = 62 * 1024 * 1024
 
 
@@ -30,31 +32,34 @@
 
 
 def grad_kernel(slot, columns, place_ref, counts_ref, grad_ref, *refs):
-    taken = sum(len(parts) for _, parts in columns)
+    taken = sum(choices for _, parts in columns for *_, choices in parts)
     part_refs = refs[:taken]
     out_ref, grad_v, hidden_v, grad_sem, hidden_sems = refs[-5:]
     rows = grad_v.shape[1]
     load_grad = pltpu.make_async_copy(grad_ref.at[slot], grad_v, grad_sem)
     load_grad.start()
+    core_here = lax.rem(place_ref[0], 2)
     loads = []
     at = 0
     for i, (_, parts) in enumerate(columns):
-        for core, start, size in parts:
-            load = pltpu.make_async_copy(
-                part_refs[at],
-                hidden_v.at[i, pl.ds(start, size), pl.ds(core * LANES, LANES)],
-                hidden_sems.at[at],
-            )
-            load.start()
-            loads.append((i, load))
-            at += 1
+        for core, start, size, choices in parts:
+            into = hidden_v.at[i, pl.ds(start, size), pl.ds(core * LANES, LANES)]
+            choice = [
+                pltpu.make_async_copy(part_refs[at + k], into, hidden_sems.at[at]) for k in range(choices)
+            ]
+            if choices == 1:
+                choice[0].start()
+            else:
+                pl.when(core_here == LEAD)(choice[0].start)
+                pl.when(core_here != LEAD)(choice[1].start)
+            loads.append((i, choice[0]))
+            at += choices
     load_grad.wait()
     live = lax.broadcasted_iota(jnp.int32, (PIECE, rows), 1) < counts_ref[slot]
     for r in range(ROW_CUTS):
         cut = grad_v[pl.ds(r * PIECE, PIECE), :]
         grad_v[pl.ds(r * PIECE, PIECE), :] = jnp.where(live, cut, jnp.zeros_like(cut))
     x_here = place_ref[0] // 2
-    core_here = lax.rem(place_ref[0], 2)
     for i, (step, _) in enumerate(columns):
         for j, load in loads:
             if i == j:
@@ -90,9 +95,10 @@
 def slot_gradient(slot, place, counts, grad_t, columns, near=None):
     rows = grad_t.shape[2]
     width = grad_t.shape[1]
-    parts = [part for _, shard in columns for _, _, part in shard]
+    parts = [part for _, shard in columns for _, _, *choices in shard for part in choices]
     plan = tuple(
-        (step, tuple((core, start, part.shape[0]) for core, start, part in shard)) for step, shard in columns
+        (step, tuple((core, start, part[0].shape[0], len(part)) for core, start, *part in shard))
+        for step, shard in columns
     )
     piece_shape = (ROW_CUTS * COL_CUTS, PIECE, LANES)
     scratch = [
@@ -216,23 +222,25 @@
         out_shape=shapes,
         in_specs=[pieces, rows, rows, rows],
         out_specs=out_specs,
-        compiler_params=pltpu.CompilerParams(vmem_limit_bytes=VMEM),
+        compiler_params=pltpu.CompilerParams(vmem_limit_bytes=VMEM if kinds is None else VMEM_LOW),
         cost_estimate=pl.CostEstimate(flops=8_000_000, bytes_accessed=9_000_000, transcendentals=0),
         name=name,
     )(gradient, master, first_moment, second_moment)
 
 
-def spread_kernel(lists_ref, owners_ref, weights_ref, out_ref):
+def spread_kernel(lists_ref, owners_ref, weights_ref, out_ref, sem):
     @pl.loop(0, lists_ref.shape[0])
     def _(e):
-        weights = weights_ref[owners_ref[e]]
+        weights = weights_ref.at[owners_ref[e]]
 
         def put(j, carry):
             g = lists_ref[e, j]
-            out_ref[g // 2, lax.rem(g, 2)] = weights
+            pltpu.make_async_copy(weights, out_ref.at[g // 2, lax.rem(g, 2)], sem).start()
             return carry
 
         lax.fori_loop(0, list_length(lists_ref, e), put, 0)
+
+    pltpu.make_async_copy(out_ref, out_ref, sem).wait()
 
 
 def spread_copies(next_replicas, owner_map, weights):
@@ -241,7 +249,8 @@
         spread_kernel,
         out_shape=jax.ShapeDtypeStruct((pieces, 2, PIECE, LANES), jnp.bfloat16),
         in_specs=[smem_spec(), smem_spec(), pl.BlockSpec(memory_space=pltpu.VMEM)],
-        out_specs=pl.BlockSpec(memory_space=pltpu.VMEM),
+        out_specs=any_spec(),
+        scratch_shapes=[pltpu.SemaphoreType.DMA],
         compiler_params=pltpu.CompilerParams(vmem_limit_bytes=VMEM_ALL),
         name="spread_copies",
     )(next_replicas, owner_map, weights)
@@ -261,13 +270,13 @@
         out_shape=jax.ShapeDtypeStruct((2, width, COL_CUTS * LANES), jnp.bfloat16),
         in_specs=[pl.BlockSpec((COL_CUTS, 2, PIECE, LANES), lambda r: (r, 0, 0, 0))],
         out_specs=pl.BlockSpec((2, PIECE, COL_CUTS * LANES), lambda r: (0, r, 0)),
-        compiler_params=pltpu.CompilerParams(vmem_limit_bytes=VMEM),
+        compiler_params=pltpu.CompilerParams(vmem_limit_bytes=VMEM_LOW),
         name="order_pieces",
     )(pieces)
 
 
-def x_shift(array, step):
-    pairs = [(2 * x + c, 2 * ((x + step) % 4) + c) for x in range(4) for c in range(2)]
+def x_shift(array, step, cores=(0, 1)):
+    pairs = [(2 * x + c, 2 * ((x + step) % 4) + c) for x in range(4) for c in cores]
     return lax.ppermute(array, "dp", pairs)
 
 
@@ -276,11 +285,10 @@
     return lax.ppermute(array, "dp", pairs)
 
 
-def gather_near(own):
-    half = own.shape[0] // 2
+def gather_near(own, way):
     ahead = x_shift(own, -1)
     behind = x_shift(own, 1)
-    far = (x_shift(behind[:half], 1), x_shift(ahead[half:], -1))
+    far = x_shift(behind if way > 0 else ahead, way)
     near = [
         (step, [(0, 0, shard), (1, 0, core_swap(shard))])
         for step, shard in ((0, own), (1, ahead), (3, behind))
@@ -289,9 +297,12 @@
 
 
 def gather_far(far):
-    top, end = far
-    half = top.shape[0]
-    return [(2, [(0, 0, top), (1, 0, core_swap(top)), (0, half, end), (1, half, core_swap(end))])]
+    return [(2, [(0, 0, far), (1, 0, core_swap(far))])]
+
+
+def gather_far_apart(far, behind_swapped):
+    to_lead = lax.ppermute(far, "dp", [(2 * x + 1 - LEAD, 2 * x + LEAD) for x in range(4)])
+    return [(2, [(0, 0, far), (1, 0, to_lead, x_shift(behind_swapped, 1, (1 - LEAD,)))])]
 
 
 def exchange(pieces):
@@ -311,17 +322,16 @@
 ):
     place = lax.axis_index("dp").reshape(1).astype(jnp.int32)
     grad_t = jnp.swapaxes(out_grad, 1, 2)
-    near, far, arrived = gather_near(hidden_rows[0])
+    near, far, arrived = gather_near(hidden_rows[0], 1)
     own_later, *_ = lax.optimization_barrier((hidden_rows[1], *arrived))
-    near_later, far_later, hop_later = gather_near(own_later)
+    near_later, far_later, _ = gather_near(own_later, -1)
     pieces = slot_gradient(0, place, row_counts, grad_t, near)
-    pieces, *far = lax.optimization_barrier((pieces, *far))
+    pieces, far = lax.optimization_barrier((pieces, far))
     pieces = slot_gradient(0, place, row_counts, grad_t, gather_far(far), pieces)
-    pieces, *_ = lax.optimization_barrier((pieces, *hop_later))
+    pieces, _ = lax.optimization_barrier((pieces, near_later[1][1][1][2]))
     received_first = exchange(pieces)
-    pieces = slot_gradient(1, place, row_counts, grad_t, near_later)
-    pieces, *far = lax.optimization_barrier((pieces, *far_later))
-    received_second = exchange(slot_gradient(1, place, row_counts, grad_t, gather_far(far), pieces))
+    columns = near_later + gather_far_apart(far_later, near_later[2][1][1][2])
+    received_second = exchange(slot_gradient(1, place, row_counts, grad_t, columns))
     owner_pieces = sum_copies(replicas, owner_map, received_first, received_second)
     gradient = exchange(owner_pieces)
     state = (gradient, master, first_moment, second_moment)

time: 226 us -> 202 us (0.89)
  waiting for transfers between devices: 113 us -> 101 us
  blocking collectives: 29.7 us -> 22.1 us
  local copies, waits for them, and re-layouts: 6.74 us -> 3.52 us
  Pallas kernels: 33.8 us -> 31.2 us
  starting transfers between devices: 40.5 us -> 42.8 us
    all_to_all x4, waiting for transfers between devices: 96.1 us -> 63 us  [exchange(): return lax.all_to_all(pieces, 'ep', split_axis=0, concat_axis=0, tiled=True)]
    ppermute x8 -> x7, waiting for transfers between devices: 14.3 us -> 37.2 us  [x_shift(): return lax.ppermute(array, 'dp', pairs)]
    all_to_all x1, blocking collectives: 29.7 us -> 22.1 us  [exchange(): return lax.all_to_all(pieces, 'ep', split_axis=0, concat_axis=0, tiled=True)]
    all_to_all x4, starting transfers between devices: 27 us -> 31.2 us  [exchange(): return lax.all_to_all(pieces, 'ep', split_axis=0, concat_axis=0, tiled=True)]
    pallas_call x2 -> x1, Pallas kernels: 5.37 us -> 2.29 us  [slot_gradient(): pl.pallas_call(functools.partial(grad_far_kernel, slot, plan), out_shape=...]
    ppermute x10 -> x7, waiting for transfers between devices: 3.11 us -> 0.41 us  [core_swap(): return lax.ppermute(array, 'dp', pairs)]
    ppermute x8 -> x7, starting transfers between devices: 11.2 us -> 9.71 us  [x_shift(): return lax.ppermute(array, 'dp', pairs)]
  transfers between devices with their start and end apart: 22 -> 19, of which waited for: 12 -> 11; matrix products, arithmetic and copies ran while one was open for 1% -> 0% of each run, Pallas kernels for 9% -> 9%
where the time goes in v4:
time: 202 us; the launch traced here: 201 us
  waiting for transfers between devices  101 us (50%)
  starting transfers between devices  42.8 us (21%)
  Pallas kernels  31.2 us (15%)
  blocking collectives  22.1 us (11%)
  local copies, waits for them, and re-layouts  3.52 us (2%)
    all_to_all x4, waiting for transfers between devices, exchange(): return lax.all_to_all(pieces, 'ep', split_axis=0, concat_axis=0, tiled=True)  63 us
    ppermute x7, waiting for transfers between devices, x_shift(): return lax.ppermute(array, 'dp', pairs)  37.2 us
    all_to_all x4, starting transfers between devices, exchange(): return lax.all_to_all(pieces, 'ep', split_axis=0, concat_axis=0, tiled=True)  31.2 us
    all_to_all x1, blocking collectives, exchange(): return lax.all_to_all(pieces, 'ep', split_axis=0, concat_axis=0, tiled=True)  22.1 us
    pallas_call x2, Pallas kernels, slot_gradient(): pl.pallas_call(functools.partial(grad_kernel, slot, plan), out_shape=jax....  12.9 us
    ppermute x7, starting transfers between devices, x_shift(): return lax.ppermute(array, 'dp', pairs)  9.71 us
    pallas_call x2, Pallas kernels, adam_update(): pl.pallas_call(kernel, grid=(ROW_CUTS,), out_shape=shapes, in_specs=[piec...  5.28 us
  transfers between devices with their start and end apart: 19, of which 11 were waited for; matrix products, arithmetic and copies ran while one was open for 0% of the time, Pallas kernels for 9%

profile of v4, /device:TPU:6, one launch (start us, length us, event | category | flops | bytes accessed | tf_op | source)
XLA Modules:
  0.0 201.1 jit_solution(5347396014677645148)
XLA Ops:
  0.6 1.2 slice_bitcast_fusion
  1.9 2.3 %collective-permute-start.3 = (bf16[1792,128]{1,0:T(8,128)(2,1)S(1)}, bf16[1792,128]{1,0:T(8,128)(2,1)S(1)}, u32[]{:S(2)}, u32[]{:S(2)}) collective-permute-start(bf16[1792,128]{1,0:T(8,128)(2,1)S(1)} %get-tuple-element.19.refs_0_), channel_id=1, source_target_pairs={{0,2},{1,3},{2,4},{3,5},{4,6},{5,7},{6,0},{7,1},{8,10},{9,11},{10,... | collective-permute-start | bytes 1376264 | tf_op jit(solution)/shard_map/ppermute | solution.py:280
  4.2 10.0 %collective-permute-done.3.refs_4_ = bf16[1792,128]{1,0:T(8,128)(2,1)S(1)} collective-permute-done((bf16[1792,128]{1,0:T(8,128)(2,1)S(1)}, bf16[1792,128]{1,0:T(8,128)(2,1)S(1)}, u32[]{:S(2)}, u32[]{:S(2)}) %collective-permute-start.3) | collective-permute-done | bytes 458784 | tf_op jit(solution)/shard_map/ppermute | solution.py:280
  14.2 1.3 collective-permute-done.1.refs_2_
  15.5 0.7 collective-permute-start.5
  16.2 1.3 collective-permute-start.7
  17.6 5.9 %gradient_near.2.refs_2_ = bf16[32,112,128]{2,1,0:T(8,128)(2,1)} custom-call(s32[1]{0:T(128)} %bitcast.place_ref, s32[2]{0:T(128)S(1)} %copy-done.6, bf16[2,448,1792]{2,1,0:T(8,128)(2,1)} %bitcast.6, bf16[1792,128]{1,0:T(8,128)(2,1)S(1)} %get-tuple-element.19.refs_0_, bf16[1792,128]{1,0:T(8,128)(2,1)S(1)} %collective-permute-done.refs_1_, ...), custom_call_target="tpu_custom_call" | custom-call | flops 1233125376 | bytes 6000000 | tf_op jit(solution)/shard_map/gradient_near/pallas_call | solution.py:115
  23.5 5.0 %collective-permute-done.5.refs_0_ = bf16[1792,128]{1,0:T(8,128)(2,1)S(1)} collective-permute-done((bf16[1792,128]{1,0:T(8,128)(2,1)S(1)}, bf16[1792,128]{1,0:T(8,128)(2,1)S(1)}, u32[]{:S(2)}, u32[]{:S(2)}) %collective-permute-start.5) | collective-permute-done | bytes 458784 | tf_op jit(solution)/shard_map/ppermute | solution.py:280
  28.4 1.4 collective-permute-done.7.refs_2_
  30.3 2.3 %gradient_far.1 = bf16[32,112,128]{2,1,0:T(8,128)(2,1)} custom-call(s32[1]{0:T(128)} %bitcast.place_ref, s32[2]{0:T(128)S(1)} %copy-done.6, bf16[2,448,1792]{2,1,0:T(8,128)(2,1)S(1)} %bitcast.8, bf16[1792,128]{1,0:T(8,128)(2,1)S(1)} %collective-permute-done.5.refs_0_, ...), custom_call_target="tpu_custom_call", output_to_operand_aliasing={{}: (5, {})} | custom-call | flops 411041792 | bytes 2000000 | tf_op jit(solution)/shard_map/gradient_far/pallas_call | solution.py:125
  32.6 11.6 %all-to-all-start = ((bf16[32,112,128]{2,1,0:T(8,128)(2,1)}), bf16[32,112,128]{2,1,0:T(8,128)(2,1)S(1)}, u32[]{:S(2)}, u32[]{:S(2)}) async-start(bf16[32,112,128]{2,1,0:T(8,128)(2,1)} %gradient_far.1), calls=%async_computation | async-start | bytes 1835008 | tf_op jit(solution)/shard_map/all_to_all | solution.py:309
  44.2 1.6 collective-permute-start.10
  46.3 10.3 %collective-permute-done.10.refs_4_ = bf16[1792,128]{1,0:T(8,128)(2,1)S(1)} collective-permute-done((bf16[1792,128]{1,0:T(8,128)(2,1)S(1)}, bf16[1792,128]{1,0:T(8,128)(2,1)S(1)}, u32[]{:S(2)}, u32[]{:S(2)}) %collective-permute-start.10) | collective-permute-done | bytes 458784 | tf_op jit(solution)/shard_map/ppermute | solution.py:280
  57.1 2.1 %collective-permute-done.12.refs_6_ = bf16[1792,128]{1,0:T(8,128)(2,1)S(1)} collective-permute-done((bf16[1792,128]{1,0:T(8,128)(2,1)}, bf16[1792,128]{1,0:T(8,128)(2,1)S(1)}, u32[]{:S(2)}, u32[]{:S(2)}) %collective-permute-start.12) | collective-permute-done | bytes 458784 | tf_op jit(solution)/shard_map/ppermute | solution.py:280
  59.2 1.3 collective-permute-start.13
  60.5 3.3 %collective-permute-start.14 = (bf16[1792,128]{1,0:T(8,128)(2,1)S(1)}, bf16[1792,128]{1,0:T(8,128)(2,1)S(1)}, u32[]{:S(2)}, u32[]{:S(2)}) collective-permute-start(bf16[1792,128]{1,0:T(8,128)(2,1)S(1)} %collective-permute-done.11.refs_5_), channel_id=1, source_target_pairs={{0,2},{2,4},{4,6},{6,0},{8,10},{10,12},{12,14},{14,8},{16,18},{18,... | collective-permute-start | bytes 1376264 | tf_op jit(solution)/shard_map/ppermute | solution.py:280
  63.8 7.1 %collective-permute-done.14.refs_8_ = bf16[1792,128]{1,0:T(8,128)(2,1)S(1)} collective-permute-done((bf16[1792,128]{1,0:T(8,128)(2,1)S(1)}, bf16[1792,128]{1,0:T(8,128)(2,1)S(1)}, u32[]{:S(2)}, u32[]{:S(2)}) %collective-permute-start.14) | collective-permute-done | bytes 458784 | tf_op jit(solution)/shard_map/ppermute | solution.py:280
  70.9 7.0 %gradient_near.3 = bf16[32,112,128]{2,1,0:T(8,128)(2,1)} custom-call(s32[1]{0:T(128)} %bitcast.place_ref, s32[2]{0:T(128)S(1)} %copy-done.6, bf16[2,448,1792]{2,1,0:T(8,128)(2,1)} %bitcast.7, bf16[1792,128]{1,0:T(8,128)(2,1)S(1)} %get-tuple-element.13.refs_0_, bf16[1792,128]{1,0:T(8,128)(2,1)S(1)} %collective-permute-done.9.refs_1_, ...), custom_call_target="tpu_custom_call" | custom-call | flops 1644167168 | bytes 160000000 | tf_op jit(solution)/shard_map/gradient_near/pallas_call | solution.py:115
  77.9 9.5 %all-to-all-start.1 = ((bf16[32,112,128]{2,1,0:T(8,128)(2,1)}), bf16[32,112,128]{2,1,0:T(8,128)(2,1)S(1)}, u32[]{:S(2)}, u32[]{:S(2)}) async-start(bf16[32,112,128]{2,1,0:T(8,128)(2,1)} %gradient_near.3), calls=%async_computation.1 | async-start | bytes 1835008 | tf_op jit(solution)/shard_map/all_to_all | solution.py:309
  87.6 17.3 %all-to-all-done.1.second_ref = bf16[32,112,128]{2,1,0:T(8,128)(2,1)S(1)} async-done(((bf16[32,112,128]{2,1,0:T(8,128)(2,1)}), bf16[32,112,128]{2,1,0:T(8,128)(2,1)S(1)}, u32[]{:S(2)}, u32[]{:S(2)}) %all-to-all-start.1) | async-done | bytes 917536 | tf_op jit(solution)/shard_map/all_to_all | solution.py:309
  104.9 3.4 %sum_copies.1 = bf16[32,112,128]{2,1,0:T(8,128)(2,1)S(1)} custom-call(s32[32,8]{1,0:T(8,128)S(1)} %copy.14.replicas_ref, s32[32]{0:T(128)S(1)} %copy-done.7, bf16[32,112,128]{2,1,0:T(8,128)(2,1)S(1)} %all-to-all-done.first_ref, bf16[32,112,128]{2,1,0:T(8,128)(2,1)S(1)} %all-to-all-done.1.second_ref), custom_call_target="tpu_custom_call" | custom-call | tf_op jit(solution)/shard_map/sum_copies/pallas_call | solution.py:171
  108.4 22.1 %all_to_all.25.grad_ref = bf16[32,112,128]{2,1,0:T(8,128)(2,1)S(1)} all-to-all(bf16[32,112,128]{2,1,0:T(8,128)(2,1)S(1)} %sum_copies.1), channel_id=1, replica_groups=mesh['ep'=32,'dp'=8] {'ep'}, dimensions={0} | all-to-all | bytes 1835008 | tf_op jit(solution)/shard_map/all_to_all | solution.py:309
  130.5 2.4 %new_weights.1 = bf16[32,112,128]{2,1,0:T(8,128)(2,1)} custom-call(bf16[32,112,128]{2,1,0:T(8,128)(2,1)S(1)} %all_to_all.25.grad_ref, f32[1,448,1024]{2,1,0:T(8,128)S(1)} %copy-done.1, bf16[1,448,1024]{2,1,0:T(8,128)(2,1)S(1)} %copy-done.3, bf16[1,448,1024]{2,1,0:T(8,128)(2,1)S(1)} %copy-done.4), custom_call_target="tpu_custom_call" | custom-call | flops 8000000 | bytes 9000000 | tf_op jit(solution)/shard_map/new_weights/pallas_call | solution.py:219
  132.9 5.0 %all-to-all-start.3 = ((bf16[32,112,128]{2,1,0:T(8,128)(2,1)}), bf16[32,112,128]{2,1,0:T(8,128)(2,1)}, u32[]{:S(2)}, u32[]{:S(2)}) async-start(bf16[32,112,128]{2,1,0:T(8,128)(2,1)} %new_weights.1), calls=%async_computation.3 | async-start | bytes 1835008 | tf_op jit(solution)/shard_map/all_to_all | solution.py:309
  138.0 0.7 copy.15.lists_ref
  138.6 16.5 %all-to-all-done.3.weights_ref = bf16[32,112,128]{2,1,0:T(8,128)(2,1)} async-done(((bf16[32,112,128]{2,1,0:T(8,128)(2,1)}), bf16[32,112,128]{2,1,0:T(8,128)(2,1)}, u32[]{:S(2)}, u32[]{:S(2)}) %all-to-all-start.3) | async-done | bytes 917536 | tf_op jit(solution)/shard_map/all_to_all | solution.py:309
  155.2 3.5 %spread_copies.1 = bf16[32,2,112,128]{3,2,1,0:T(8,128)(2,1)} custom-call(s32[32,8]{1,0:T(8,128)} %copy.15.lists_ref, s32[32]{0:T(128)} %owners_ref.3, bf16[32,112,128]{2,1,0:T(8,128)(2,1)} %all-to-all-done.3.weights_ref), custom_call_target="tpu_custom_call" | custom-call | tf_op jit(solution)/shard_map/spread_copies/pallas_call | solution.py:248
  158.6 5.1 %all-to-all-start.4 = ((bf16[32,2,112,128]{3,2,1,0:T(8,128)(2,1)}), bf16[32,2,112,128]{3,2,1,0:T(8,128)(2,1)}, u32[]{:S(2)}, u32[]{:S(2)}) async-start(bf16[32,2,112,128]{3,2,1,0:T(8,128)(2,1)} %spread_copies.1), calls=%async_computation.4 | async-start | bytes 3670016 | tf_op jit(solution)/shard_map/all_to_all | solution.py:309
  163.8 1.5 copy-done.2
  165.3 2.8 %new_state.1 = (f32[1,448,1024]{2,1,0:T(8,128)}, bf16[1,448,1024]{2,1,0:T(8,128)(2,1)}, bf16[1,448,1024]{2,1,0:T(8,128)(2,1)}) custom-call(bf16[32,112,128]{2,1,0:T(8,128)(2,1)S(1)} %all_to_all.25.grad_ref, f32[1,448,1024]{2,1,0:T(8,128)S(1)} %copy-done.2, bf16[1,448,1024]{2,1,0:T(8,128)(2,1)S(1)} %copy-done.3, bf16[1,448,1024]{2,1,0:T(8,128)(2,1)S(1)} %copy-done.5), custom_call_target="tpu_custom_call" | custom-call | flops 8000000 | bytes 9000000 | tf_op jit(solution)/shard_map/new_state/pallas_call | solution.py:219
  168.1 29.1 %all-to-all-done.4.pieces_ref = bf16[32,2,112,128]{3,2,1,0:T(8,128)(2,1)} async-done(((bf16[32,2,112,128]{3,2,1,0:T(8,128)(2,1)}), bf16[32,2,112,128]{3,2,1,0:T(8,128)(2,1)}, u32[]{:S(2)}, u32[]{:S(2)}) %all-to-all-start.4) | async-done | bytes 1835040 | tf_op jit(solution)/shard_map/all_to_all | solution.py:309
  197.2 3.8 %order_pieces.1 = bf16[2,448,1024]{2,1,0:T(8,128)(2,1)} custom-call(bf16[32,2,112,128]{3,2,1,0:T(8,128)(2,1)} %all-to-all-done.4.pieces_ref), custom_call_target="tpu_custom_call" | custom-call | tf_op jit(solution)/shard_map/order_pieces/pallas_call | solution.py:267
  (38 shorter events, 1.6 us)
Async XLA Ops:
  0.6 16.9 %copy-start.6 = (s32[2]{0:T(128)S(1)}, s32[2]{0:T(128)}, u32[]{:S(2)}) copy-start(s32[2]{0:T(128)} %counts_ref.5) | copy-start | bytes 28
  1.9 12.3 %collective-permute-start.3 = (bf16[1792,128]{1,0:T(8,128)(2,1)S(1)}, bf16[1792,128]{1,0:T(8,128)(2,1)S(1)}, u32[]{:S(2)}, u32[]{:S(2)}) collective-permute-start(bf16[1792,128]{1,0:T(8,128)(2,1)S(1)} %get-tuple-element.19.refs_0_), channel_id=1, source_target_pairs={{0,2},{1,3},{2,4},{3,5},{4,6},{5,7},{6,0},{7,1},{8,10},{9,11},{10,... | collective-permute-start | bytes 1376264 | tf_op jit(solution)/shard_map/ppermute | solution.py:280
  4.2 11.3 %collective-permute-start.1 = (bf16[1792,128]{1,0:T(8,128)(2,1)S(1)}, bf16[1792,128]{1,0:T(8,128)(2,1)S(1)}, u32[]{:S(2)}, u32[]{:S(2)}) collective-permute-start(bf16[1792,128]{1,0:T(8,128)(2,1)S(1)} %get-tuple-element.19.refs_0_), channel_id=1, source_target_pairs={{0,6},{1,7},{2,0},{3,1},{4,2},{5,3},{6,4},{7,5},{8,14},{9,15},{10,... | collective-permute-start | bytes 1376264 | tf_op jit(solution)/shard_map/ppermute | solution.py:280
  4.2 13.4 %collective-permute-start = (bf16[1792,128]{1,0:T(8,128)(2,1)S(1)}, bf16[1792,128]{1,0:T(8,128)(2,1)S(1)}, u32[]{:S(2)}, u32[]{:S(2)}) collective-permute-start(bf16[1792,128]{1,0:T(8,128)(2,1)S(1)} %get-tuple-element.19.refs_0_), channel_id=1, source_target_pairs={{0,1},{1,0},{2,3},{3,2},{4,5},{5,4},{6,7},{7,6},{8,9},{9,8},{10,11... | collective-permute-start | bytes 1376264 | tf_op jit(solution)/shard_map/ppermute | solution.py:285
  14.2 3.3 %collective-permute-start.4 = (bf16[1792,128]{1,0:T(8,128)(2,1)S(1)}, bf16[1792,128]{1,0:T(8,128)(2,1)S(1)}, u32[]{:S(2)}, u32[]{:S(2)}) collective-permute-start(bf16[1792,128]{1,0:T(8,128)(2,1)S(1)} %collective-permute-done.3.refs_4_), channel_id=1, source_target_pairs={{0,1},{1,0},{2,3},{3,2},{4,5},{5,4},{6,7},{7,6},{8,9},{9,8},{10,11... | collective-permute-start | bytes 1376264 | tf_op jit(solution)/shard_map/ppermute | solution.py:285
  15.5 2.0 %collective-permute-start.2 = (bf16[1792,128]{1,0:T(8,128)(2,1)S(1)}, bf16[1792,128]{1,0:T(8,128)(2,1)}, u32[]{:S(2)}, u32[]{:S(2)}) collective-permute-start(bf16[1792,128]{1,0:T(8,128)(2,1)S(1)} %collective-permute-done.1.refs_2_), channel_id=1, source_target_pairs={{0,1},{1,0},{2,3},{3,2},{4,5},{5,4},{6,7},{7,6},{8,9},{9,8},{10,11... | collective-permute-start | bytes 1376264 | tf_op jit(solution)/shard_map/ppermute | solution.py:285
  15.5 12.9 %collective-permute-start.5 = (bf16[1792,128]{1,0:T(8,128)(2,1)S(1)}, bf16[1792,128]{1,0:T(8,128)(2,1)S(1)}, u32[]{:S(2)}, u32[]{:S(2)}) collective-permute-start(bf16[1792,128]{1,0:T(8,128)(2,1)S(1)} %collective-permute-done.3.refs_4_), channel_id=1, source_target_pairs={{0,2},{1,3},{2,4},{3,5},{4,6},{5,7},{6,0},{7,1},{8,10},{9,11},{10,... | collective-permute-start | bytes 1376264 | tf_op jit(solution)/shard_map/ppermute | solution.py:280
  16.2 13.6 %collective-permute-start.7 = (bf16[1792,128]{1,0:T(8,128)(2,1)S(1)}, bf16[1792,128]{1,0:T(8,128)(2,1)}, u32[]{:S(2)}, u32[]{:S(2)}) collective-permute-start(bf16[1792,128]{1,0:T(8,128)(2,1)S(1)} %get-tuple-element.13.refs_0_), channel_id=1, source_target_pairs={{0,6},{1,7},{2,0},{3,1},{4,2},{5,3},{6,4},{7,5},{8,14},{9,15},{10,... | collective-permute-start | bytes 1376264 | tf_op jit(solution)/shard_map/ppermute | solution.py:280
  17.6 12.7 %copy-start = (bf16[2,1792,448]{1,2,0:T(8,128)(2,1)S(1)}, bf16[2,1792,448]{1,2,0:T(8,128)(2,1)}, u32[]{:S(2)}) copy-start(bf16[2,1792,448]{1,2,0:T(8,128)(2,1)} %param.10) | copy-start | bytes 9633796
  28.4 1.8 collective-permute-start.6
  29.9 2.7 %collective-permute-start.8 = (bf16[1792,128]{1,0:T(8,128)(2,1)}, bf16[1792,128]{1,0:T(8,128)(2,1)S(1)}, u32[]{:S(2)}, u32[]{:S(2)}) collective-permute-start(bf16[1792,128]{1,0:T(8,128)(2,1)} %collective-permute-done.7.refs_2_), channel_id=1, source_target_pairs={{0,1},{1,0},{2,3},{3,2},{4,5},{5,4},{6,7},{7,6},{8,9},{9,8},{10,11... | collective-permute-start | bytes 1376264 | tf_op jit(solution)/shard_map/ppermute | solution.py:285
  32.6 45.4 %all-to-all-start = ((bf16[32,112,128]{2,1,0:T(8,128)(2,1)}), bf16[32,112,128]{2,1,0:T(8,128)(2,1)S(1)}, u32[]{:S(2)}, u32[]{:S(2)}) async-start(bf16[32,112,128]{2,1,0:T(8,128)(2,1)} %gradient_far.1), calls=%async_computation | async-start | bytes 1835008 | tf_op jit(solution)/shard_map/all_to_all | solution.py:309
  44.2 12.4 %collective-permute-start.10 = (bf16[1792,128]{1,0:T(8,128)(2,1)S(1)}, bf16[1792,128]{1,0:T(8,128)(2,1)S(1)}, u32[]{:S(2)}, u32[]{:S(2)}) collective-permute-start(bf16[1792,128]{1,0:T(8,128)(2,1)S(1)} %get-tuple-element.13.refs_0_), channel_id=1, source_target_pairs={{0,2},{1,3},{2,4},{3,5},{4,6},{5,7},{6,0},{7,1},{8,10},{9,11},{10,... | collective-permute-start | bytes 1376264 | tf_op jit(solution)/shard_map/ppermute | solution.py:280
  45.8 13.4 %collective-permute-start.12 = (bf16[1792,128]{1,0:T(8,128)(2,1)}, bf16[1792,128]{1,0:T(8,128)(2,1)S(1)}, u32[]{:S(2)}, u32[]{:S(2)}) collective-permute-start(bf16[1792,128]{1,0:T(8,128)(2,1)} %collective-permute-done.7.refs_2_), channel_id=1, source_target_pairs={{0,6},{1,7},{2,0},{3,1},{4,2},{5,3},{6,4},{7,5},{8,14},{9,15},{10,... | collective-permute-start | bytes 1376264 | tf_op jit(solution)/shard_map/ppermute | solution.py:280
  56.5 4.0 %collective-permute-start.11 = (bf16[1792,128]{1,0:T(8,128)(2,1)S(1)}, bf16[1792,128]{1,0:T(8,128)(2,1)S(1)}, u32[]{:S(2)}, u32[]{:S(2)}) collective-permute-start(bf16[1792,128]{1,0:T(8,128)(2,1)S(1)} %collective-permute-done.10.refs_4_), channel_id=1, source_target_pairs={{0,1},{1,0},{2,3},{3,2},{4,5},{5,4},{6,7},{7,6},{8,9},{9,8},{10,11... | collective-permute-start | bytes 1376264 | tf_op jit(solution)/shard_map/ppermute | solution.py:285
  56.5 7.3 %collective-permute-start.9 = (bf16[1792,128]{1,0:T(8,128)(2,1)S(1)}, bf16[1792,128]{1,0:T(8,128)(2,1)S(1)}, u32[]{:S(2)}, u32[]{:S(2)}) collective-permute-start(bf16[1792,128]{1,0:T(8,128)(2,1)S(1)} %get-tuple-element.13.refs_0_), channel_id=1, source_target_pairs={{0,1},{1,0},{2,3},{3,2},{4,5},{5,4},{6,7},{7,6},{8,9},{9,8},{10,11... | collective-permute-start | bytes 1376264 | tf_op jit(solution)/shard_map/ppermute | solution.py:285
  59.2 4.6 %collective-permute-start.13 = (bf16[1792,128]{1,0:T(8,128)(2,1)S(1)}, bf16[1792,128]{1,0:T(8,128)(2,1)S(1)}, u32[]{:S(2)}, u32[]{:S(2)}) collective-permute-start(bf16[1792,128]{1,0:T(8,128)(2,1)S(1)} %collective-permute-done.12.refs_6_), channel_id=1, source_target_pairs={{0,1},{2,3},{4,5},{6,7},{8,9},{10,11},{12,13},{14,15},{16,17},{18,... | collective-permute-start | bytes 1376264 | tf_op jit(solution)/shard_map/ppermute | solution.py:304
  60.5 10.4 %collective-permute-start.14 = (bf16[1792,128]{1,0:T(8,128)(2,1)S(1)}, bf16[1792,128]{1,0:T(8,128)(2,1)S(1)}, u32[]{:S(2)}, u32[]{:S(2)}) collective-permute-start(bf16[1792,128]{1,0:T(8,128)(2,1)S(1)} %collective-permute-done.11.refs_5_), channel_id=1, source_target_pairs={{0,2},{2,4},{4,6},{6,0},{8,10},{10,12},{12,14},{14,8},{16,18},{18,... | collective-permute-start | bytes 1376264 | tf_op jit(solution)/shard_map/ppermute | solution.py:280
  77.9 9.6 %copy-start.8 = (s32[32,8]{0,1:T(8,128)S(1)}, s32[32,8]{0,1:T(8,128)}, u32[]{:S(2)}) copy-start(s32[32,8]{0,1:T(8,128)} %param.12) | copy-start | bytes 3076
  77.9 27.0 %copy-start.7 = (s32[32]{0:T(128)S(1)}, s32[32]{0:T(128)}, u32[]{:S(2)}) copy-start(s32[32]{0:T(128)} %owners_ref.3) | copy-start | bytes 388
  77.9 27.0 %all-to-all-start.1 = ((bf16[32,112,128]{2,1,0:T(8,128)(2,1)}), bf16[32,112,128]{2,1,0:T(8,128)(2,1)S(1)}, u32[]{:S(2)}, u32[]{:S(2)}) async-start(bf16[32,112,128]{2,1,0:T(8,128)(2,1)} %gradient_near.3), calls=%async_computation.1 | async-start | bytes 1835008 | tf_op jit(solution)/shard_map/all_to_all | solution.py:309
  87.6 42.9 %copy-start.3 = (bf16[1,448,1024]{2,1,0:T(8,128)(2,1)S(1)}, bf16[1,448,1024]{2,1,0:T(8,128)(2,1)}, u32[]{:S(2)}) copy-start(bf16[1,448,1024]{2,1,0:T(8,128)(2,1)} %first_ref.3) | copy-start | bytes 2752516
  104.9 25.6 %copy-start.1 = (f32[1,448,1024]{2,1,0:T(8,128)S(1)}, f32[1,448,1024]{2,1,0:T(8,128)}, u32[]{:S(2)}) copy-start(f32[1,448,1024]{2,1,0:T(8,128)} %master_ref.3) | copy-start | bytes 5505028
  104.9 25.6 %copy-start.4 = (bf16[1,448,1024]{2,1,0:T(8,128)(2,1)S(1)}, bf16[1,448,1024]{2,1,0:T(8,128)(2,1)}, u32[]{:S(2)}) copy-start(bf16[1,448,1024]{2,1,0:T(8,128)(2,1)} %second_ref.3) | copy-start | bytes 2752516
  132.9 5.0 %copy-start.9 = (s32[32,8]{0,1:T(8,128)S(1)}, s32[32,8]{0,1:T(8,128)}, u32[]{:S(2)}) copy-start(s32[32,8]{0,1:T(8,128)} %param.13) | copy-start | bytes 3076
  132.9 22.2 %all-to-all-start.3 = ((bf16[32,112,128]{2,1,0:T(8,128)(2,1)}), bf16[32,112,128]{2,1,0:T(8,128)(2,1)}, u32[]{:S(2)}, u32[]{:S(2)}) async-start(bf16[32,112,128]{2,1,0:T(8,128)(2,1)} %new_weights.1), calls=%async_computation.3 | async-start | bytes 1835008 | tf_op jit(solution)/shard_map/all_to_all | solution.py:309
  158.6 5.1 %copy-start.5 = (bf16[1,448,1024]{2,1,0:T(8,128)(2,1)S(1)}, bf16[1,448,1024]{2,1,0:T(8,128)(2,1)}, u32[]{:S(2)}) copy-start(bf16[1,448,1024]{2,1,0:T(8,128)(2,1)} %second_ref.3) | copy-start | bytes 2752516
  158.6 38.6 %all-to-all-start.4 = ((bf16[32,2,112,128]{3,2,1,0:T(8,128)(2,1)}), bf16[32,2,112,128]{3,2,1,0:T(8,128)(2,1)}, u32[]{:S(2)}, u32[]{:S(2)}) async-start(bf16[32,2,112,128]{3,2,1,0:T(8,128)(2,1)} %spread_copies.1), calls=%async_computation.4 | async-start | bytes 3670016 | tf_op jit(solution)/shard_map/all_to_all | solution.py:309
  163.8 1.5 copy-start.2

commit v5 on v4

--- a/solution.py
+++ b/solution.py
@@ -60,10 +60,12 @@
         cut = grad_v[pl.ds(r * PIECE, PIECE), :]
         grad_v[pl.ds(r * PIECE, PIECE), :] = jnp.where(live, cut, jnp.zeros_like(cut))
     x_here = place_ref[0] // 2
-    for i, (step, _) in enumerate(columns):
-        for j, load in loads:
-            if i == j:
-                load.wait()
+    for _, load in loads:
+        load.wait()
+
+    @pl.loop(0, len(columns))
+    def _(i):
+        step = sum(jnp.where(i == k, there, 0) for k, (there, _) in enumerate(columns))
         product = jnp.dot(grad_v[...], hidden_v[i], preferred_element_type=jnp.float32)
         product = product.astype(out_ref.dtype)
         x_there = lax.rem(x_here + step, COL_CUTS // 2)
@@ -156,12 +158,12 @@
 
     @pl.loop(0, replicas_ref.shape[0])
     def _(e):
-        def add(j, total):
+        def take(j):
             g = replicas_ref[e, j]
-            return total + held[lax.rem(g, 2), g // 2].astype(jnp.float32)
+            return held[lax.rem(g, 2), g // 2].astype(jnp.float32)
 
         total = lax.fori_loop(
-            0, list_length(replicas_ref, e), add, jnp.zeros((PIECE, LANES), jnp.float32)
+            1, list_length(replicas_ref, e), lambda j, total: total + take(j), take(0)
         )
         out_ref[owners_ref[e]] = total.astype(out_ref.dtype)
 
@@ -256,23 +258,45 @@
     )(next_replicas, owner_map, weights)
 
 
-def order_kernel(pieces_ref, out_ref):
-    for s in range(2):
-        for c in range(COL_CUTS):
-            out_ref[s, :, pl.ds(c * LANES, LANES)] = pieces_ref[c, s]
+def order_kernel(pieces_ref, out_ref, ordered, load_sems, store_sems):
+    loads = [
+        [
+            pltpu.make_async_copy(
+                pieces_ref.at[r, c], ordered.at[:, r, :, pl.ds(c * LANES, LANES)], load_sems.at[r, c]
+            )
+            for c in range(COL_CUTS)
+        ]
+        for r in range(ROW_CUTS)
+    ]
+    for row in loads:
+        for load in row:
+            load.start()
+    stores = []
+    for r, row in enumerate(loads):
+        for load in row:
+            load.wait()
+        store = pltpu.make_async_copy(ordered.at[:, r], out_ref.at[:, r], store_sems.at[r])
+        store.start()
+        stores.append(store)
+    for store in stores:
+        store.wait()
 
 
 def order_pieces(pieces):
-    width = ROW_CUTS * PIECE
+    shape = (2, ROW_CUTS, PIECE, COL_CUTS * LANES)
     return pl.pallas_call(
         order_kernel,
-        grid=(ROW_CUTS,),
-        out_shape=jax.ShapeDtypeStruct((2, width, COL_CUTS * LANES), jnp.bfloat16),
-        in_specs=[pl.BlockSpec((COL_CUTS, 2, PIECE, LANES), lambda r: (r, 0, 0, 0))],
-        out_specs=pl.BlockSpec((2, PIECE, COL_CUTS * LANES), lambda r: (0, r, 0)),
+        out_shape=jax.ShapeDtypeStruct(shape, jnp.bfloat16),
+        in_specs=[any_spec()],
+        out_specs=any_spec(),
+        scratch_shapes=[
+            pltpu.VMEM(shape, jnp.bfloat16),
+            pltpu.SemaphoreType.DMA((ROW_CUTS, COL_CUTS)),
+            pltpu.SemaphoreType.DMA((ROW_CUTS,)),
+        ],
         compiler_params=pltpu.CompilerParams(vmem_limit_bytes=VMEM_LOW),
         name="order_pieces",
-    )(pieces)
+    )(pieces.reshape(ROW_CUTS, COL_CUTS, 2, PIECE, LANES)).reshape(2, ROW_CUTS * PIECE, COL_CUTS * LANES)
 
 
 def x_shift(array, step, cores=(0, 1)):

time: 202 us -> 199 us (0.985)
  Pallas kernels: 31.2 us -> 27.1 us
    pallas_call x2, Pallas kernels: 12.9 us -> 10.6 us  [slot_gradient(): pl.pallas_call(functools.partial(grad_kernel, slot, plan), out_shape=jax....]
  transfers between devices with their start and end apart: 19 -> 19, of which waited for: 11 -> 11; matrix products, arithmetic and copies ran while one was open for 0% -> 0% of each run, Pallas kernels for 9% -> 8%
where the time goes in v5:
time: 199 us; the launch traced here: 198 us
  waiting for transfers between devices  102 us (51%)
  starting transfers between devices  42.6 us (21%)
  Pallas kernels  27.1 us (14%)
  blocking collectives  22.1 us (11%)
  local copies, waits for them, and re-layouts  3.52 us (2%)
    all_to_all x4, waiting for transfers between devices, exchange(): return lax.all_to_all(pieces, 'ep', split_axis=0, concat_axis=0, tiled=True)  63 us
    ppermute x7, waiting for transfers between devices, x_shift(): return lax.ppermute(array, 'dp', pairs)  38.1 us
    all_to_all x4, starting transfers between devices, exchange(): return lax.all_to_all(pieces, 'ep', split_axis=0, concat_axis=0, tiled=True)  31.2 us
    all_to_all x1, blocking collectives, exchange(): return lax.all_to_all(pieces, 'ep', split_axis=0, concat_axis=0, tiled=True)  22.1 us
    pallas_call x2, Pallas kernels, slot_gradient(): pl.pallas_call(functools.partial(grad_kernel, slot, plan), out_shape=jax....  10.6 us
    ppermute x7, starting transfers between devices, x_shift(): return lax.ppermute(array, 'dp', pairs)  9.53 us
    pallas_call x2, Pallas kernels, adam_update(): pl.pallas_call(kernel, grid=(ROW_CUTS,), out_shape=shapes, in_specs=[piec...  5.28 us
  transfers between devices with their start and end apart: 19, of which 11 were waited for; matrix products, arithmetic and copies ran while one was open for 0% of the time, Pallas kernels for 8%

profile of v5, /device:TPU:6, one launch (start us, length us, event | category | flops | bytes accessed | tf_op | source)
XLA Modules:
  0.0 197.9 jit_solution(3595387395693698402)
XLA Ops:
  0.6 1.2 slice_bitcast_fusion
  1.9 2.3 %collective-permute-start.3 = (bf16[1792,128]{1,0:T(8,128)(2,1)S(1)}, bf16[1792,128]{1,0:T(8,128)(2,1)S(1)}, u32[]{:S(2)}, u32[]{:S(2)}) collective-permute-start(bf16[1792,128]{1,0:T(8,128)(2,1)S(1)} %get-tuple-element.19.refs_0_), channel_id=1, source_target_pairs={{0,2},{1,3},{2,4},{3,5},{4,6},{5,7},{6,0},{7,1},{8,10},{9,11},{10,... | collective-permute-start | bytes 1376264 | tf_op jit(solution)/shard_map/ppermute | solution.py:304
  4.2 10.0 %collective-permute-done.3.refs_4_ = bf16[1792,128]{1,0:T(8,128)(2,1)S(1)} collective-permute-done((bf16[1792,128]{1,0:T(8,128)(2,1)S(1)}, bf16[1792,128]{1,0:T(8,128)(2,1)S(1)}, u32[]{:S(2)}, u32[]{:S(2)}) %collective-permute-start.3) | collective-permute-done | bytes 458784 | tf_op jit(solution)/shard_map/ppermute | solution.py:304
  14.2 1.3 collective-permute-done.1.refs_2_
  15.5 0.7 collective-permute-start.5
  16.2 1.3 collective-permute-start.7
  17.6 5.1 %gradient_near.2.refs_2_ = bf16[32,112,128]{2,1,0:T(8,128)(2,1)} custom-call(s32[1]{0:T(128)} %bitcast.place_ref, s32[2]{0:T(128)S(1)} %copy-done.6, bf16[2,448,1792]{2,1,0:T(8,128)(2,1)} %bitcast.8, bf16[1792,128]{1,0:T(8,128)(2,1)S(1)} %get-tuple-element.19.refs_0_, bf16[1792,128]{1,0:T(8,128)(2,1)S(1)} %collective-permute-done.refs_1_, ...), custom_call_target="tpu_custom_call" | custom-call | flops 1233125376 | bytes 6000000 | tf_op jit(solution)/shard_map/gradient_near/pallas_call | solution.py:117
  22.7 5.7 %collective-permute-done.5.refs_0_ = bf16[1792,128]{1,0:T(8,128)(2,1)S(1)} collective-permute-done((bf16[1792,128]{1,0:T(8,128)(2,1)S(1)}, bf16[1792,128]{1,0:T(8,128)(2,1)S(1)}, u32[]{:S(2)}, u32[]{:S(2)}) %collective-permute-start.5) | collective-permute-done | bytes 458784 | tf_op jit(solution)/shard_map/ppermute | solution.py:304
  28.4 1.4 collective-permute-done.7.refs_2_
  30.3 2.3 %gradient_far.1 = bf16[32,112,128]{2,1,0:T(8,128)(2,1)} custom-call(s32[1]{0:T(128)} %bitcast.place_ref, s32[2]{0:T(128)S(1)} %copy-done.6, bf16[2,448,1792]{2,1,0:T(8,128)(2,1)S(1)} %bitcast.10, bf16[1792,128]{1,0:T(8,128)(2,1)S(1)} %collective-permute-done.5.refs_0_, ...), custom_call_target="tpu_custom_call", output_to_operand_aliasing={{}: (5, {})} | custom-call | flops 411041792 | bytes 2000000 | tf_op jit(solution)/shard_map/gradient_far/pallas_call | solution.py:127
  32.6 11.6 %all-to-all-start = ((bf16[32,112,128]{2,1,0:T(8,128)(2,1)}), bf16[32,112,128]{2,1,0:T(8,128)(2,1)S(1)}, u32[]{:S(2)}, u32[]{:S(2)}) async-start(bf16[32,112,128]{2,1,0:T(8,128)(2,1)} %gradient_far.1), calls=%async_computation | async-start | bytes 1835008 | tf_op jit(solution)/shard_map/all_to_all | solution.py:333
  44.2 1.6 collective-permute-start.10
  46.3 10.3 %collective-permute-done.10.refs_4_ = bf16[1792,128]{1,0:T(8,128)(2,1)S(1)} collective-permute-done((bf16[1792,128]{1,0:T(8,128)(2,1)S(1)}, bf16[1792,128]{1,0:T(8,128)(2,1)S(1)}, u32[]{:S(2)}, u32[]{:S(2)}) %collective-permute-start.10) | collective-permute-done | bytes 458784 | tf_op jit(solution)/shard_map/ppermute | solution.py:304
  57.1 2.1 %collective-permute-done.12.refs_6_ = bf16[1792,128]{1,0:T(8,128)(2,1)S(1)} collective-permute-done((bf16[1792,128]{1,0:T(8,128)(2,1)}, bf16[1792,128]{1,0:T(8,128)(2,1)S(1)}, u32[]{:S(2)}, u32[]{:S(2)}) %collective-permute-start.12) | collective-permute-done | bytes 458784 | tf_op jit(solution)/shard_map/ppermute | solution.py:304
  59.2 1.3 collective-permute-start.13
  60.5 3.1 %collective-permute-start.14 = (bf16[1792,128]{1,0:T(8,128)(2,1)S(1)}, bf16[1792,128]{1,0:T(8,128)(2,1)S(1)}, u32[]{:S(2)}, u32[]{:S(2)}) collective-permute-start(bf16[1792,128]{1,0:T(8,128)(2,1)S(1)} %collective-permute-done.11.refs_5_), channel_id=1, source_target_pairs={{0,2},{2,4},{4,6},{6,0},{8,10},{10,12},{12,14},{14,8},{16,18},{18,... | collective-permute-start | bytes 1376264 | tf_op jit(solution)/shard_map/ppermute | solution.py:304
  63.6 7.2 %collective-permute-done.14.refs_8_ = bf16[1792,128]{1,0:T(8,128)(2,1)S(1)} collective-permute-done((bf16[1792,128]{1,0:T(8,128)(2,1)S(1)}, bf16[1792,128]{1,0:T(8,128)(2,1)S(1)}, u32[]{:S(2)}, u32[]{:S(2)}) %collective-permute-start.14) | collective-permute-done | bytes 458784 | tf_op jit(solution)/shard_map/ppermute | solution.py:304
  70.9 5.5 %gradient_near.3 = bf16[32,112,128]{2,1,0:T(8,128)(2,1)} custom-call(s32[1]{0:T(128)} %bitcast.place_ref, s32[2]{0:T(128)S(1)} %copy-done.6, bf16[2,448,1792]{2,1,0:T(8,128)(2,1)} %bitcast.9, bf16[1792,128]{1,0:T(8,128)(2,1)S(1)} %get-tuple-element.13.refs_0_, bf16[1792,128]{1,0:T(8,128)(2,1)S(1)} %collective-permute-done.9.refs_1_, ...), custom_call_target="tpu_custom_call" | custom-call | flops 1644167168 | bytes 160000000 | tf_op jit(solution)/shard_map/gradient_near/pallas_call | solution.py:117
  76.4 9.5 %all-to-all-start.1 = ((bf16[32,112,128]{2,1,0:T(8,128)(2,1)}), bf16[32,112,128]{2,1,0:T(8,128)(2,1)S(1)}, u32[]{:S(2)}, u32[]{:S(2)}) async-start(bf16[32,112,128]{2,1,0:T(8,128)(2,1)} %gradient_near.3), calls=%async_computation.1 | async-start | bytes 1835008 | tf_op jit(solution)/shard_map/all_to_all | solution.py:333
  86.0 17.3 %all-to-all-done.1.second_ref = bf16[32,112,128]{2,1,0:T(8,128)(2,1)S(1)} async-done(((bf16[32,112,128]{2,1,0:T(8,128)(2,1)}), bf16[32,112,128]{2,1,0:T(8,128)(2,1)S(1)}, u32[]{:S(2)}, u32[]{:S(2)}) %all-to-all-start.1) | async-done | bytes 917536 | tf_op jit(solution)/shard_map/all_to_all | solution.py:333
  103.3 3.0 %sum_copies.1 = bf16[32,112,128]{2,1,0:T(8,128)(2,1)S(1)} custom-call(s32[32,8]{1,0:T(8,128)S(1)} %copy.14.replicas_ref, s32[32]{0:T(128)S(1)} %copy-done.7, bf16[32,112,128]{2,1,0:T(8,128)(2,1)S(1)} %all-to-all-done.first_ref, bf16[32,112,128]{2,1,0:T(8,128)(2,1)S(1)} %all-to-all-done.1.second_ref), custom_call_target="tpu_custom_call" | custom-call | tf_op jit(solution)/shard_map/sum_copies/pallas_call | solution.py:173
  106.3 22.1 %all_to_all.25.grad_ref = bf16[32,112,128]{2,1,0:T(8,128)(2,1)S(1)} all-to-all(bf16[32,112,128]{2,1,0:T(8,128)(2,1)S(1)} %sum_copies.1), channel_id=1, replica_groups=mesh['ep'=32,'dp'=8] {'ep'}, dimensions={0} | all-to-all | bytes 1835008 | tf_op jit(solution)/shard_map/all_to_all | solution.py:333
  128.4 2.4 %new_weights.1 = bf16[32,112,128]{2,1,0:T(8,128)(2,1)} custom-call(bf16[32,112,128]{2,1,0:T(8,128)(2,1)S(1)} %all_to_all.25.grad_ref, f32[1,448,1024]{2,1,0:T(8,128)S(1)} %copy-done.1, bf16[1,448,1024]{2,1,0:T(8,128)(2,1)S(1)} %copy-done.3, bf16[1,448,1024]{2,1,0:T(8,128)(2,1)S(1)} %copy-done.4), custom_call_target="tpu_custom_call" | custom-call | flops 8000000 | bytes 9000000 | tf_op jit(solution)/shard_map/new_weights/pallas_call | solution.py:221
  130.9 5.0 %all-to-all-start.3 = ((bf16[32,112,128]{2,1,0:T(8,128)(2,1)}), bf16[32,112,128]{2,1,0:T(8,128)(2,1)}, u32[]{:S(2)}, u32[]{:S(2)}) async-start(bf16[32,112,128]{2,1,0:T(8,128)(2,1)} %new_weights.1), calls=%async_computation.3 | async-start | bytes 1835008 | tf_op jit(solution)/shard_map/all_to_all | solution.py:333
  135.9 0.7 copy.15.lists_ref
  136.6 16.5 %all-to-all-done.3.weights_ref = bf16[32,112,128]{2,1,0:T(8,128)(2,1)} async-done(((bf16[32,112,128]{2,1,0:T(8,128)(2,1)}), bf16[32,112,128]{2,1,0:T(8,128)(2,1)}, u32[]{:S(2)}, u32[]{:S(2)}) %all-to-all-start.3) | async-done | bytes 917536 | tf_op jit(solution)/shard_map/all_to_all | solution.py:333
  153.1 3.5 %spread_copies.1 = bf16[32,2,112,128]{3,2,1,0:T(8,128)(2,1)} custom-call(s32[32,8]{1,0:T(8,128)} %copy.15.lists_ref, s32[32]{0:T(128)} %owners_ref.3, bf16[32,112,128]{2,1,0:T(8,128)(2,1)} %all-to-all-done.3.weights_ref), custom_call_target="tpu_custom_call" | custom-call | tf_op jit(solution)/shard_map/spread_copies/pallas_call | solution.py:250
  156.6 5.1 %all-to-all-start.4 = ((bf16[32,2,112,128]{3,2,1,0:T(8,128)(2,1)}), bf16[32,2,112,128]{3,2,1,0:T(8,128)(2,1)}, u32[]{:S(2)}, u32[]{:S(2)}) async-start(bf16[32,2,112,128]{3,2,1,0:T(8,128)(2,1)} %spread_copies.1), calls=%async_computation.4 | async-start | bytes 3670016 | tf_op jit(solution)/shard_map/all_to_all | solution.py:333
  161.8 1.5 copy-done.2
  163.2 2.8 %new_state.1 = (f32[1,448,1024]{2,1,0:T(8,128)}, bf16[1,448,1024]{2,1,0:T(8,128)(2,1)}, bf16[1,448,1024]{2,1,0:T(8,128)(2,1)}) custom-call(bf16[32,112,128]{2,1,0:T(8,128)(2,1)S(1)} %all_to_all.25.grad_ref, f32[1,448,1024]{2,1,0:T(8,128)S(1)} %copy-done.2, bf16[1,448,1024]{2,1,0:T(8,128)(2,1)S(1)} %copy-done.3, bf16[1,448,1024]{2,1,0:T(8,128)(2,1)S(1)} %copy-done.5), custom_call_target="tpu_custom_call" | custom-call | flops 8000000 | bytes 9000000 | tf_op jit(solution)/shard_map/new_state/pallas_call | solution.py:221
  166.1 29.1 %all-to-all-done.4 = bf16[32,2,112,128]{3,2,1,0:T(8,128)(2,1)} async-done(((bf16[32,2,112,128]{3,2,1,0:T(8,128)(2,1)}), bf16[32,2,112,128]{3,2,1,0:T(8,128)(2,1)}, u32[]{:S(2)}, u32[]{:S(2)}) %all-to-all-start.4) | async-done | bytes 1835040 | tf_op jit(solution)/shard_map/all_to_all | solution.py:333
  195.2 2.6 %order_pieces.1 = bf16[2,4,112,1024]{3,2,1,0:T(8,128)(2,1)} custom-call(bf16[4,8,2,112,128]{4,3,2,1,0:T(8,128)(2,1)} %bitcast.4.pieces_ref), custom_call_target="tpu_custom_call" | custom-call | tf_op jit(solution)/shard_map/order_pieces/pallas_call | solution.py:287
  (38 shorter events, 1.6 us)
Async XLA Ops:
  0.6 16.9 %copy-start.6 = (s32[2]{0:T(128)S(1)}, s32[2]{0:T(128)}, u32[]{:S(2)}) copy-start(s32[2]{0:T(128)} %counts_ref.5) | copy-start | bytes 28
  1.9 12.3 %collective-permute-start.3 = (bf16[1792,128]{1,0:T(8,128)(2,1)S(1)}, bf16[1792,128]{1,0:T(8,128)(2,1)S(1)}, u32[]{:S(2)}, u32[]{:S(2)}) collective-permute-start(bf16[1792,128]{1,0:T(8,128)(2,1)S(1)} %get-tuple-element.19.refs_0_), channel_id=1, source_target_pairs={{0,2},{1,3},{2,4},{3,5},{4,6},{5,7},{6,0},{7,1},{8,10},{9,11},{10,... | collective-permute-start | bytes 1376264 | tf_op jit(solution)/shard_map/ppermute | solution.py:304
  4.2 11.3 %collective-permute-start.1 = (bf16[1792,128]{1,0:T(8,128)(2,1)S(1)}, bf16[1792,128]{1,0:T(8,128)(2,1)S(1)}, u32[]{:S(2)}, u32[]{:S(2)}) collective-permute-start(bf16[1792,128]{1,0:T(8,128)(2,1)S(1)} %get-tuple-element.19.refs_0_), channel_id=1, source_target_pairs={{0,6},{1,7},{2,0},{3,1},{4,2},{5,3},{6,4},{7,5},{8,14},{9,15},{10,... | collective-permute-start | bytes 1376264 | tf_op jit(solution)/shard_map/ppermute | solution.py:304
  4.2 13.4 %collective-permute-start = (bf16[1792,128]{1,0:T(8,128)(2,1)S(1)}, bf16[1792,128]{1,0:T(8,128)(2,1)S(1)}, u32[]{:S(2)}, u32[]{:S(2)}) collective-permute-start(bf16[1792,128]{1,0:T(8,128)(2,1)S(1)} %get-tuple-element.19.refs_0_), channel_id=1, source_target_pairs={{0,1},{1,0},{2,3},{3,2},{4,5},{5,4},{6,7},{7,6},{8,9},{9,8},{10,11... | collective-permute-start | bytes 1376264 | tf_op jit(solution)/shard_map/ppermute | solution.py:309
  14.2 3.3 %collective-permute-start.4 = (bf16[1792,128]{1,0:T(8,128)(2,1)S(1)}, bf16[1792,128]{1,0:T(8,128)(2,1)S(1)}, u32[]{:S(2)}, u32[]{:S(2)}) collective-permute-start(bf16[1792,128]{1,0:T(8,128)(2,1)S(1)} %collective-permute-done.3.refs_4_), channel_id=1, source_target_pairs={{0,1},{1,0},{2,3},{3,2},{4,5},{5,4},{6,7},{7,6},{8,9},{9,8},{10,11... | collective-permute-start | bytes 1376264 | tf_op jit(solution)/shard_map/ppermute | solution.py:309
  15.5 2.0 %collective-permute-start.2 = (bf16[1792,128]{1,0:T(8,128)(2,1)S(1)}, bf16[1792,128]{1,0:T(8,128)(2,1)}, u32[]{:S(2)}, u32[]{:S(2)}) collective-permute-start(bf16[1792,128]{1,0:T(8,128)(2,1)S(1)} %collective-permute-done.1.refs_2_), channel_id=1, source_target_pairs={{0,1},{1,0},{2,3},{3,2},{4,5},{5,4},{6,7},{7,6},{8,9},{9,8},{10,11... | collective-permute-start | bytes 1376264 | tf_op jit(solution)/shard_map/ppermute | solution.py:309
  15.5 12.9 %collective-permute-start.5 = (bf16[1792,128]{1,0:T(8,128)(2,1)S(1)}, bf16[1792,128]{1,0:T(8,128)(2,1)S(1)}, u32[]{:S(2)}, u32[]{:S(2)}) collective-permute-start(bf16[1792,128]{1,0:T(8,128)(2,1)S(1)} %collective-permute-done.3.refs_4_), channel_id=1, source_target_pairs={{0,2},{1,3},{2,4},{3,5},{4,6},{5,7},{6,0},{7,1},{8,10},{9,11},{10,... | collective-permute-start | bytes 1376264 | tf_op jit(solution)/shard_map/ppermute | solution.py:304
  16.2 13.6 %collective-permute-start.7 = (bf16[1792,128]{1,0:T(8,128)(2,1)S(1)}, bf16[1792,128]{1,0:T(8,128)(2,1)}, u32[]{:S(2)}, u32[]{:S(2)}) collective-permute-start(bf16[1792,128]{1,0:T(8,128)(2,1)S(1)} %get-tuple-element.13.refs_0_), channel_id=1, source_target_pairs={{0,6},{1,7},{2,0},{3,1},{4,2},{5,3},{6,4},{7,5},{8,14},{9,15},{10,... | collective-permute-start | bytes 1376264 | tf_op jit(solution)/shard_map/ppermute | solution.py:304
  17.6 12.7 %copy-start = (bf16[2,1792,448]{1,2,0:T(8,128)(2,1)S(1)}, bf16[2,1792,448]{1,2,0:T(8,128)(2,1)}, u32[]{:S(2)}) copy-start(bf16[2,1792,448]{1,2,0:T(8,128)(2,1)} %param.10) | copy-start | bytes 9633796
  28.4 1.8 collective-permute-start.6
  29.9 2.7 %collective-permute-start.8 = (bf16[1792,128]{1,0:T(8,128)(2,1)}, bf16[1792,128]{1,0:T(8,128)(2,1)S(1)}, u32[]{:S(2)}, u32[]{:S(2)}) collective-permute-start(bf16[1792,128]{1,0:T(8,128)(2,1)} %collective-permute-done.7.refs_2_), channel_id=1, source_target_pairs={{0,1},{1,0},{2,3},{3,2},{4,5},{5,4},{6,7},{7,6},{8,9},{9,8},{10,11... | collective-permute-start | bytes 1376264 | tf_op jit(solution)/shard_map/ppermute | solution.py:309
  32.6 43.8 %all-to-all-start = ((bf16[32,112,128]{2,1,0:T(8,128)(2,1)}), bf16[32,112,128]{2,1,0:T(8,128)(2,1)S(1)}, u32[]{:S(2)}, u32[]{:S(2)}) async-start(bf16[32,112,128]{2,1,0:T(8,128)(2,1)} %gradient_far.1), calls=%async_computation | async-start | bytes 1835008 | tf_op jit(solution)/shard_map/all_to_all | solution.py:333
  44.2 12.4 %collective-permute-start.10 = (bf16[1792,128]{1,0:T(8,128)(2,1)S(1)}, bf16[1792,128]{1,0:T(8,128)(2,1)S(1)}, u32[]{:S(2)}, u32[]{:S(2)}) collective-permute-start(bf16[1792,128]{1,0:T(8,128)(2,1)S(1)} %get-tuple-element.13.refs_0_), channel_id=1, source_target_pairs={{0,2},{1,3},{2,4},{3,5},{4,6},{5,7},{6,0},{7,1},{8,10},{9,11},{10,... | collective-permute-start | bytes 1376264 | tf_op jit(solution)/shard_map/ppermute | solution.py:304
  45.8 13.4 %collective-permute-start.12 = (bf16[1792,128]{1,0:T(8,128)(2,1)}, bf16[1792,128]{1,0:T(8,128)(2,1)S(1)}, u32[]{:S(2)}, u32[]{:S(2)}) collective-permute-start(bf16[1792,128]{1,0:T(8,128)(2,1)} %collective-permute-done.7.refs_2_), channel_id=1, source_target_pairs={{0,6},{1,7},{2,0},{3,1},{4,2},{5,3},{6,4},{7,5},{8,14},{9,15},{10,... | collective-permute-start | bytes 1376264 | tf_op jit(solution)/shard_map/ppermute | solution.py:304
  56.5 4.0 %collective-permute-start.11 = (bf16[1792,128]{1,0:T(8,128)(2,1)S(1)}, bf16[1792,128]{1,0:T(8,128)(2,1)S(1)}, u32[]{:S(2)}, u32[]{:S(2)}) collective-permute-start(bf16[1792,128]{1,0:T(8,128)(2,1)S(1)} %collective-permute-done.10.refs_4_), channel_id=1, source_target_pairs={{0,1},{1,0},{2,3},{3,2},{4,5},{5,4},{6,7},{7,6},{8,9},{9,8},{10,11... | collective-permute-start | bytes 1376264 | tf_op jit(solution)/shard_map/ppermute | solution.py:309
  56.5 7.1 %collective-permute-start.9 = (bf16[1792,128]{1,0:T(8,128)(2,1)S(1)}, bf16[1792,128]{1,0:T(8,128)(2,1)S(1)}, u32[]{:S(2)}, u32[]{:S(2)}) collective-permute-start(bf16[1792,128]{1,0:T(8,128)(2,1)S(1)} %get-tuple-element.13.refs_0_), channel_id=1, source_target_pairs={{0,1},{1,0},{2,3},{3,2},{4,5},{5,4},{6,7},{7,6},{8,9},{9,8},{10,11... | collective-permute-start | bytes 1376264 | tf_op jit(solution)/shard_map/ppermute | solution.py:309
  59.2 4.5 %collective-permute-start.13 = (bf16[1792,128]{1,0:T(8,128)(2,1)S(1)}, bf16[1792,128]{1,0:T(8,128)(2,1)S(1)}, u32[]{:S(2)}, u32[]{:S(2)}) collective-permute-start(bf16[1792,128]{1,0:T(8,128)(2,1)S(1)} %collective-permute-done.12.refs_6_), channel_id=1, source_target_pairs={{0,1},{2,3},{4,5},{6,7},{8,9},{10,11},{12,13},{14,15},{16,17},{18,... | collective-permute-start | bytes 1376264 | tf_op jit(solution)/shard_map/ppermute | solution.py:328
  60.5 10.4 %collective-permute-start.14 = (bf16[1792,128]{1,0:T(8,128)(2,1)S(1)}, bf16[1792,128]{1,0:T(8,128)(2,1)S(1)}, u32[]{:S(2)}, u32[]{:S(2)}) collective-permute-start(bf16[1792,128]{1,0:T(8,128)(2,1)S(1)} %collective-permute-done.11.refs_5_), channel_id=1, source_target_pairs={{0,2},{2,4},{4,6},{6,0},{8,10},{10,12},{12,14},{14,8},{16,18},{18,... | collective-permute-start | bytes 1376264 | tf_op jit(solution)/shard_map/ppermute | solution.py:304
  76.4 9.6 %copy-start.8 = (s32[32,8]{0,1:T(8,128)S(1)}, s32[32,8]{0,1:T(8,128)}, u32[]{:S(2)}) copy-start(s32[32,8]{0,1:T(8,128)} %param.12) | copy-start | bytes 3076
  76.4 27.0 %copy-start.7 = (s32[32]{0:T(128)S(1)}, s32[32]{0:T(128)}, u32[]{:S(2)}) copy-start(s32[32]{0:T(128)} %owners_ref.3) | copy-start | bytes 388
  76.4 26.9 %all-to-all-start.1 = ((bf16[32,112,128]{2,1,0:T(8,128)(2,1)}), bf16[32,112,128]{2,1,0:T(8,128)(2,1)S(1)}, u32[]{:S(2)}, u32[]{:S(2)}) async-start(bf16[32,112,128]{2,1,0:T(8,128)(2,1)} %gradient_near.3), calls=%async_computation.1 | async-start | bytes 1835008 | tf_op jit(solution)/shard_map/all_to_all | solution.py:333
  86.0 42.4 %copy-start.3 = (bf16[1,448,1024]{2,1,0:T(8,128)(2,1)S(1)}, bf16[1,448,1024]{2,1,0:T(8,128)(2,1)}, u32[]{:S(2)}) copy-start(bf16[1,448,1024]{2,1,0:T(8,128)(2,1)} %first_ref.3) | copy-start | bytes 2752516
  103.3 25.1 %copy-start.1 = (f32[1,448,1024]{2,1,0:T(8,128)S(1)}, f32[1,448,1024]{2,1,0:T(8,128)}, u32[]{:S(2)}) copy-start(f32[1,448,1024]{2,1,0:T(8,128)} %master_ref.3) | copy-start | bytes 5505028
  103.3 25.1 %copy-start.4 = (bf16[1,448,1024]{2,1,0:T(8,128)(2,1)S(1)}, bf16[1,448,1024]{2,1,0:T(8,128)(2,1)}, u32[]{:S(2)}) copy-start(bf16[1,448,1024]{2,1,0:T(8,128)(2,1)} %second_ref.3) | copy-start | bytes 2752516
  130.9 5.0 %copy-start.9 = (s32[32,8]{0,1:T(8,128)S(1)}, s32[32,8]{0,1:T(8,128)}, u32[]{:S(2)}) copy-start(s32[32,8]{0,1:T(8,128)} %param.13) | copy-start | bytes 3076
  130.9 22.2 %all-to-all-start.3 = ((bf16[32,112,128]{2,1,0:T(8,128)(2,1)}), bf16[32,112,128]{2,1,0:T(8,128)(2,1)}, u32[]{:S(2)}, u32[]{:S(2)}) async-start(bf16[32,112,128]{2,1,0:T(8,128)(2,1)} %new_weights.1), calls=%async_computation.3 | async-start | bytes 1835008 | tf_op jit(solution)/shard_map/all_to_all | solution.py:333
  156.6 5.1 %copy-start.5 = (bf16[1,448,1024]{2,1,0:T(8,128)(2,1)S(1)}, bf16[1,448,1024]{2,1,0:T(8,128)(2,1)}, u32[]{:S(2)}) copy-start(bf16[1,448,1024]{2,1,0:T(8,128)(2,1)} %second_ref.3) | copy-start | bytes 2752516
  156.6 38.6 %all-to-all-start.4 = ((bf16[32,2,112,128]{3,2,1,0:T(8,128)(2,1)}), bf16[32,2,112,128]{3,2,1,0:T(8,128)(2,1)}, u32[]{:S(2)}, u32[]{:S(2)}) async-start(bf16[32,2,112,128]{3,2,1,0:T(8,128)(2,1)} %spread_copies.1), calls=%async_computation.4 | async-start | bytes 3670016 | tf_op jit(solution)/shard_map/all_to_all | solution.py:333
  161.7 1.5 copy-start.2

commit v6 on v5

--- a/solution.py
+++ b/solution.py
@@ -1,4 +1,5 @@
 import functools
+import itertools
 
 import jax
 import jax.numpy as jnp
@@ -184,34 +185,34 @@
     )(replicas, owner_map, first, second)
 
 
-def adam_cut(c, grad_ref, master_ref, first_ref, second_ref):
-    cut = pl.ds(c * LANES, LANES)
-    gradient = grad_ref[c].astype(jnp.float32)
-    first_new = beta_first * first_ref[0, :, cut].astype(jnp.float32) + (1.0 - beta_first) * gradient
+def adam_cut(r, c, grad_ref, master_ref, first_ref, second_ref):
+    cut = (0, pl.ds(r * PIECE, PIECE), pl.ds(c * LANES, LANES))
+    gradient = grad_ref[r * COL_CUTS + c].astype(jnp.float32)
+    first_new = beta_first * first_ref[cut].astype(jnp.float32) + (1.0 - beta_first) * gradient
     second_new = (
-        beta_second * second_ref[0, :, cut].astype(jnp.float32) + (1.0 - beta_second) * gradient * gradient
-    )
-    updated = master_ref[0, :, cut] - learn_rate * first_new / (jnp.sqrt(second_new) + adam_epsilon)
+        beta_second * second_ref[cut].astype(jnp.float32) + (1.0 - beta_second) * gradient * gradient
+    )
+    updated = master_ref[cut] - learn_rate * first_new / (jnp.sqrt(second_new) + adam_epsilon)
     return cut, first_new, second_new, updated
 
 
 def weights_kernel(grad_ref, master_ref, first_ref, second_ref, sent_ref):
-    for c in range(COL_CUTS):
-        _, _, _, updated = adam_cut(c, grad_ref, master_ref, first_ref, second_ref)
-        sent_ref[c] = updated.astype(sent_ref.dtype)
+    for r, c in itertools.product(range(2), range(COL_CUTS)):
+        _, _, _, updated = adam_cut(r, c, grad_ref, master_ref, first_ref, second_ref)
+        sent_ref[r * COL_CUTS + c] = updated.astype(sent_ref.dtype)
 
 
 def state_kernel(grad_ref, master_ref, first_ref, second_ref, master_out, first_out, second_out):
-    for c in range(COL_CUTS):
-        cut, first_new, second_new, updated = adam_cut(c, grad_ref, master_ref, first_ref, second_ref)
-        master_out[0, :, cut] = updated
-        first_out[0, :, cut] = first_new.astype(first_out.dtype)
-        second_out[0, :, cut] = second_new.astype(second_out.dtype)
+    for r, c in itertools.product(range(2), range(COL_CUTS)):
+        cut, first_new, second_new, updated = adam_cut(r, c, grad_ref, master_ref, first_ref, second_ref)
+        master_out[cut] = updated
+        first_out[cut] = first_new.astype(first_out.dtype)
+        second_out[cut] = second_new.astype(second_out.dtype)
 
 
 def adam_update(kernel, name, kinds, gradient, master, first_moment, second_moment):
-    rows = pl.BlockSpec((1, PIECE, COL_CUTS * LANES), lambda r: (0, r, 0))
-    pieces = pl.BlockSpec((COL_CUTS, PIECE, LANES), lambda r: (r, 0, 0))
+    rows = pl.BlockSpec((1, 2 * PIECE, COL_CUTS * LANES), lambda r: (0, r, 0))
+    pieces = pl.BlockSpec((2 * COL_CUTS, PIECE, LANES), lambda r: (r, 0, 0))
     if kinds is None:
         shapes = jax.ShapeDtypeStruct(gradient.shape, jnp.bfloat16)
         out_specs = pieces
@@ -220,7 +221,7 @@
         out_specs = (rows,) * len(kinds)
     return pl.pallas_call(
         kernel,
-        grid=(ROW_CUTS,),
+        grid=(ROW_CUTS // 2,),
         out_shape=shapes,
         in_specs=[pieces, rows, rows, rows],
         out_specs=out_specs,

time: 199 us -> 198 us (level)
  no operation moved by 1% of the time
where the time goes in v6:
time: 198 us
  waiting for transfers between devices  102 us (52%)
  starting transfers between devices  42.5 us (21%)
  Pallas kernels  26.6 us (13%)
  blocking collectives  22.2 us (11%)
  local copies, waits for them, and re-layouts  3.52 us (2%)
    all_to_all x4, waiting for transfers between devices, exchange(): return lax.all_to_all(pieces, 'ep', split_axis=0, concat_axis=0, tiled=True)  63.2 us
    ppermute x7, waiting for transfers between devices, x_shift(): return lax.ppermute(array, 'dp', pairs)  38.1 us
    all_to_all x4, starting transfers between devices, exchange(): return lax.all_to_all(pieces, 'ep', split_axis=0, concat_axis=0, tiled=True)  31.2 us
    all_to_all x1, blocking collectives, exchange(): return lax.all_to_all(pieces, 'ep', split_axis=0, concat_axis=0, tiled=True)  22.2 us
    pallas_call x2, Pallas kernels, slot_gradient(): pl.pallas_call(functools.partial(grad_kernel, slot, plan), out_shape=jax....  10.6 us
    ppermute x7, starting transfers between devices, x_shift(): return lax.ppermute(array, 'dp', pairs)  9.53 us
    pallas_call x2, Pallas kernels, adam_update(): pl.pallas_call(kernel, grid=(ROW_CUTS // 2,), out_shape=shapes, in_specs=...  4.75 us
  transfers between devices with their start and end apart: 19, of which 11 were waited for; matrix products, arithmetic and copies ran while one was open for 0% of the time, Pallas kernels for 8%

profile of v6, /device:TPU:6, one launch (start us, length us, event | category | flops | bytes accessed | tf_op | source)
XLA Modules:
  0.0 197.6 jit_solution(10422289911036929526)
XLA Ops:
  0.6 1.2 slice_bitcast_fusion
  1.9 2.3 %collective-permute-start.3 = (bf16[1792,128]{1,0:T(8,128)(2,1)S(1)}, bf16[1792,128]{1,0:T(8,128)(2,1)S(1)}, u32[]{:S(2)}, u32[]{:S(2)}) collective-permute-start(bf16[1792,128]{1,0:T(8,128)(2,1)S(1)} %get-tuple-element.19.refs_0_), channel_id=1, source_target_pairs={{0,2},{1,3},{2,4},{3,5},{4,6},{5,7},{6,0},{7,1},{8,10},{9,11},{10,... | collective-permute-start | bytes 1376264 | tf_op jit(solution)/shard_map/ppermute | solution.py:305
  4.2 10.0 %collective-permute-done.3.refs_4_ = bf16[1792,128]{1,0:T(8,128)(2,1)S(1)} collective-permute-done((bf16[1792,128]{1,0:T(8,128)(2,1)S(1)}, bf16[1792,128]{1,0:T(8,128)(2,1)S(1)}, u32[]{:S(2)}, u32[]{:S(2)}) %collective-permute-start.3) | collective-permute-done | bytes 458784 | tf_op jit(solution)/shard_map/ppermute | solution.py:305
  14.2 1.3 collective-permute-done.1.refs_2_
  15.5 0.7 collective-permute-start.5
  16.2 1.3 collective-permute-start.7
  17.6 5.1 %gradient_near.2.refs_2_ = bf16[32,112,128]{2,1,0:T(8,128)(2,1)} custom-call(s32[1]{0:T(128)} %bitcast.place_ref, s32[2]{0:T(128)S(1)} %copy-done.6, bf16[2,448,1792]{2,1,0:T(8,128)(2,1)} %bitcast.8, bf16[1792,128]{1,0:T(8,128)(2,1)S(1)} %get-tuple-element.19.refs_0_, bf16[1792,128]{1,0:T(8,128)(2,1)S(1)} %collective-permute-done.refs_1_, ...), custom_call_target="tpu_custom_call" | custom-call | flops 1233125376 | bytes 6000000 | tf_op jit(solution)/shard_map/gradient_near/pallas_call | solution.py:118
  22.7 5.7 %collective-permute-done.5.refs_0_ = bf16[1792,128]{1,0:T(8,128)(2,1)S(1)} collective-permute-done((bf16[1792,128]{1,0:T(8,128)(2,1)S(1)}, bf16[1792,128]{1,0:T(8,128)(2,1)S(1)}, u32[]{:S(2)}, u32[]{:S(2)}) %collective-permute-start.5) | collective-permute-done | bytes 458784 | tf_op jit(solution)/shard_map/ppermute | solution.py:305
  28.4 1.4 collective-permute-done.7.refs_2_
  30.3 2.3 %gradient_far.1 = bf16[32,112,128]{2,1,0:T(8,128)(2,1)} custom-call(s32[1]{0:T(128)} %bitcast.place_ref, s32[2]{0:T(128)S(1)} %copy-done.6, bf16[2,448,1792]{2,1,0:T(8,128)(2,1)S(1)} %bitcast.10, bf16[1792,128]{1,0:T(8,128)(2,1)S(1)} %collective-permute-done.5.refs_0_, ...), custom_call_target="tpu_custom_call", output_to_operand_aliasing={{}: (5, {})} | custom-call | flops 411041792 | bytes 2000000 | tf_op jit(solution)/shard_map/gradient_far/pallas_call | solution.py:128
  32.6 11.6 %all-to-all-start = ((bf16[32,112,128]{2,1,0:T(8,128)(2,1)}), bf16[32,112,128]{2,1,0:T(8,128)(2,1)S(1)}, u32[]{:S(2)}, u32[]{:S(2)}) async-start(bf16[32,112,128]{2,1,0:T(8,128)(2,1)} %gradient_far.1), calls=%async_computation | async-start | bytes 1835008 | tf_op jit(solution)/shard_map/all_to_all | solution.py:334
  44.2 1.6 collective-permute-start.10
  46.3 10.3 %collective-permute-done.10.refs_4_ = bf16[1792,128]{1,0:T(8,128)(2,1)S(1)} collective-permute-done((bf16[1792,128]{1,0:T(8,128)(2,1)S(1)}, bf16[1792,128]{1,0:T(8,128)(2,1)S(1)}, u32[]{:S(2)}, u32[]{:S(2)}) %collective-permute-start.10) | collective-permute-done | bytes 458784 | tf_op jit(solution)/shard_map/ppermute | solution.py:305
  57.1 2.1 %collective-permute-done.12.refs_6_ = bf16[1792,128]{1,0:T(8,128)(2,1)S(1)} collective-permute-done((bf16[1792,128]{1,0:T(8,128)(2,1)}, bf16[1792,128]{1,0:T(8,128)(2,1)S(1)}, u32[]{:S(2)}, u32[]{:S(2)}) %collective-permute-start.12) | collective-permute-done | bytes 458784 | tf_op jit(solution)/shard_map/ppermute | solution.py:305
  59.2 1.3 collective-permute-start.13
  60.5 3.1 %collective-permute-start.14 = (bf16[1792,128]{1,0:T(8,128)(2,1)S(1)}, bf16[1792,128]{1,0:T(8,128)(2,1)S(1)}, u32[]{:S(2)}, u32[]{:S(2)}) collective-permute-start(bf16[1792,128]{1,0:T(8,128)(2,1)S(1)} %collective-permute-done.11.refs_5_), channel_id=1, source_target_pairs={{0,2},{2,4},{4,6},{6,0},{8,10},{10,12},{12,14},{14,8},{16,18},{18,... | collective-permute-start | bytes 1376264 | tf_op jit(solution)/shard_map/ppermute | solution.py:305
  63.6 7.2 %collective-permute-done.14.refs_8_ = bf16[1792,128]{1,0:T(8,128)(2,1)S(1)} collective-permute-done((bf16[1792,128]{1,0:T(8,128)(2,1)S(1)}, bf16[1792,128]{1,0:T(8,128)(2,1)S(1)}, u32[]{:S(2)}, u32[]{:S(2)}) %collective-permute-start.14) | collective-permute-done | bytes 458784 | tf_op jit(solution)/shard_map/ppermute | solution.py:305
  70.9 5.5 %gradient_near.3 = bf16[32,112,128]{2,1,0:T(8,128)(2,1)} custom-call(s32[1]{0:T(128)} %bitcast.place_ref, s32[2]{0:T(128)S(1)} %copy-done.6, bf16[2,448,1792]{2,1,0:T(8,128)(2,1)} %bitcast.9, bf16[1792,128]{1,0:T(8,128)(2,1)S(1)} %get-tuple-element.13.refs_0_, bf16[1792,128]{1,0:T(8,128)(2,1)S(1)} %collective-permute-done.9.refs_1_, ...), custom_call_target="tpu_custom_call" | custom-call | flops 1644167168 | bytes 160000000 | tf_op jit(solution)/shard_map/gradient_near/pallas_call | solution.py:118
  76.4 9.5 %all-to-all-start.1 = ((bf16[32,112,128]{2,1,0:T(8,128)(2,1)}), bf16[32,112,128]{2,1,0:T(8,128)(2,1)S(1)}, u32[]{:S(2)}, u32[]{:S(2)}) async-start(bf16[32,112,128]{2,1,0:T(8,128)(2,1)} %gradient_near.3), calls=%async_computation.1 | async-start | bytes 1835008 | tf_op jit(solution)/shard_map/all_to_all | solution.py:334
  86.0 17.3 %all-to-all-done.1.second_ref = bf16[32,112,128]{2,1,0:T(8,128)(2,1)S(1)} async-done(((bf16[32,112,128]{2,1,0:T(8,128)(2,1)}), bf16[32,112,128]{2,1,0:T(8,128)(2,1)S(1)}, u32[]{:S(2)}, u32[]{:S(2)}) %all-to-all-start.1) | async-done | bytes 917536 | tf_op jit(solution)/shard_map/all_to_all | solution.py:334
  103.3 3.0 %sum_copies.1 = bf16[32,112,128]{2,1,0:T(8,128)(2,1)S(1)} custom-call(s32[32,8]{1,0:T(8,128)S(1)} %copy.14.replicas_ref, s32[32]{0:T(128)S(1)} %copy-done.7, bf16[32,112,128]{2,1,0:T(8,128)(2,1)S(1)} %all-to-all-done.first_ref, bf16[32,112,128]{2,1,0:T(8,128)(2,1)S(1)} %all-to-all-done.1.second_ref), custom_call_target="tpu_custom_call" | custom-call | tf_op jit(solution)/shard_map/sum_copies/pallas_call | solution.py:174
  106.3 22.2 %all_to_all.25.grad_ref = bf16[32,112,128]{2,1,0:T(8,128)(2,1)S(1)} all-to-all(bf16[32,112,128]{2,1,0:T(8,128)(2,1)S(1)} %sum_copies.1), channel_id=1, replica_groups=mesh['ep'=32,'dp'=8] {'ep'}, dimensions={0} | all-to-all | bytes 1835008 | tf_op jit(solution)/shard_map/all_to_all | solution.py:334
  128.5 2.2 %new_weights.1 = bf16[32,112,128]{2,1,0:T(8,128)(2,1)} custom-call(bf16[32,112,128]{2,1,0:T(8,128)(2,1)S(1)} %all_to_all.25.grad_ref, f32[1,448,1024]{2,1,0:T(8,128)S(1)} %copy-done.1, bf16[1,448,1024]{2,1,0:T(8,128)(2,1)S(1)} %copy-done.3, bf16[1,448,1024]{2,1,0:T(8,128)(2,1)S(1)} %copy-done.4), custom_call_target="tpu_custom_call" | custom-call | flops 8000000 | bytes 9000000 | tf_op jit(solution)/shard_map/new_weights/pallas_call | solution.py:222
  130.7 4.9 %all-to-all-start.3 = ((bf16[32,112,128]{2,1,0:T(8,128)(2,1)}), bf16[32,112,128]{2,1,0:T(8,128)(2,1)}, u32[]{:S(2)}, u32[]{:S(2)}) async-start(bf16[32,112,128]{2,1,0:T(8,128)(2,1)} %new_weights.1), calls=%async_computation.3 | async-start | bytes 1835008 | tf_op jit(solution)/shard_map/all_to_all | solution.py:334
  135.6 0.7 copy.15.lists_ref
  136.3 16.5 %all-to-all-done.3.weights_ref = bf16[32,112,128]{2,1,0:T(8,128)(2,1)} async-done(((bf16[32,112,128]{2,1,0:T(8,128)(2,1)}), bf16[32,112,128]{2,1,0:T(8,128)(2,1)}, u32[]{:S(2)}, u32[]{:S(2)}) %all-to-all-start.3) | async-done | bytes 917536 | tf_op jit(solution)/shard_map/all_to_all | solution.py:334
  152.8 3.5 %spread_copies.1 = bf16[32,2,112,128]{3,2,1,0:T(8,128)(2,1)} custom-call(s32[32,8]{1,0:T(8,128)} %copy.15.lists_ref, s32[32]{0:T(128)} %owners_ref.3, bf16[32,112,128]{2,1,0:T(8,128)(2,1)} %all-to-all-done.3.weights_ref), custom_call_target="tpu_custom_call" | custom-call | tf_op jit(solution)/shard_map/spread_copies/pallas_call | solution.py:251
  156.3 5.1 %all-to-all-start.4 = ((bf16[32,2,112,128]{3,2,1,0:T(8,128)(2,1)}), bf16[32,2,112,128]{3,2,1,0:T(8,128)(2,1)}, u32[]{:S(2)}, u32[]{:S(2)}) async-start(bf16[32,2,112,128]{3,2,1,0:T(8,128)(2,1)} %spread_copies.1), calls=%async_computation.4 | async-start | bytes 3670016 | tf_op jit(solution)/shard_map/all_to_all | solution.py:334
  161.5 1.5 copy-done.2
  163.0 2.6 %new_state.1 = (f32[1,448,1024]{2,1,0:T(8,128)}, bf16[1,448,1024]{2,1,0:T(8,128)(2,1)}, bf16[1,448,1024]{2,1,0:T(8,128)(2,1)}) custom-call(bf16[32,112,128]{2,1,0:T(8,128)(2,1)S(1)} %all_to_all.25.grad_ref, f32[1,448,1024]{2,1,0:T(8,128)S(1)} %copy-done.2, bf16[1,448,1024]{2,1,0:T(8,128)(2,1)S(1)} %copy-done.3, bf16[1,448,1024]{2,1,0:T(8,128)(2,1)S(1)} %copy-done.5), custom_call_target="tpu_custom_call" | custom-call | flops 8000000 | bytes 9000000 | tf_op jit(solution)/shard_map/new_state/pallas_call | solution.py:222
  165.6 29.4 %all-to-all-done.4 = bf16[32,2,112,128]{3,2,1,0:T(8,128)(2,1)} async-done(((bf16[32,2,112,128]{3,2,1,0:T(8,128)(2,1)}), bf16[32,2,112,128]{3,2,1,0:T(8,128)(2,1)}, u32[]{:S(2)}, u32[]{:S(2)}) %all-to-all-start.4) | async-done | bytes 1835040 | tf_op jit(solution)/shard_map/all_to_all | solution.py:334
  194.9 2.6 %order_pieces.1 = bf16[2,4,112,1024]{3,2,1,0:T(8,128)(2,1)} custom-call(bf16[4,8,2,112,128]{4,3,2,1,0:T(8,128)(2,1)} %bitcast.4.pieces_ref), custom_call_target="tpu_custom_call" | custom-call | tf_op jit(solution)/shard_map/order_pieces/pallas_call | solution.py:288
  (38 shorter events, 1.6 us)
Async XLA Ops:
  0.6 16.9 %copy-start.6 = (s32[2]{0:T(128)S(1)}, s32[2]{0:T(128)}, u32[]{:S(2)}) copy-start(s32[2]{0:T(128)} %counts_ref.5) | copy-start | bytes 28
  1.9 12.3 %collective-permute-start.3 = (bf16[1792,128]{1,0:T(8,128)(2,1)S(1)}, bf16[1792,128]{1,0:T(8,128)(2,1)S(1)}, u32[]{:S(2)}, u32[]{:S(2)}) collective-permute-start(bf16[1792,128]{1,0:T(8,128)(2,1)S(1)} %get-tuple-element.19.refs_0_), channel_id=1, source_target_pairs={{0,2},{1,3},{2,4},{3,5},{4,6},{5,7},{6,0},{7,1},{8,10},{9,11},{10,... | collective-permute-start | bytes 1376264 | tf_op jit(solution)/shard_map/ppermute | solution.py:305
  4.2 11.3 %collective-permute-start.1 = (bf16[1792,128]{1,0:T(8,128)(2,1)S(1)}, bf16[1792,128]{1,0:T(8,128)(2,1)S(1)}, u32[]{:S(2)}, u32[]{:S(2)}) collective-permute-start(bf16[1792,128]{1,0:T(8,128)(2,1)S(1)} %get-tuple-element.19.refs_0_), channel_id=1, source_target_pairs={{0,6},{1,7},{2,0},{3,1},{4,2},{5,3},{6,4},{7,5},{8,14},{9,15},{10,... | collective-permute-start | bytes 1376264 | tf_op jit(solution)/shard_map/ppermute | solution.py:305
  4.2 13.4 %collective-permute-start = (bf16[1792,128]{1,0:T(8,128)(2,1)S(1)}, bf16[1792,128]{1,0:T(8,128)(2,1)S(1)}, u32[]{:S(2)}, u32[]{:S(2)}) collective-permute-start(bf16[1792,128]{1,0:T(8,128)(2,1)S(1)} %get-tuple-element.19.refs_0_), channel_id=1, source_target_pairs={{0,1},{1,0},{2,3},{3,2},{4,5},{5,4},{6,7},{7,6},{8,9},{9,8},{10,11... | collective-permute-start | bytes 1376264 | tf_op jit(solution)/shard_map/ppermute | solution.py:310
  14.2 3.3 %collective-permute-start.4 = (bf16[1792,128]{1,0:T(8,128)(2,1)S(1)}, bf16[1792,128]{1,0:T(8,128)(2,1)S(1)}, u32[]{:S(2)}, u32[]{:S(2)}) collective-permute-start(bf16[1792,128]{1,0:T(8,128)(2,1)S(1)} %collective-permute-done.3.refs_4_), channel_id=1, source_target_pairs={{0,1},{1,0},{2,3},{3,2},{4,5},{5,4},{6,7},{7,6},{8,9},{9,8},{10,11... | collective-permute-start | bytes 1376264 | tf_op jit(solution)/shard_map/ppermute | solution.py:310
  15.5 2.0 %collective-permute-start.2 = (bf16[1792,128]{1,0:T(8,128)(2,1)S(1)}, bf16[1792,128]{1,0:T(8,128)(2,1)}, u32[]{:S(2)}, u32[]{:S(2)}) collective-permute-start(bf16[1792,128]{1,0:T(8,128)(2,1)S(1)} %collective-permute-done.1.refs_2_), channel_id=1, source_target_pairs={{0,1},{1,0},{2,3},{3,2},{4,5},{5,4},{6,7},{7,6},{8,9},{9,8},{10,11... | collective-permute-start | bytes 1376264 | tf_op jit(solution)/shard_map/ppermute | solution.py:310
  15.5 12.9 %collective-permute-start.5 = (bf16[1792,128]{1,0:T(8,128)(2,1)S(1)}, bf16[1792,128]{1,0:T(8,128)(2,1)S(1)}, u32[]{:S(2)}, u32[]{:S(2)}) collective-permute-start(bf16[1792,128]{1,0:T(8,128)(2,1)S(1)} %collective-permute-done.3.refs_4_), channel_id=1, source_target_pairs={{0,2},{1,3},{2,4},{3,5},{4,6},{5,7},{6,0},{7,1},{8,10},{9,11},{10,... | collective-permute-start | bytes 1376264 | tf_op jit(solution)/shard_map/ppermute | solution.py:305
  16.2 13.6 %collective-permute-start.7 = (bf16[1792,128]{1,0:T(8,128)(2,1)S(1)}, bf16[1792,128]{1,0:T(8,128)(2,1)}, u32[]{:S(2)}, u32[]{:S(2)}) collective-permute-start(bf16[1792,128]{1,0:T(8,128)(2,1)S(1)} %get-tuple-element.13.refs_0_), channel_id=1, source_target_pairs={{0,6},{1,7},{2,0},{3,1},{4,2},{5,3},{6,4},{7,5},{8,14},{9,15},{10,... | collective-permute-start | bytes 1376264 | tf_op jit(solution)/shard_map/ppermute | solution.py:305
  17.6 12.7 %copy-start = (bf16[2,1792,448]{1,2,0:T(8,128)(2,1)S(1)}, bf16[2,1792,448]{1,2,0:T(8,128)(2,1)}, u32[]{:S(2)}) copy-start(bf16[2,1792,448]{1,2,0:T(8,128)(2,1)} %param.10) | copy-start | bytes 9633796
  28.4 1.8 collective-permute-start.6
  29.9 2.7 %collective-permute-start.8 = (bf16[1792,128]{1,0:T(8,128)(2,1)}, bf16[1792,128]{1,0:T(8,128)(2,1)S(1)}, u32[]{:S(2)}, u32[]{:S(2)}) collective-permute-start(bf16[1792,128]{1,0:T(8,128)(2,1)} %collective-permute-done.7.refs_2_), channel_id=1, source_target_pairs={{0,1},{1,0},{2,3},{3,2},{4,5},{5,4},{6,7},{7,6},{8,9},{9,8},{10,11... | collective-permute-start | bytes 1376264 | tf_op jit(solution)/shard_map/ppermute | solution.py:310
  32.6 43.8 %all-to-all-start = ((bf16[32,112,128]{2,1,0:T(8,128)(2,1)}), bf16[32,112,128]{2,1,0:T(8,128)(2,1)S(1)}, u32[]{:S(2)}, u32[]{:S(2)}) async-start(bf16[32,112,128]{2,1,0:T(8,128)(2,1)} %gradient_far.1), calls=%async_computation | async-start | bytes 1835008 | tf_op jit(solution)/shard_map/all_to_all | solution.py:334
  44.2 12.4 %collective-permute-start.10 = (bf16[1792,128]{1,0:T(8,128)(2,1)S(1)}, bf16[1792,128]{1,0:T(8,128)(2,1)S(1)}, u32[]{:S(2)}, u32[]{:S(2)}) collective-permute-start(bf16[1792,128]{1,0:T(8,128)(2,1)S(1)} %get-tuple-element.13.refs_0_), channel_id=1, source_target_pairs={{0,2},{1,3},{2,4},{3,5},{4,6},{5,7},{6,0},{7,1},{8,10},{9,11},{10,... | collective-permute-start | bytes 1376264 | tf_op jit(solution)/shard_map/ppermute | solution.py:305
  45.8 13.4 %collective-permute-start.12 = (bf16[1792,128]{1,0:T(8,128)(2,1)}, bf16[1792,128]{1,0:T(8,128)(2,1)S(1)}, u32[]{:S(2)}, u32[]{:S(2)}) collective-permute-start(bf16[1792,128]{1,0:T(8,128)(2,1)} %collective-permute-done.7.refs_2_), channel_id=1, source_target_pairs={{0,6},{1,7},{2,0},{3,1},{4,2},{5,3},{6,4},{7,5},{8,14},{9,15},{10,... | collective-permute-start | bytes 1376264 | tf_op jit(solution)/shard_map/ppermute | solution.py:305
  56.5 4.0 %collective-permute-start.11 = (bf16[1792,128]{1,0:T(8,128)(2,1)S(1)}, bf16[1792,128]{1,0:T(8,128)(2,1)S(1)}, u32[]{:S(2)}, u32[]{:S(2)}) collective-permute-start(bf16[1792,128]{1,0:T(8,128)(2,1)S(1)} %collective-permute-done.10.refs_4_), channel_id=1, source_target_pairs={{0,1},{1,0},{2,3},{3,2},{4,5},{5,4},{6,7},{7,6},{8,9},{9,8},{10,11... | collective-permute-start | bytes 1376264 | tf_op jit(solution)/shard_map/ppermute | solution.py:310
  56.5 7.1 %collective-permute-start.9 = (bf16[1792,128]{1,0:T(8,128)(2,1)S(1)}, bf16[1792,128]{1,0:T(8,128)(2,1)S(1)}, u32[]{:S(2)}, u32[]{:S(2)}) collective-permute-start(bf16[1792,128]{1,0:T(8,128)(2,1)S(1)} %get-tuple-element.13.refs_0_), channel_id=1, source_target_pairs={{0,1},{1,0},{2,3},{3,2},{4,5},{5,4},{6,7},{7,6},{8,9},{9,8},{10,11... | collective-permute-start | bytes 1376264 | tf_op jit(solution)/shard_map/ppermute | solution.py:310
  59.2 4.5 %collective-permute-start.13 = (bf16[1792,128]{1,0:T(8,128)(2,1)S(1)}, bf16[1792,128]{1,0:T(8,128)(2,1)S(1)}, u32[]{:S(2)}, u32[]{:S(2)}) collective-permute-start(bf16[1792,128]{1,0:T(8,128)(2,1)S(1)} %collective-permute-done.12.refs_6_), channel_id=1, source_target_pairs={{0,1},{2,3},{4,5},{6,7},{8,9},{10,11},{12,13},{14,15},{16,17},{18,... | collective-permute-start | bytes 1376264 | tf_op jit(solution)/shard_map/ppermute | solution.py:329
  60.5 10.4 %collective-permute-start.14 = (bf16[1792,128]{1,0:T(8,128)(2,1)S(1)}, bf16[1792,128]{1,0:T(8,128)(2,1)S(1)}, u32[]{:S(2)}, u32[]{:S(2)}) collective-permute-start(bf16[1792,128]{1,0:T(8,128)(2,1)S(1)} %collective-permute-done.11.refs_5_), channel_id=1, source_target_pairs={{0,2},{2,4},{4,6},{6,0},{8,10},{10,12},{12,14},{14,8},{16,18},{18,... | collective-permute-start | bytes 1376264 | tf_op jit(solution)/shard_map/ppermute | solution.py:305
  76.4 9.6 %copy-start.8 = (s32[32,8]{0,1:T(8,128)S(1)}, s32[32,8]{0,1:T(8,128)}, u32[]{:S(2)}) copy-start(s32[32,8]{0,1:T(8,128)} %param.12) | copy-start | bytes 3076
  76.4 27.0 %copy-start.7 = (s32[32]{0:T(128)S(1)}, s32[32]{0:T(128)}, u32[]{:S(2)}) copy-start(s32[32]{0:T(128)} %owners_ref.3) | copy-start | bytes 388
  76.4 26.9 %all-to-all-start.1 = ((bf16[32,112,128]{2,1,0:T(8,128)(2,1)}), bf16[32,112,128]{2,1,0:T(8,128)(2,1)S(1)}, u32[]{:S(2)}, u32[]{:S(2)}) async-start(bf16[32,112,128]{2,1,0:T(8,128)(2,1)} %gradient_near.3), calls=%async_computation.1 | async-start | bytes 1835008 | tf_op jit(solution)/shard_map/all_to_all | solution.py:334
  86.0 42.5 %copy-start.3 = (bf16[1,448,1024]{2,1,0:T(8,128)(2,1)S(1)}, bf16[1,448,1024]{2,1,0:T(8,128)(2,1)}, u32[]{:S(2)}) copy-start(bf16[1,448,1024]{2,1,0:T(8,128)(2,1)} %first_ref.3) | copy-start | bytes 2752516
  103.3 25.2 %copy-start.1 = (f32[1,448,1024]{2,1,0:T(8,128)S(1)}, f32[1,448,1024]{2,1,0:T(8,128)}, u32[]{:S(2)}) copy-start(f32[1,448,1024]{2,1,0:T(8,128)} %master_ref.3) | copy-start | bytes 5505028
  103.3 25.2 %copy-start.4 = (bf16[1,448,1024]{2,1,0:T(8,128)(2,1)S(1)}, bf16[1,448,1024]{2,1,0:T(8,128)(2,1)}, u32[]{:S(2)}) copy-start(bf16[1,448,1024]{2,1,0:T(8,128)(2,1)} %second_ref.3) | copy-start | bytes 2752516
  130.7 4.9 %copy-start.9 = (s32[32,8]{0,1:T(8,128)S(1)}, s32[32,8]{0,1:T(8,128)}, u32[]{:S(2)}) copy-start(s32[32,8]{0,1:T(8,128)} %param.13) | copy-start | bytes 3076
  130.7 22.1 %all-to-all-start.3 = ((bf16[32,112,128]{2,1,0:T(8,128)(2,1)}), bf16[32,112,128]{2,1,0:T(8,128)(2,1)}, u32[]{:S(2)}, u32[]{:S(2)}) async-start(bf16[32,112,128]{2,1,0:T(8,128)(2,1)} %new_weights.1), calls=%async_computation.3 | async-start | bytes 1835008 | tf_op jit(solution)/shard_map/all_to_all | solution.py:334
  156.3 5.1 %copy-start.5 = (bf16[1,448,1024]{2,1,0:T(8,128)(2,1)S(1)}, bf16[1,448,1024]{2,1,0:T(8,128)(2,1)}, u32[]{:S(2)}) copy-start(bf16[1,448,1024]{2,1,0:T(8,128)(2,1)} %second_ref.3) | copy-start | bytes 2752516
  156.3 38.6 %all-to-all-start.4 = ((bf16[32,2,112,128]{3,2,1,0:T(8,128)(2,1)}), bf16[32,2,112,128]{3,2,1,0:T(8,128)(2,1)}, u32[]{:S(2)}, u32[]{:S(2)}) async-start(bf16[32,2,112,128]{3,2,1,0:T(8,128)(2,1)} %spread_copies.1), calls=%async_computation.4 | async-start | bytes 3670016 | tf_op jit(solution)/shard_map/all_to_all | solution.py:334
  161.5 1.5 copy-start.2
